TPU v7x, 32 devices: a whole 2x2x4 slice. The times are simulated.
32 devices in a mesh: doc: 4 (over y, x), tm: 8 (over z, core).
Axes of the slice: x: 2, y: 2, z: 4, core: 2. Of those that a mesh axis runs over, the one named last changes fastest.
Arguments:
- tokens: bfloat16 [2, 4, 1024, 1024], P(None, 'doc', 'tm'), may hold values from -6 to 6
- cotangent: bfloat16 [2, 4, 1024, 1024], P(None, 'doc', 'tm'), may hold values from -6 to 6
- given_cache: bfloat16 [2, 4, 8192, 896], P(None, 'doc', 'tm'), may hold values from -6 to 6
- value_routes: int32 [2, 4, 1024, 4, 2], P(None, 'doc', 'tm'), may hold values from 0 to 4, all different within a row
- output_routes: int32 [2, 4, 1024, 4, 2], P(None, 'doc', 'tm'), may hold values from 0 to 4, all different within a row
- valid_counts: int32 [2, 4, 8], P(None, 'doc', 'tm'), may hold values from 1 to 128, as said below
- doc_starts: int32 [2, 4, 8], P(None, 'doc', 'tm'), may hold values from 0 to 1, as said below
- norm1_gain: bfloat16 [1024], P(('doc', 'tm')), may hold values from 0.5 to 1.5
- norm1_shift: bfloat16 [1024], P(('doc', 'tm')), may hold values from -1 to 1
- qk_weight: bfloat16 [1024, 896], P(('doc', 'tm')), may hold values from -0.1875 to 0.1875
- router_weight: bfloat16 [1024, 40], P(('doc', 'tm')), may hold values from -0.125 to 0.125
- value_weight: bfloat16 [1024, 2240], P(('doc', 'tm')), may hold values from -0.1875 to 0.1875
- output_weight: bfloat16 [2240, 1024], P(None, ('doc', 'tm')), may hold values from -2 to 2
- rel_bias: bfloat16 [4, 256], P(None, ('doc', 'tm')), may hold values from -4 to 4
- norm2_gain: bfloat16 [1024], P(('doc', 'tm')), may hold values from 0.5 to 1.5
- norm2_shift: bfloat16 [1024], P(('doc', 'tm')), may hold values from -1 to 1
- ffn_in: bfloat16 [1024, 4096], P(('doc', 'tm')), may hold values from -0.1875 to 0.1875
- ffn_out: bfloat16 [4096, 1024], P(('doc', 'tm')), may hold values from -0.09375 to 0.09375
Outputs:
- layer_out: bfloat16 [2, 4, 1024, 1024], P(None, 'doc', 'tm')
- input_grad: float32 [2, 4, 1024, 1024], P(None, 'doc', 'tm')
- norm1_gain_grad: float32 [1024], P(('doc', 'tm'))
- norm1_shift_grad: float32 [1024], P(('doc', 'tm'))
- qk_weight_grad: float32 [1024, 896], P(('doc', 'tm'))
- router_weight_grad: float32 [1024, 40], P(('doc', 'tm'))
- value_weight_grad: float32 [1024, 2240], P(('doc', 'tm'))
- output_weight_grad: float32 [2240, 1024], P(None, ('doc', 'tm'))
- rel_bias_grad: float32 [4, 256], P(None, ('doc', 'tm'))
- norm2_gain_grad: float32 [1024], P(('doc', 'tm'))
- norm2_shift_grad: float32 [1024], P(('doc', 'tm'))
- ffn_in_grad: float32 [1024, 4096], P(('doc', 'tm'))
- ffn_out_grad: float32 [4096, 1024], P(('doc', 'tm'))
Inputs may be any that keep to these rules, and one draw needn't show every extreme that they name: `doc_starts`: 1 marks a block where a document begins; the first block of every row is 1, and so is every block after one with fewer than 128 valid tokens. `valid_counts`: the valid tokens lead their block; fewer than 128 only in the last block of a document. `value_routes`: the 2 experts of a token and head differ. `output_routes`: the 2 experts of a token and head differ.
All inputs are finite; a program needn't handle non-finite values.
Results may differ from a plain program's by a relative error of at most 0.017.
Values may be sent and summed in bfloat16 or wider, within the bound.
A program may use at most 320 MiB of HBM per device.

v0:
```python
import jax
import jax.numpy as jnp
from jax import lax
from jax.sharding import PartitionSpec as P

HEADS = 4
HEAD_DIM = 112
EXPERTS = 5
TOPK = 2
MEM = 1024
BUCKETS = 256
NEAR = 128
STEP = 16


EPS = 1e-05
NEG = -1e30
HIGH = lax.Precision.HIGHEST


def shortened(array):
    return jax.tree.map(lambda a: a.astype(jnp.bfloat16) if a.dtype == jnp.float32 else a, array)


def from_behind(value, axis, steps):
    count = lax.axis_size(axis)
    first, last = (max(0, -steps), min(count, count - steps))
    return lax.ppermute(value, axis, [(source, source + steps) for source in range(first, last)])


def norm_forward(values, gain, shift):
    center_mean = jnp.mean(values, axis=-1, keepdims=True)
    centered = values - center_mean
    inverse = lax.rsqrt(jnp.mean(centered * centered, axis=-1, keepdims=True) + EPS)
    normed = centered * inverse
    return (normed * gain + shift, normed, inverse)


def norm_backward(upstream, normed, inverse, gain):
    scaled = upstream * gain
    inside = (
        scaled
        - jnp.mean(scaled, axis=-1, keepdims=True)
        - normed * jnp.mean(scaled * normed, axis=-1, keepdims=True)
    )
    return (inside * inverse, jnp.sum(upstream * normed, axis=0), jnp.sum(upstream, axis=0))


def selection(routes):
    expert_ids = jnp.arange(EXPERTS, dtype=jnp.int32)
    return jnp.sum((routes[..., None] == expert_ids).astype(jnp.float32), axis=-2)


def bucket_index(distance):
    far_bucket = NEAR + (distance - NEAR) // STEP
    return jnp.clip(jnp.where(distance < NEAR, distance, far_bucket), 0, BUCKETS - 1)


def gelu_slope(pre_act):
    return (
        0.5 * (1.0 + lax.erf(pre_act * 0.7071067811865476))
        + pre_act * jnp.exp(-0.5 * pre_act * pre_act) * 0.3989422804014327
    )


def flatten(matrix):
    return matrix.reshape(-1)


def bucket_matrix(local_len):
    spread = MEM + 2 * local_len - 1
    distance = jnp.arange(spread, dtype=jnp.int32) - (local_len - 1)
    bucket_ids = jnp.arange(BUCKETS, dtype=jnp.int32)
    return (bucket_index(distance)[:, None] == bucket_ids[None, :]).astype(jnp.float32)


def bias_matrix(table, local_len):
    spread = MEM + 2 * local_len - 1
    window = MEM + local_len
    by_distance = jnp.einsum("hc,kc->hk", table, bucket_matrix(local_len), precision=HIGH)
    turned = jnp.concatenate([by_distance[:, ::-1], jnp.zeros((HEADS, 1), jnp.float32)], axis=1)
    tiled = jnp.tile(turned, (1, local_len))[:, : local_len * spread].reshape(
        HEADS, local_len, spread
    )
    return tiled[:, :, local_len - 1 : local_len - 1 + window]


def bias_backward(score_sum, local_len):
    spread = MEM + 2 * local_len - 1
    padded = jnp.pad(score_sum, ((0, 0), (0, 0), (local_len - 1, 0))).reshape(
        HEADS, local_len * spread
    )
    padded = jnp.pad(padded, ((0, 0), (0, local_len))).reshape(HEADS, local_len, spread + 1)
    by_distance = jnp.sum(padded, axis=1)[:, :spread][:, ::-1]
    return jnp.einsum("hk,kc->hc", by_distance, bucket_matrix(local_len), precision=HIGH)


def attention_scores(queries, keys, table, counts):
    local_len = queries.shape[1]
    window = keys.shape[1]
    raw = jnp.einsum(
        "bqhd,bkhd->bhqk", queries, keys, preferred_element_type=jnp.float32
    ) * HEAD_DIM ** (-0.5)
    row_ids = jnp.arange(local_len, dtype=jnp.int32)[:, None]
    col_ids = jnp.arange(window, dtype=jnp.int32)[None, :]
    bias = bias_matrix(table, local_len)
    own_ids = col_ids - MEM
    causal = (own_ids <= row_ids)[None, None]
    live = own_ids[None, None] < counts[:, None, None, None]
    valid = jnp.logical_or((col_ids < MEM)[None, None], jnp.logical_and(causal, live))
    return (jnp.where(valid, raw + bias[None], NEG), valid)


def memory_by_hops(cache_own, given, starts, local_len):
    hops_total = MEM // local_len
    open_flag = jnp.logical_not(starts)[:, None, None]
    memory_slots = [jnp.zeros_like(cache_own) for _ in range(hops_total)]
    start_marks = starts.astype(jnp.bfloat16)
    for distance in range(1, hops_total + 1):
        if distance < hops_total:
            outgoing = (cache_own, start_marks, given[:, distance * local_len :])
        else:
            outgoing = (cache_own, start_marks)
        incoming = jax.tree.map(
            lambda part, own: part.astype(own.dtype),
            from_behind(shortened(outgoing), "tm", distance),
            outgoing,
        )
        memory_slots[hops_total - distance] = jnp.where(
            open_flag, incoming[0], memory_slots[hops_total - distance]
        )
        arrived = jnp.logical_and(open_flag, (incoming[1] > 0)[:, None, None])
        if distance < hops_total:
            for position in range(hops_total - distance):
                portion = incoming[2][:, position * local_len : (position + 1) * local_len]
                memory_slots[position] = jnp.where(arrived, portion, memory_slots[position])
        open_flag = jnp.logical_and(open_flag, jnp.logical_not(arrived))
    assembled = jnp.concatenate(memory_slots, axis=1)
    return jnp.where(starts[:, None, None], given, assembled)


def on_device(
    tokens,
    cotangent,
    given_cache,
    value_routes,
    output_routes,
    valid_counts,
    doc_starts,
    norm1_gain,
    norm1_shift,
    qk_weight,
    router_weight,
    value_weight,
    output_weight,
    rel_bias,
    norm2_gain,
    norm2_shift,
    ffn_in,
    ffn_out,
):
    batches, unused_row, local_len, model_width = tokens.shape
    row_count = batches * local_len
    inner_width = HEADS * HEAD_DIM
    head_experts = HEADS * EXPERTS
    full_weights = (
        lax.all_gather(norm1_gain, ("doc", "tm"), axis=0, tiled=True),
        lax.all_gather(norm1_shift, ("doc", "tm"), axis=0, tiled=True),
        lax.all_gather(qk_weight, ("doc", "tm"), axis=0, tiled=True),
        lax.all_gather(router_weight, ("doc", "tm"), axis=0, tiled=True),
        lax.all_gather(value_weight, ("doc", "tm"), axis=0, tiled=True),
        lax.all_gather(output_weight, ("doc", "tm"), axis=1, tiled=True),
        lax.all_gather(rel_bias, ("doc", "tm"), axis=1, tiled=True),
        lax.all_gather(norm2_gain, ("doc", "tm"), axis=0, tiled=True),
        lax.all_gather(norm2_shift, ("doc", "tm"), axis=0, tiled=True),
        lax.all_gather(ffn_in, ("doc", "tm"), axis=0, tiled=True),
        lax.all_gather(ffn_out, ("doc", "tm"), axis=0, tiled=True),
    )
    (
        gain_one,
        shift_one,
        w_qk,
        w_router,
        w_value,
        w_output,
        table_bf,
        gain_two,
        shift_two,
        w_in,
        w_out,
    ) = full_weights
    gain_one = gain_one.astype(jnp.float32)
    shift_one = shift_one.astype(jnp.float32)
    gain_two = gain_two.astype(jnp.float32)
    shift_two = shift_two.astype(jnp.float32)
    table = table_bf.astype(jnp.float32)
    router_f = w_router.astype(jnp.float32)
    inputs = tokens.reshape(row_count, model_width).astype(jnp.float32)
    counts = valid_counts.reshape(batches)
    starts = doc_starts.reshape(batches) > 0
    token_mask = (
        (jnp.arange(local_len, dtype=jnp.int32)[None, :] < counts[:, None])
        .astype(jnp.float32)
        .reshape(row_count, 1)
    )
    value_pick = selection(value_routes.reshape(row_count, HEADS, TOPK))
    output_pick = selection(output_routes.reshape(row_count, HEADS, TOPK))
    normed_one, norm1_unit, norm1_inv = norm_forward(inputs, gain_one, shift_one)
    act_one = normed_one.astype(jnp.bfloat16)
    qk_vals = jnp.dot(act_one, w_qk, preferred_element_type=jnp.float32).astype(jnp.bfloat16)
    gates = jax.nn.sigmoid(jnp.dot(act_one, w_router, preferred_element_type=jnp.float32))
    gate_value = gates[:, :head_experts].reshape(row_count, HEADS, EXPERTS) * value_pick
    gate_output = gates[:, head_experts:].reshape(row_count, HEADS, EXPERTS) * output_pick
    value_gate_t = jnp.transpose(gate_value, (0, 2, 1))[..., None]
    output_gate_t = jnp.transpose(gate_output, (0, 2, 1))[..., None]
    parts = jnp.dot(act_one, w_value, preferred_element_type=jnp.float32).reshape(
        row_count, EXPERTS, HEADS, HEAD_DIM
    )
    values = (
        jnp.sum(value_gate_t * parts, axis=1).reshape(row_count, inner_width).astype(jnp.bfloat16)
    )
    cache_own = jnp.concatenate([qk_vals[:, inner_width:], values], axis=1).reshape(
        batches, local_len, 2 * inner_width
    )
    given = given_cache.reshape(batches, MEM, 2 * inner_width)
    memory = memory_by_hops(cache_own, given, starts, local_len)
    queries = qk_vals[:, :inner_width].reshape(batches, local_len, HEADS, HEAD_DIM)
    keys = jnp.concatenate([memory[:, :, :inner_width], cache_own[:, :, :inner_width]], axis=1)
    keys = keys.reshape(batches, MEM + local_len, HEADS, HEAD_DIM)
    vals = jnp.concatenate([memory[:, :, inner_width:], cache_own[:, :, inner_width:]], axis=1)
    vals = vals.reshape(batches, MEM + local_len, HEADS, HEAD_DIM)
    scores, valid = attention_scores(queries, keys, table, counts)
    top = jnp.max(scores, axis=-1, keepdims=True)
    expo = jnp.exp(scores - top)
    denom = jnp.sum(expo, axis=-1, keepdims=True)
    log_total = top + jnp.log(denom)
    probs_b = (expo / denom).astype(jnp.bfloat16)
    attended = jnp.einsum("bhqk,bkhd->bqhd", probs_b, vals, preferred_element_type=jnp.float32)
    attended = attended.reshape(row_count, inner_width).astype(jnp.bfloat16)
    attended_f = attended.astype(jnp.float32).reshape(row_count, 1, HEADS, HEAD_DIM)
    mixed = (
        (output_gate_t * attended_f).reshape(row_count, EXPERTS * inner_width).astype(jnp.bfloat16)
    )
    hidden = inputs + jnp.dot(mixed, w_output, preferred_element_type=jnp.float32)
    normed_two, norm2_unit, norm2_inv = norm_forward(hidden, gain_two, shift_two)
    act_two = normed_two.astype(jnp.bfloat16)
    pre_act = jnp.dot(act_two, w_in, preferred_element_type=jnp.float32)
    activated = jax.nn.gelu(pre_act, approximate=False).astype(jnp.bfloat16)
    ffn_result = jnp.dot(activated, w_out, preferred_element_type=jnp.float32)
    layer_out = (token_mask * (hidden + ffn_result)).astype(jnp.bfloat16).reshape(tokens.shape)
    upstream = cotangent.reshape(row_count, model_width).astype(jnp.float32) * token_mask
    upstream_b = upstream.astype(jnp.bfloat16)
    d_out_w = jnp.einsum("nf,nd->fd", activated, upstream_b, preferred_element_type=jnp.float32)
    d_act = jnp.einsum("nd,fd->nf", upstream_b, w_out, preferred_element_type=jnp.float32)
    d_pre = (d_act * gelu_slope(pre_act)).astype(jnp.bfloat16)
    d_in_w = jnp.einsum("nd,nf->df", act_two, d_pre, preferred_element_type=jnp.float32)
    d_norm_two = jnp.einsum("nf,df->nd", d_pre, w_in, preferred_element_type=jnp.float32)
    d_from_two, d_gain_two, d_shift_two = norm_backward(d_norm_two, norm2_unit, norm2_inv, gain_two)
    d_hidden = upstream + d_from_two
    ffn_width = d_in_w.shape[1]
    d_branch = d_hidden.astype(jnp.bfloat16)
    d_output_t = jnp.einsum("nd,nk->dk", d_branch, mixed, preferred_element_type=jnp.float32)
    d_mixed = jnp.einsum(
        "nd,kd->nk", d_branch, w_output, preferred_element_type=jnp.float32
    ).astype(jnp.bfloat16)
    d_mixed = d_mixed.astype(jnp.float32).reshape(row_count, EXPERTS, HEADS, HEAD_DIM)
    d_gate_out = jnp.sum(d_mixed * attended_f, axis=-1)
    d_attended = (
        jnp.sum(d_mixed * output_gate_t, axis=1)
        .astype(jnp.bfloat16)
        .reshape(batches, local_len, HEADS, HEAD_DIM)
    )
    probs = jnp.where(valid, jnp.exp(scores - log_total), 0.0)
    d_probs = jnp.einsum("bqhd,bkhd->bhqk", d_attended, vals, preferred_element_type=jnp.float32)
    delta = jnp.sum(d_probs * probs, axis=-1, keepdims=True)
    d_scores = probs * (d_probs - delta)
    score_sum = jnp.sum(d_scores, axis=0)
    d_table = bias_backward(score_sum, local_len)
    d_scores_b = d_scores.astype(jnp.bfloat16)
    scale = HEAD_DIM ** (-0.5)
    d_queries = (
        jnp.einsum("bhqk,bkhd->bqhd", d_scores_b, keys, preferred_element_type=jnp.float32) * scale
    )
    d_keys = (
        jnp.einsum(
            "bhqk,bqhd->bkhd", d_scores_b[..., MEM:], queries, preferred_element_type=jnp.float32
        )
        * scale
    )
    d_vals = jnp.einsum(
        "bhqk,bqhd->bkhd", probs_b[..., MEM:], d_attended, preferred_element_type=jnp.float32
    )
    d_qk = jnp.concatenate(
        [d_queries.reshape(row_count, inner_width), d_keys.reshape(row_count, inner_width)], axis=1
    ).astype(jnp.bfloat16)
    d_values = (
        d_vals.reshape(row_count, 1, HEADS, HEAD_DIM).astype(jnp.bfloat16).astype(jnp.float32)
    )
    d_gate_val = jnp.sum(parts * d_values, axis=-1)
    d_parts = (
        (value_gate_t * d_values).reshape(row_count, EXPERTS * inner_width).astype(jnp.bfloat16)
    )
    d_gates = jnp.concatenate(
        [
            jnp.transpose(d_gate_val, (0, 2, 1)).reshape(row_count, head_experts)
            * value_pick.reshape(row_count, head_experts),
            jnp.transpose(d_gate_out, (0, 2, 1)).reshape(row_count, head_experts)
            * output_pick.reshape(row_count, head_experts),
        ],
        axis=1,
    )
    d_logits = d_gates * gates * (1.0 - gates)
    d_qk_w = jnp.einsum("nd,nk->dk", act_one, d_qk, preferred_element_type=jnp.float32)
    d_value_w = jnp.einsum("nd,nk->dk", act_one, d_parts, preferred_element_type=jnp.float32)
    d_router_w = jnp.einsum("nd,nk->dk", act_one.astype(jnp.float32), d_logits, precision=HIGH)
    d_norm_one = jnp.einsum("nk,dk->nd", d_qk, w_qk, preferred_element_type=jnp.float32)
    d_norm_one = d_norm_one + jnp.einsum(
        "nk,dk->nd", d_parts, w_value, preferred_element_type=jnp.float32
    )
    d_norm_one = d_norm_one + jnp.einsum("nk,dk->nd", d_logits, router_f, precision=HIGH)
    d_from_one, d_gain_one, d_shift_one = norm_backward(d_norm_one, norm1_unit, norm1_inv, gain_one)
    input_grad = (d_hidden + d_from_one).reshape(tokens.shape)
    shares = (
        lax.psum_scatter(d_gain_one, ("doc", "tm"), scatter_dimension=0, tiled=True),
        lax.psum_scatter(d_shift_one, ("doc", "tm"), scatter_dimension=0, tiled=True),
        lax.psum_scatter(flatten(d_qk_w), ("doc", "tm"), scatter_dimension=0, tiled=True),
        lax.psum_scatter(flatten(d_router_w), ("doc", "tm"), scatter_dimension=0, tiled=True),
        lax.psum_scatter(flatten(d_value_w), ("doc", "tm"), scatter_dimension=0, tiled=True),
        lax.psum_scatter(flatten(d_output_t), ("doc", "tm"), scatter_dimension=0, tiled=True),
        lax.psum_scatter(d_table, ("doc", "tm"), scatter_dimension=1, tiled=True),
        lax.psum_scatter(d_gain_two, ("doc", "tm"), scatter_dimension=0, tiled=True),
        lax.psum_scatter(d_shift_two, ("doc", "tm"), scatter_dimension=0, tiled=True),
        lax.psum_scatter(flatten(d_in_w), ("doc", "tm"), scatter_dimension=0, tiled=True),
        lax.psum_scatter(flatten(d_out_w), ("doc", "tm"), scatter_dimension=0, tiled=True),
    )
    qk_share = shares[2].reshape(-1, 2 * inner_width)
    router_share = shares[3].reshape(-1, 2 * head_experts)
    value_share = shares[4].reshape(-1, EXPERTS * inner_width)
    output_share = shares[5].reshape(-1, EXPERTS * inner_width).T
    in_share = shares[9].reshape(-1, ffn_width)
    out_share = shares[10].reshape(-1, model_width)
    return (
        layer_out,
        input_grad,
        shares[0],
        shares[1],
        qk_share,
        router_share,
        value_share,
        output_share,
        shares[6],
        shares[7],
        shares[8],
        in_share,
        out_share,
    )


def solution(mesh):
    return jax.shard_map(
        on_device,
        mesh=mesh,
        in_specs=(
            P(None, "doc", "tm", None),
            P(None, "doc", "tm", None),
            P(None, "doc", "tm", None),
            P(None, "doc", "tm", None, None),
            P(None, "doc", "tm", None, None),
            P(None, "doc", "tm"),
            P(None, "doc", "tm"),
            P(("doc", "tm")),
            P(("doc", "tm")),
            P(("doc", "tm"), None),
            P(("doc", "tm"), None),
            P(("doc", "tm"), None),
            P(None, ("doc", "tm")),
            P(None, ("doc", "tm")),
            P(("doc", "tm")),
            P(("doc", "tm")),
            P(("doc", "tm"), None),
            P(("doc", "tm"), None),
        ),
        out_specs=(
            P(None, "doc", "tm", None),
            P(None, "doc", "tm", None),
            P(("doc", "tm")),
            P(("doc", "tm")),
            P(("doc", "tm"), None),
            P(("doc", "tm"), None),
            P(("doc", "tm"), None),
            P(None, ("doc", "tm")),
            P(None, ("doc", "tm")),
            P(("doc", "tm")),
            P(("doc", "tm")),
            P(("doc", "tm"), None),
            P(("doc", "tm"), None),
        ),
        check_vma=False,
    )
```

profile of v0, /device:TPU:0, one launch (start us, length us, event | category | flops | bytes accessed | tf_op | source)
XLA Modules:
  0.0 1624.5 jit_solution(9024831273839024242)
XLA Ops:
  11.2 6.4 collective-permute-start.6
  24.9 3.8 slice.202
  34.1 71.1 %all-reduce.20 = (bf16[1024]{0:T(1024)(128)(2,1)S(1)}, bf16[1024]{0:T(1024)(128)(2,1)S(1)}, bf16[1024]{0:T(1024)(128)(2,1)S(1)}, bf16[1024]{0:T(1024)(128)(2,1)S(1)}) all-reduce(bf16[1024]{0:T(1024)(128)(2,1)S(1)} %dynamic-update-slice.1, bf16[1024]{0:T(1024)(128)(2,1)S(1)} %dynamic-update-slice, ...), channel_id=1, replica_groups=mesh['doc'=4,'tm'=8] {'doc','tm'}, use_global_device_ids=true, to_apply=%add.4 | all-reduce | flops 4096 | bytes 16384
  105.3 40.6 %all-gather = bf16[32,8,4]{1,2,0:T(4,128)(2,1)S(1)} all-gather(bf16[1,8,4]{1,2,0:T(4,128)(2,1)S(1)} %bitcast.229), channel_id=1, replica_groups=mesh['doc'=4,'tm'=8] {'doc','tm'}, dimensions={0}, use_global_device_ids=true | all-gather | bytes 2112 | tf_op jit(solution)/shard_map/all_gather | solution.py:173
  146.0 38.3 %all_gather.35 = bf16[1024,40]{1,0:T(8,128)(2,1)S(1)} all-gather(bf16[32,40]{1,0:T(8,128)(2,1)S(1)} %copy-done.38), channel_id=1, replica_groups=mesh['doc'=4,'tm'=8] {'doc','tm'}, dimensions={0}, use_global_device_ids=true | all-gather | bytes 84480 | tf_op jit(solution)/shard_map/all_gather | solution.py:170
  200.3 6.2 reshape.483
  222.3 4.4 collective-permute-start.13
  240.7 6.6 copy.98
  247.3 6.0 multiply_reduce_fusion.2
  257.1 223.7 %collective-permute-done.10 = bf16[2,384,896]{2,1,0:T(8,128)(2,1)} collective-permute-done((bf16[2,384,896]{2,1,0:T(8,128)(2,1)}, bf16[2,384,896]{2,1,0:T(8,128)(2,1)}, u32[]{:S(2)}, u32[]{:S(2)}) %collective-permute-start.10) | collective-permute-done | bytes 1376288 | tf_op jit(solution)/shard_map/ppermute | solution.py:28
  486.9 94.1 %collective-permute-start.15 = (bf16[2,128,896]{2,1,0:T(8,128)(2,1)}, bf16[2,128,896]{2,1,0:T(8,128)(2,1)S(1)}, u32[]{:S(2)}, u32[]{:S(2)}) collective-permute-start(bf16[2,128,896]{2,1,0:T(8,128)(2,1)} %bitcast.16), channel_id=1, source_target_pairs={{0,7},{8,15},{16,23},{24,31}} | collective-permute-start | bytes 1376264 | tf_op jit(solution)/shard_map/ppermute | solution.py:28
  595.8 25.9 %collective-permute-done.16 = bf16[2,128,896]{2,1,0:T(8,128)(2,1)S(1)} collective-permute-done((bf16[2,128,896]{2,1,0:T(8,128)(2,1)}, bf16[2,128,896]{2,1,0:T(8,128)(2,1)S(1)}, u32[]{:S(2)}, u32[]{:S(2)}) %collective-permute-start.16) | collective-permute-done | bytes 458784 | tf_op jit(solution)/shard_map/ppermute | solution.py:28
  625.1 6.4 collective-permute-done.17
  633.4 7.1 collective-permute-done.18
  649.2 4.2 copy.100
  653.4 4.2 copy.102
  667.1 4.2 fusion.115
  672.6 15.5 fusion.5
  688.2 6.9 fusion
  709.7 5.1 fusion.78
  714.8 8.3 convolution_bitcast_fusion.1
  734.1 4.6 reshape.490
  738.7 11.2 reshape.496
  749.9 6.4 fusion.119
  756.3 11.2 reshape.494
  767.5 14.7 copy.139
  784.6 8.1 copy.140
  794.9 5.8 reshape.498
  804.8 3.9 fusion.117
  811.7 53.0 %all-reduce.18 = (f32[1024]{0:T(1024)S(1)}, f32[1024]{0:T(1024)S(1)}, f32[4,256]{1,0:T(4,128)S(1)}, f32[1024]{0:T(1024)S(1)}, f32[1024]{0:T(1024)S(1)}) all-reduce(f32[1024]{0:T(1024)S(1)} %get-tuple-element.67, f32[1024]{0:T(1024)S(1)} %get-tuple-element.74, ...), channel_id=2, replica_groups=mesh['doc'=4,'tm'=8] {'doc','tm'}, use_global_device_ids=true, to_apply=%region_18.19.clone | all-reduce | flops 5120 | bytes 40960
  870.2 7.4 fusion.22
  877.6 729.2 %all-reduce.23.cloned.1.call-done = (f32[917504]{0:T(1024)}, f32[40960]{0:T(1024)}, f32[2293760]{0:T(1024)}, f32[2293760]{0:T(1024)}, f32[4194304]{0:T(1024)}, /*index=5*/f32[4194304]{0:T(1024)}) async-done(((f32[917504]{0:T(1024)}, f32[40960]{0:T(1024)}, f32[2293760]{0:T(1024)}, f32[2293760]{0:T(1024)}, f32[4194304]{0:T(1024)}, /*index=5*/f32[4194304]{0:T(1024)}), (f32[917504]{0:T(1024)}, f32[40960]{0:T(1024)}, ...) | async-done | bytes 55738384
  (351 shorter events, 164.4 us)
Async XLA Ops:
  7.2 230.4 %all-gather.7.cloned.1.call-start = ((), (), s32[]{:S(2)}) async-start(), calls=%async_computation | async-start | bytes 1892352 | tf_op jit(solution)/shard_map/all_gather | solution.py:169
  7.9 232.8 %all-gather.9.cloned.1.call-start = ((), (), s32[]{:S(2)}) async-start(), calls=%async_computation.1 | async-start | bytes 4866048 | tf_op jit(solution)/shard_map/all_gather | solution.py:171
  8.7 658.5 %all-gather.11.cloned.1.call-start = ((), (), s32[]{:S(2)}) async-start(), calls=%async_computation.2 | async-start | bytes 4866048 | tf_op jit(solution)/shard_map/all_gather | solution.py:172
  9.4 663.2 %all-gather.13.cloned.1.call-start = ((), (), s32[]{:S(2)}) async-start(), calls=%async_computation.3 | async-start | bytes 8650752 | tf_op jit(solution)/shard_map/all_gather | solution.py:176
  10.0 678.2 %all-gather.15.cloned.1.call-start = ((), (), s32[]{:S(2)}) async-start(), calls=%async_computation.4 | async-start | bytes 8650752 | tf_op jit(solution)/shard_map/all_gather | solution.py:177
  11.2 197.8 %collective-permute-start.6 = (bf16[2]{0:T(256)(128)(2,1)}, bf16[2]{0:T(256)(128)(2,1)S(1)}, u32[]{:S(2)}, u32[]{:S(2)}) collective-permute-start(bf16[2]{0:T(256)(128)(2,1)} %get-tuple-element.115), channel_id=1, source_target_pairs={{0,7},{8,15},{16,23},{24,31}} | collective-permute-start | bytes 20 | tf_op jit(solution)/shard_map/ppermute | solution.py:28
  17.6 192.7 %collective-permute-start.5 = (bf16[2]{0:T(256)(128)(2,1)}, bf16[2]{0:T(256)(128)(2,1)S(1)}, u32[]{:S(2)}, u32[]{:S(2)}) collective-permute-start(bf16[2]{0:T(256)(128)(2,1)} %get-tuple-element.115), channel_id=1, source_target_pairs={{0,6},{1,7},{8,14},{9,15},{16,22},{17,23},{24,30},{25,31}} | collective-permute-start | bytes 20 | tf_op jit(solution)/shard_map/ppermute | solution.py:28
  18.9 194.6 %collective-permute-start.4 = (bf16[2]{0:T(256)(128)(2,1)}, bf16[2]{0:T(256)(128)(2,1)S(1)}, u32[]{:S(2)}, u32[]{:S(2)}) collective-permute-start(bf16[2]{0:T(256)(128)(2,1)} %get-tuple-element.115), channel_id=1, source_target_pairs={{0,5},{1,6},{2,7},{8,13},{9,14},{10,15},{16,21},{17,22},{18,23},{2... | collective-permute-start | bytes 20 | tf_op jit(solution)/shard_map/ppermute | solution.py:28
  22.5 164.3 %copy-start.25 = (bf16[2,1,128,1024]{3,2,1,0:T(8,128)(2,1)S(1)}, bf16[2,1,128,1024]{3,2,1,0:T(8,128)(2,1)}, u32[]{:S(2)}) copy-start(bf16[2,1,128,1024]{3,2,1,0:T(8,128)(2,1)} %param.19) | copy-start | bytes 1572868
  22.5 210.3 %collective-permute-start.9 = (bf16[2,256,896]{2,1,0:T(8,128)(2,1)}, bf16[2,256,896]{2,1,0:T(8,128)(2,1)}, u32[]{:S(2)}, u32[]{:S(2)}) collective-permute-start(bf16[2,256,896]{2,1,0:T(8,128)(2,1)} %slice.192), channel_id=1, source_target_pairs={{0,6},{1,7},{8,14},{9,15},{16,22},{17,23},{24,30},{25,31}} | collective-permute-start | bytes 2752520 | tf_op jit(solution)/shard_map/ppermute | solution.py:28
  28.8 556.1 %collective-permute-start.14 = (bf16[2,896,896]{2,1,0:T(8,128)(2,1)}, bf16[2,896,896]{2,1,0:T(8,128)(2,1)}, u32[]{:S(2)}, u32[]{:S(2)}) collective-permute-start(bf16[2,896,896]{2,1,0:T(8,128)(2,1)} %slice.202), channel_id=1, source_target_pairs={{0,1},{1,2},{2,3},{3,4},{4,5},{5,6},{6,7},{8,9},{9,10},{10,11},{11... | collective-permute-start | bytes 9633800 | tf_op jit(solution)/shard_map/ppermute | solution.py:28
  32.5 1574.4 %all-reduce.23.cloned.1.call-start = ((), (), s32[]{:S(2)}) async-start(), calls=%async_computation.5 | async-start | bytes 111476736
  209.0 5.9 collective-permute-start.3
  210.3 7.2 collective-permute-start.2
  213.5 6.1 collective-permute-start.1
  214.9 7.4 collective-permute-start
  217.5 12.7 collective-permute-start.8
  219.6 362.6 %collective-permute-start.12 = (bf16[2,640,896]{2,1,0:T(8,128)(2,1)}, bf16[2,640,896]{2,1,0:T(8,128)(2,1)}, u32[]{:S(2)}, u32[]{:S(2)}) collective-permute-start(bf16[2,640,896]{2,1,0:T(8,128)(2,1)} %slice.198), channel_id=1, source_target_pairs={{0,3},{1,4},{2,5},{3,6},{4,7},{8,11},{9,12},{10,13},{11,14},{12,15... | collective-permute-start | bytes 6881288 | tf_op jit(solution)/shard_map/ppermute | solution.py:28
  222.3 361.3 %collective-permute-start.13 = (bf16[2,768,896]{2,1,0:T(8,128)(2,1)}, bf16[2,768,896]{2,1,0:T(8,128)(2,1)}, u32[]{:S(2)}, u32[]{:S(2)}) collective-permute-start(bf16[2,768,896]{2,1,0:T(8,128)(2,1)} %slice.200), channel_id=1, source_target_pairs={{0,2},{1,3},{2,4},{3,5},{4,6},{5,7},{8,10},{9,11},{10,12},{11,13},... | collective-permute-start | bytes 8257544 | tf_op jit(solution)/shard_map/ppermute | solution.py:28
  230.2 256.7 %collective-permute-start.11 = (bf16[2,512,896]{2,1,0:T(8,128)(2,1)}, bf16[2,512,896]{2,1,0:T(8,128)(2,1)}, u32[]{:S(2)}, u32[]{:S(2)}) collective-permute-start(bf16[2,512,896]{2,1,0:T(8,128)(2,1)} %slice.196), channel_id=1, source_target_pairs={{0,4},{1,5},{2,6},{3,7},{8,12},{9,13},{10,14},{11,15},{16,20},{17,... | collective-permute-start | bytes 5505032 | tf_op jit(solution)/shard_map/ppermute | solution.py:28
  232.8 248.0 %collective-permute-start.10 = (bf16[2,384,896]{2,1,0:T(8,128)(2,1)}, bf16[2,384,896]{2,1,0:T(8,128)(2,1)}, u32[]{:S(2)}, u32[]{:S(2)}) collective-permute-start(bf16[2,384,896]{2,1,0:T(8,128)(2,1)} %slice.194), channel_id=1, source_target_pairs={{0,5},{1,6},{2,7},{8,13},{9,14},{10,15},{16,21},{17,22},{18,23},{2... | collective-permute-start | bytes 4128776 | tf_op jit(solution)/shard_map/ppermute | solution.py:28
  253.3 340.2 %copy-start.43 = (pred[2]{0:T(512)(128)(4,1)S(1)}, pred[2]{0:T(512)(128)(4,1)}, u32[]{:S(2)}) copy-start(pred[2]{0:T(512)(128)(4,1)} %compare_and_fusion.2) | copy-start | bytes 10
  253.3 340.2 %copy-start.48 = (pred[2]{0:T(512)(128)(4,1)S(1)}, pred[2]{0:T(512)(128)(4,1)}, u32[]{:S(2)}) copy-start(pred[2]{0:T(512)(128)(4,1)} %compare_and_fusion.1) | copy-start | bytes 10
  253.3 340.2 %copy-start.53 = (pred[2]{0:T(512)(128)(4,1)S(1)}, pred[2]{0:T(512)(128)(4,1)}, u32[]{:S(2)}) copy-start(pred[2]{0:T(512)(128)(4,1)} %get-tuple-element.91) | copy-start | bytes 10
  480.8 105.4 %collective-permute-start.7 = (bf16[2,128,896]{2,1,0:T(8,128)(2,1)}, bf16[2,128,896]{2,1,0:T(8,128)(2,1)}, u32[]{:S(2)}, u32[]{:S(2)}) collective-permute-start(bf16[2,128,896]{2,1,0:T(8,128)(2,1)} %bitcast.16), channel_id=1, source_target_pairs={} | collective-permute-start | bytes 1376264 | tf_op jit(solution)/shard_map/ppermute | solution.py:28
  486.9 105.2 %collective-permute-start.15 = (bf16[2,128,896]{2,1,0:T(8,128)(2,1)}, bf16[2,128,896]{2,1,0:T(8,128)(2,1)S(1)}, u32[]{:S(2)}, u32[]{:S(2)}) collective-permute-start(bf16[2,128,896]{2,1,0:T(8,128)(2,1)} %bitcast.16), channel_id=1, source_target_pairs={{0,7},{8,15},{16,23},{24,31}} | collective-permute-start | bytes 1376264 | tf_op jit(solution)/shard_map/ppermute | solution.py:28
  582.2 62.7 %collective-permute-start.21 = (bf16[2,128,896]{2,1,0:T(8,128)(2,1)}, bf16[2,128,896]{2,1,0:T(8,128)(2,1)S(1)}, u32[]{:S(2)}, u32[]{:S(2)}) collective-permute-start(bf16[2,128,896]{2,1,0:T(8,128)(2,1)} %bitcast.16), channel_id=1, source_target_pairs={{0,1},{1,2},{2,3},{3,4},{4,5},{5,6},{6,7},{8,9},{9,10},{10,11},{11... | collective-permute-start | bytes 1376264 | tf_op jit(solution)/shard_map/ppermute | solution.py:28
  583.6 60.0 %collective-permute-start.20 = (bf16[2,128,896]{2,1,0:T(8,128)(2,1)}, bf16[2,128,896]{2,1,0:T(8,128)(2,1)S(1)}, u32[]{:S(2)}, u32[]{:S(2)}) collective-permute-start(bf16[2,128,896]{2,1,0:T(8,128)(2,1)} %bitcast.16), channel_id=1, source_target_pairs={{0,2},{1,3},{2,4},{3,5},{4,6},{5,7},{8,10},{9,11},{10,12},{11,13},... | collective-permute-start | bytes 1376264 | tf_op jit(solution)/shard_map/ppermute | solution.py:28
  584.9 57.2 %collective-permute-start.19 = (bf16[2,128,896]{2,1,0:T(8,128)(2,1)}, bf16[2,128,896]{2,1,0:T(8,128)(2,1)S(1)}, u32[]{:S(2)}, u32[]{:S(2)}) collective-permute-start(bf16[2,128,896]{2,1,0:T(8,128)(2,1)} %bitcast.16), channel_id=1, source_target_pairs={{0,3},{1,4},{2,5},{3,6},{4,7},{8,11},{9,12},{10,13},{11,14},{12,15... | collective-permute-start | bytes 1376264 | tf_op jit(solution)/shard_map/ppermute | solution.py:28
  586.2 35.4 %collective-permute-start.16 = (bf16[2,128,896]{2,1,0:T(8,128)(2,1)}, bf16[2,128,896]{2,1,0:T(8,128)(2,1)S(1)}, u32[]{:S(2)}, u32[]{:S(2)}) collective-permute-start(bf16[2,128,896]{2,1,0:T(8,128)(2,1)} %bitcast.16), channel_id=1, source_target_pairs={{0,6},{1,7},{8,14},{9,15},{16,22},{17,23},{24,30},{25,31}} | collective-permute-start | bytes 1376264 | tf_op jit(solution)/shard_map/ppermute | solution.py:28
  592.2 39.3 %collective-permute-start.17 = (bf16[2,128,896]{2,1,0:T(8,128)(2,1)}, bf16[2,128,896]{2,1,0:T(8,128)(2,1)S(1)}, u32[]{:S(2)}, u32[]{:S(2)}) collective-permute-start(bf16[2,128,896]{2,1,0:T(8,128)(2,1)} %bitcast.16), channel_id=1, source_target_pairs={{0,5},{1,6},{2,7},{8,13},{9,14},{10,15},{16,21},{17,22},{18,23},{2... | collective-permute-start | bytes 1376264 | tf_op jit(solution)/shard_map/ppermute | solution.py:28
  621.7 18.7 %collective-permute-start.18 = (bf16[2,128,896]{2,1,0:T(8,128)(2,1)}, bf16[2,128,896]{2,1,0:T(8,128)(2,1)S(1)}, u32[]{:S(2)}, u32[]{:S(2)}) collective-permute-start(bf16[2,128,896]{2,1,0:T(8,128)(2,1)} %bitcast.16), channel_id=1, source_target_pairs={{0,4},{1,5},{2,6},{3,7},{8,12},{9,13},{10,14},{11,15},{16,20},{17,... | collective-permute-start | bytes 1376264 | tf_op jit(solution)/shard_map/ppermute | solution.py:28
  (72 other events, 2072.5 us)
Sparse Core Ops, SparseCore 0:
  10.9 73.3 all-gather.6
  87.3 63.1 all-gather.8
  153.5 62.7 all-gather.10
  219.1 103.9 all-gather.12
  326.0 104.5 all-gather.14
  792.8 814.0 all-reduce.22
where the time goes:
time: 1640 us; the launch traced here: 1620 us
  waiting for transfers between devices  998 us (61%)
  blocking collectives  203 us (12%)
  starting transfers between devices  142 us (9%)
  local copies, waits for them, and re-layouts  135 us (8%)
  matrix products  91.2 us (6%)
  other arithmetic  38.6 us (2%)
    unnamed x7, waiting for transfers between devices  732 us
    ppermute x22, waiting for transfers between devices, from_behind(): lax.ppermute(value, axis, [(source, source + steps) for source in range(f...  267 us
    ppermute x22, starting transfers between devices, from_behind(): lax.ppermute(value, axis, [(source, source + steps) for source in range(f...  142 us
    unnamed x2, blocking collectives  124 us
    unnamed x180, local copies, waits for them, and re-layouts  42 us
    all_gather x1, blocking collectives, on_device(): lax.all_gather(rel_bias, ('doc', 'tm'), axis=1, tiled=True)  40.6 us
    all_gather x1, blocking collectives, on_device(): lax.all_gather(router_weight, ('doc', 'tm'), axis=0, tiled=True)  38.3 us
  transfers between devices with their start and end apart: 28, of which 7 were waited for; matrix products, arithmetic and copies ran while one was open for 9% of the time, Pallas kernels for 0%

commit v1 on v0

--- a/solution.py
+++ b/solution.py
@@ -1,6 +1,10 @@
+import functools
+
 import jax
 import jax.numpy as jnp
 from jax import lax
+from jax.experimental import pallas as pl
+from jax.experimental.pallas import tpu as pltpu
 from jax.sharding import PartitionSpec as P
 
 HEADS = 4
@@ -356,9 +360,695 @@
     )
 
 
+MESH = pl.DeviceIdType.MESH
+PAD = 128
+SIDE = 2
+HALF_HEADS = HEADS // SIDE
+W_QK = 2 * HALF_HEADS * PAD
+W_VAL = EXPERTS * HALF_HEADS * PAD
+W_MISC = 128
+W_A = W_QK + W_VAL + W_MISC
+W_O = EXPERTS * HALF_HEADS * PAD
+MISC = W_QK + W_VAL
+N_ROUTE = 2 * HALF_HEADS * EXPERTS
+COL_NORM = N_ROUTE
+COL_BIAS = N_ROUTE + 4
+VMEM_BYTES = 60 * 1024 * 1024
+SCALE = HEAD_DIM ** (-0.5)
+
+
+def pad_last(a, width):
+    return jnp.pad(a, [(0, 0)] * (a.ndim - 1) + [(0, width - a.shape[-1])])
+
+
+def swap(a):
+    count = lax.axis_size("tm")
+    return lax.ppermute(a, "tm", [(i, i ^ 1) for i in range(count)])
+
+
+def neighbours(count):
+    d, t = lax.axis_index("doc"), lax.axis_index("tm")
+    z, c = t // 2, t % 2
+    return dict(
+        c=(d, z * 2 + 1 - c),
+        x=(d + 1 - 2 * (d % 2), t),
+        y=((d + 2) % 4, t),
+        up=(d, jnp.minimum(t + 2, count - 1)),
+        down=(d, jnp.maximum(t - 2, 0)),
+    )
+
+
+def enter(nb, z, levels):
+    barrier = pltpu.get_barrier_semaphore()
+    for name in ("c", "x", "y"):
+        pl.semaphore_signal(barrier, inc=1, device_id=nb[name], device_id_type=MESH)
+
+    @pl.when(z < levels - 1)
+    def _():
+        pl.semaphore_signal(barrier, inc=1, device_id=nb["up"], device_id_type=MESH)
+
+    @pl.when(z > 0)
+    def _():
+        pl.semaphore_signal(barrier, inc=1, device_id=nb["down"], device_id_type=MESH)
+
+    ends = jnp.where(z < levels - 1, 1, 0) + jnp.where(z > 0, 1, 0)
+    pl.semaphore_wait(barrier, 3 + ends)
+
+
+class Gather:
+    def __init__(self, ref, sems, nb, d, z, levels):
+        self.ref, self.nb, self.d, self.z, self.levels = ref, nb, d, z, levels
+        self.send, self.recv = sems
+        self.half = ref.shape[2] // 2
+
+    def copy(self, part, slot, to):
+        return pltpu.make_async_remote_copy(
+            src_ref=part, dst_ref=part, send_sem=self.send.at[slot], recv_sem=self.recv.at[slot],
+            device_id=self.nb[to], device_id_type=MESH)
+
+    def along(self, level, distance, to):
+        base = 0 if to == "up" else self.levels
+        return self.copy(self.ref.at[self.d, level], base + distance, to)
+
+    def across(self, level, to, column=None):
+        base = (2 if to == "x" else 3) * self.levels
+        column = self.d if column is None else column
+        return self.copy(self.ref.at[column, level], base + level, to)
+
+    def corner(self, level, to, column):
+        base = (4 if to == "x" else 5) * self.levels
+        rows = pl.ds(self.half, self.half) if to == "x" else pl.ds(0, self.half)
+        return self.copy(self.ref.at[column, level, rows], base + level, to)
+
+    def begin(self):
+        z, levels = self.z, self.levels
+
+        @pl.when(z < levels - 1)
+        def _():
+            self.along(z, 1, "up").start()
+
+        @pl.when(z > 0)
+        def _():
+            self.along(z, 1, "down").start()
+
+        self.across(z, "x").start()
+        self.across(z, "y").start()
+
+    def line(self, k):
+        z, levels = self.z, self.levels
+
+        @pl.when(z >= k)
+        def _():
+            self.along(z - k, k, "up").wait_recv()
+
+            @pl.when(z < levels - 1)
+            def _():
+                self.along(z - k, k + 1, "up").start()
+
+            self.across(z - k, "x").start()
+            self.across(z - k, "y").start()
+
+        @pl.when(z + k < levels)
+        def _():
+            self.along(z + k, k, "down").wait_recv()
+
+            @pl.when(z > 0)
+            def _():
+                self.along(z + k, k + 1, "down").start()
+
+            self.across(z + k, "x").start()
+            self.across(z + k, "y").start()
+
+    def turn(self, k):
+        z, levels, d = self.z, self.levels, self.d
+        by_x, by_y = d + 1 - 2 * (d % 2), (d + 2) % 4
+
+        def one(level):
+            self.across(level, "x").wait_recv()
+            self.corner(level, "y", by_x).start()
+            self.across(level, "y").wait_recv()
+            self.corner(level, "x", by_y).start()
+
+        if k == 0:
+            one(z)
+        else:
+            pl.when(z >= k)(lambda: one(z - k))
+            pl.when(z + k < levels)(lambda: one(z + k))
+
+    def finish(self, k):
+        z, levels, d = self.z, self.levels, self.d
+        by_x, by_y = d + 1 - 2 * (d % 2), (d + 2) % 4
+
+        def one(level):
+            self.corner(level, "x", by_y).wait_recv()
+            self.corner(level, "y", by_x).wait_recv()
+
+        if k == 0:
+            one(z)
+        else:
+            pl.when(z >= k)(lambda: one(z - k))
+            pl.when(z + k < levels)(lambda: one(z + k))
+
+    def drain(self):
+        z, levels, d = self.z, self.levels, self.d
+        by_x, by_y = d + 1 - 2 * (d % 2), (d + 2) % 4
+        for level in range(levels):
+            self.across(level, "x").wait_send()
+            self.across(level, "y").wait_send()
+            self.corner(level, "x", by_y).wait_send()
+            self.corner(level, "y", by_x).wait_send()
+        for k in range(1, levels):
+
+            @pl.when(jnp.logical_and(z >= k - 1, z < levels - 1))
+            def _():
+                self.along(z - k + 1, k, "up").wait_send()
+
+            @pl.when(jnp.logical_and(z + k - 1 < levels, z > 0))
+            def _():
+                self.along(z + k - 1, k, "down").wait_send()
+
+
+def gather_kernel(
+    levels, a_in, o_in, i_in, f_in, x_in, g_in,
+    a_all, o_all, i_all, f_all, x_all, g_all,
+    send, recv, csend, crecv, lsem,
+):
+    d, t = lax.axis_index("doc"), lax.axis_index("tm")
+    z, c = t // 2, t % 2
+    nb = neighbours(2 * levels)
+    rows = a_in.shape[1]
+    own = pl.ds(pl.multiple_of(c * rows, 16), rows)
+    locals_, remotes = [], []
+
+    def place(index, src_mine, src_other, dst):
+        locals_.append(pltpu.make_async_copy(src_mine, dst, lsem.at[index]))
+        if src_other is not None:
+            remotes.append(pltpu.make_async_remote_copy(
+                src_ref=src_other, dst_ref=dst, send_sem=csend.at[index], recv_sem=crecv.at[index],
+                device_id=nb["c"], device_id_type=MESH))
+
+    place(0, a_in.at[c], a_in.at[1 - c], a_all.at[d, z, own])
+    place(1, o_in.at[c], o_in.at[1 - c], o_all.at[d, z, own])
+    place(2, i_in.at[c], i_in.at[1 - c], i_all.at[d, z, own])
+    place(3, x_in, x_in, x_all.at[c])
+    place(4, g_in.at[c], g_in.at[1 - c], g_all.at[c])
+    place(5, f_in, None, f_all.at[d, z])
+    for cp in locals_:
+        cp.start()
+    enter(nb, z, levels)
+    for cp in remotes:
+        cp.start()
+    groups = [
+        Gather(ref, (send.at[i], recv.at[i]), nb, d, z, levels)
+        for i, ref in enumerate((a_all, o_all, i_all, f_all))
+    ]
+    for i, group in enumerate(groups):
+        if i < 3:
+            locals_[i].wait()
+            remotes[i].wait()
+        else:
+            locals_[5].wait()
+        group.begin()
+        for k in range(1, levels):
+            group.line(k)
+        if i:
+            for k in range(levels):
+                groups[i - 1].turn(k)
+    for k in range(levels):
+        groups[-1].turn(k)
+    for group in groups:
+        for k in range(levels):
+            group.finish(k)
+        group.drain()
+    locals_[3].wait()
+    locals_[4].wait()
+    remotes[3].wait()
+    remotes[4].wait()
+
+
+def gather(levels, packs):
+    a, o, i, f, x, g = packs
+    two = lambda v: (4, levels, 2 * v.shape[1], v.shape[2])
+    shapes = [two(a), two(o), two(i), (4, levels) + f.shape, (2,) + x.shape, (2,) + g.shape[1:]]
+    hbm = pl.BlockSpec(memory_space=pl.ANY)
+    return pl.pallas_call(
+        functools.partial(gather_kernel, levels),
+        out_shape=[jax.ShapeDtypeStruct(s, jnp.bfloat16) for s in shapes],
+        in_specs=[hbm] * 6,
+        out_specs=[hbm] * 6,
+        scratch_shapes=[
+            pltpu.SemaphoreType.DMA((4, 6 * levels)),
+            pltpu.SemaphoreType.DMA((4, 6 * levels)),
+            pltpu.SemaphoreType.DMA((6,)),
+            pltpu.SemaphoreType.DMA((6,)),
+            pltpu.SemaphoreType.DMA((6,)),
+        ],
+        compiler_params=pltpu.CompilerParams(
+            collective_id=1, has_side_effects=True, vmem_limit_bytes=VMEM_BYTES),
+    )(a, o, i, f, x, g)
+
+
+def add_rows(dst, terms):
+    rows, width = dst.shape
+    step = 16
+
+    def body(i, carry):
+        at = pl.ds(pl.multiple_of(i * step, step), step)
+        total = terms[0][at].astype(jnp.float32)
+        for term in terms[1:]:
+            total = total + term[at].astype(jnp.float32)
+        dst[at] = total.astype(dst.dtype)
+        return carry
+
+    lax.fori_loop(0, rows // step, body, 0)
+
+
+class Scatter:
+    def __init__(self, src, bufs, sems, nb, d, z, levels):
+        self.src, self.nb, self.d, self.z, self.levels = src, nb, d, z, levels
+        self.cx, self.cy, self.rx, self.ry, self.up, self.down = bufs
+        self.send, self.recv = sems
+        self.half = src.shape[2] // 2
+        self.by_x, self.by_y = d + 1 - 2 * (d % 2), (d + 2) % 4
+        self.low, self.high = pl.ds(0, self.half), pl.ds(self.half, self.half)
+
+    def copy(self, src, dst, slot, to):
+        return pltpu.make_async_remote_copy(
+            src_ref=src, dst_ref=dst, send_sem=self.send.at[slot], recv_sem=self.recv.at[slot],
+            device_id=self.nb[to], device_id_type=MESH)
+
+    def corner(self, j, to):
+        part = self.low if to == "x" else self.high
+        buf = self.cx if to == "x" else self.cy
+        return self.copy(self.src.at[3 - self.d, j, part], buf.at[j], (0 if to == "x" else self.levels) + j, to)
+
+    def direct(self, j, to):
+        part = self.low if to == "x" else self.high
+        column = self.by_x if to == "x" else self.by_y
+        buf = self.rx if to == "x" else self.ry
+        return self.copy(self.src.at[column, j, part], buf.at[j, part], (2 if to == "x" else 3) * self.levels + j, to)
+
+    def relay(self, j, to):
+        part = self.high if to == "x" else self.low
+        held = self.cy if to == "x" else self.cx
+        buf = self.rx if to == "x" else self.ry
+        return self.copy(held.at[j], buf.at[j, part], (4 if to == "x" else 5) * self.levels + j, to)
+
+    def along(self, j, to):
+        buf = self.up if to == "up" else self.down
+        return self.copy(buf.at[j], buf.at[j], (6 if to == "up" else 7) * self.levels + j, to)
+
+    def begin(self):
+        for j in range(self.levels):
+            self.corner(j, "x").start()
+            self.corner(j, "y").start()
+        for j in range(self.levels):
+            self.direct(j, "x").start()
+            self.direct(j, "y").start()
+
+    def turn(self, j):
+        self.corner(j, "x").wait_recv()
+        add_rows(self.cx.at[j], [self.cx.at[j], self.src.at[self.by_y, j, self.low]])
+        self.relay(j, "y").start()
+        self.corner(j, "y").wait_recv()
+        add_rows(self.cy.at[j], [self.cy.at[j], self.src.at[self.by_x, j, self.high]])
+        self.relay(j, "x").start()
+
+    def column(self, j):
+        self.direct(j, "x").wait_recv()
+        self.direct(j, "y").wait_recv()
+        self.relay(j, "x").wait_recv()
+        self.relay(j, "y").wait_recv()
+        add_rows(self.rx.at[j], [self.rx.at[j], self.ry.at[j], self.src.at[self.d, j]])
+
+    def line(self, j):
+        z, levels = self.z, self.levels
+
+        @pl.when(z < j)
+        def _():
+            @pl.when(z > 0)
+            def _():
+                self.along(j, "up").wait_recv()
+                add_rows(self.up.at[j], [self.up.at[j], self.rx.at[j]])
+
+            @pl.when(z == 0)
+            def _():
+                add_rows(self.up.at[j], [self.rx.at[j]])
+
+            self.along(j, "up").start()
+
+        @pl.when(z > j)
+        def _():
+            @pl.when(z < levels - 1)
+            def _():
+                self.along(j, "down").wait_recv()
+                add_rows(self.down.at[j], [self.down.at[j], self.rx.at[j]])
+
+            @pl.when(z == levels - 1)
+            def _():
+                add_rows(self.down.at[j], [self.rx.at[j]])
+
+            self.along(j, "down").start()
+
+    def total(self, dst):
+        z, levels = self.z, self.levels
+
+        @pl.when(z == 0)
+        def _():
+            self.along(z, "down").wait_recv()
+            add_rows(dst, [self.rx.at[z], self.down.at[z]])
+
+        @pl.when(z == levels - 1)
+        def _():
+            self.along(z, "up").wait_recv()
+            add_rows(dst, [self.rx.at[z], self.up.at[z]])
+
+        @pl.when(jnp.logical_and(z > 0, z < levels - 1))
+        def _():
+            self.along(z, "up").wait_recv()
+            self.along(z, "down").wait_recv()
+            add_rows(dst, [self.rx.at[z], self.up.at[z], self.down.at[z]])
+
+    def drain(self):
+        for j in range(self.levels):
+            for to in ("x", "y"):
+                self.corner(j, to).wait_send()
+                self.direct(j, to).wait_send()
+                self.relay(j, to).wait_send()
+            pl.when(self.z < j)(lambda: self.along(j, "up").wait_send())
+            pl.when(self.z > j)(lambda: self.along(j, "down").wait_send())
+
+
+def scatter_kernel(levels, *refs):
+    d, t = lax.axis_index("doc"), lax.axis_index("tm")
+    z = t // 2
+    nb = neighbours(2 * levels)
+    count = 4
+    srcs, dsts = refs[:count], refs[count : 2 * count]
+    bufs = refs[2 * count : -2]
+    send, recv = refs[-2:]
+    enter(nb, z, levels)
+    groups = [
+        Scatter(srcs[i], bufs[6 * i : 6 * i + 6], (send.at[i], recv.at[i]), nb, d, z, levels)
+        for i in range(count)
+    ]
+    for group in groups:
+        group.begin()
+    for group in groups:
+        for j in range(levels):
+            group.turn(j)
+    for group in groups:
+        for j in range(levels):
+            group.column(j)
+        for j in range(levels):
+            group.line(j)
+    for group, dst in zip(groups, dsts):
+        group.total(dst)
+    for group in groups:
+        group.drain()
+
+
+def scatter(levels, parts):
+    scratch = []
+    for p in parts:
+        rows, width = p.shape[2:]
+        for r in (rows // 2, rows // 2, rows, rows, rows, rows):
+            scratch.append(pltpu.VMEM((levels, r, width), jnp.bfloat16))
+    vmem = pl.BlockSpec(memory_space=pltpu.VMEM)
+    return pl.pallas_call(
+        functools.partial(scatter_kernel, levels),
+        out_shape=[jax.ShapeDtypeStruct(p.shape[2:], jnp.float32) for p in parts],
+        in_specs=[vmem] * 4,
+        out_specs=[vmem] * 4,
+        scratch_shapes=scratch + [pltpu.SemaphoreType.DMA((4, 8 * levels))] * 2,
+        compiler_params=pltpu.CompilerParams(
+            collective_id=2, has_side_effects=True, vmem_limit_bytes=VMEM_BYTES),
+    )(*parts)
+
+
+def split_heads(a, lead):
+    rows = a.shape[0]
+    a = pad_last(a.reshape(rows, lead, SIDE, HALF_HEADS, HEAD_DIM), PAD)
+    return jnp.transpose(a, (2, 0, 1, 3, 4)).reshape(SIDE, rows, lead * HALF_HEADS * PAD)
+
+
+def join_heads(a, lead):
+    rows = a.shape[1]
+    a = a.reshape(SIDE, rows, lead, HALF_HEADS, PAD)[..., :HEAD_DIM]
+    return jnp.transpose(a, (1, 2, 0, 3, 4)).reshape(rows, lead * HEADS * HEAD_DIM)
+
+
+def shared_memory(cache, given, starts, levels):
+    count = 2 * levels
+    up = [(i, i + 2) for i in range(count - 2)]
+    local_len = cache.shape[2]
+
+    def follow(before, block):
+        moved = jnp.concatenate([before[0][:, local_len:], before[1]], axis=1)
+        return jnp.where(starts[block][:, None, None], given[block], moved)
+
+    odd = given[1]
+    for _ in range(levels):
+        arrived = lax.ppermute((odd, cache[1]), "tm", up)
+        even = follow(arrived, 0)
+        odd = follow((even, cache[0]), 1)
+    return jnp.stack([even, odd])
+
+
+def bias_of(table, local_len):
+    spread = MEM + 2 * local_len - 1
+    window = MEM + local_len
+    by_distance = jnp.einsum("hc,kc->hk", table, bucket_matrix(local_len), precision=HIGH)
+    heads = table.shape[0]
+    turned = jnp.concatenate([by_distance[:, ::-1], jnp.zeros((heads, 1), jnp.float32)], axis=1)
+    tiled = jnp.tile(turned, (1, local_len))[:, : local_len * spread].reshape(heads, local_len, spread)
+    return tiled[:, :, local_len - 1 : local_len - 1 + window]
+
+
+def bias_grad(score_sum, local_len):
+    heads = score_sum.shape[0]
+    spread = MEM + 2 * local_len - 1
+    padded = jnp.pad(score_sum, ((0, 0), (0, 0), (local_len - 1, 0))).reshape(heads, local_len * spread)
+    padded = jnp.pad(padded, ((0, 0), (0, local_len))).reshape(heads, local_len, spread + 1)
+    by_distance = jnp.sum(padded, axis=1)[:, :spread][:, ::-1]
+    return jnp.einsum("hk,kc->hc", by_distance, bucket_matrix(local_len), precision=HIGH)
+
+
+def on_chip(
+    tokens, cotangent, given_cache, value_routes, output_routes, valid_counts, doc_starts,
+    norm1_gain, norm1_shift, qk_weight, router_weight, value_weight, output_weight, rel_bias,
+    norm2_gain, norm2_shift, ffn_in, ffn_out,
+):
+    batches, unused_row, local_len, width = tokens.shape
+    count = lax.axis_size("tm")
+    levels = count // 2
+    side = lax.axis_index("tm") % 2
+    rows = batches * local_len
+    shard = qk_weight.shape[0]
+    blocks = 4 * levels
+    bf16, f32 = jnp.bfloat16, jnp.float32
+
+    a_qk = split_heads(qk_weight, 2)
+    a_v = split_heads(value_weight, EXPERTS)
+    a_o = split_heads(output_weight.T, EXPERTS)
+    route = jnp.transpose(
+        router_weight.reshape(shard, 2, SIDE, HALF_HEADS * EXPERTS), (2, 0, 1, 3)
+    ).reshape(SIDE, shard, N_ROUTE)
+    norms = jnp.broadcast_to(
+        jnp.stack([norm1_gain, norm1_shift, norm2_gain, norm2_shift], axis=1)[None], (SIDE, shard, 4))
+    buckets = rel_bias.shape[1]
+    bias_cols = jnp.pad(
+        jnp.transpose(rel_bias.reshape(SIDE, HALF_HEADS, buckets), (0, 2, 1)),
+        ((0, 0), (0, shard - buckets), (0, 0)))
+    misc = pad_last(jnp.concatenate([route, norms, bias_cols], axis=2), W_MISC)
+    a_pack = jnp.concatenate([a_qk, a_v, misc], axis=2)
+    hidden_block = ffn_out.shape[0]
+    i_pack = jnp.transpose(
+        ffn_in.reshape(shard, blocks, SIDE, hidden_block), (2, 0, 1, 3)
+    ).reshape(SIDE, shard, blocks * hidden_block)
+
+    mask = (jnp.arange(local_len)[None, :] < valid_counts.reshape(batches, 1)).astype(f32).reshape(rows, 1)
+    x_own = tokens.reshape(rows, width)
+    grad_own = (cotangent.reshape(rows, width).astype(f32) * mask).astype(bf16)
+    picks = [
+        jnp.transpose(
+            selection(r.reshape(rows, SIDE, HALF_HEADS, TOPK)).reshape(rows, SIDE, HALF_HEADS * EXPERTS), (1, 0, 2))
+        for r in (value_routes, output_routes)
+    ]
+    starts_col = jnp.repeat(doc_starts.reshape(batches), local_len).reshape(rows, 1).astype(bf16)
+    counts_col = jnp.repeat(valid_counts.reshape(batches), local_len).reshape(rows, 1).astype(bf16)
+    meta = pad_last(
+        jnp.concatenate(
+            [picks[0][0], picks[1][0], picks[0][1], picks[1][1], starts_col, counts_col], axis=1).astype(bf16),
+        128)
+    x_pack = jnp.concatenate([x_own, grad_own, meta], axis=1)
+    given = given_cache.reshape(batches * MEM, 2 * HEADS * HEAD_DIM)
+    g_pack = split_heads(given, 2)
+
+    a_all, o_all, i_all, f_all, x_all, g_all = gather(levels, (a_pack, a_o, i_pack, ffn_out, x_pack, g_pack))
+    w_a = a_all.reshape(width, W_A)
+    w_o = o_all.reshape(width, W_O)
+    w_i = i_all.reshape(width, -1)
+    w_f = f_all.reshape(-1, width)
+
+    vectors = w_a[:, MISC + COL_NORM : MISC + COL_NORM + 4].T.astype(f32)
+    gain_one, shift_one, gain_two, shift_two = [v.reshape(1, width) for v in vectors]
+    table = w_a[:, MISC + COL_BIAS : MISC + COL_BIAS + HALF_HEADS].reshape(4 * count, shard, HALF_HEADS)
+    table = jnp.transpose(table[:, :buckets].reshape(BUCKETS, HALF_HEADS)).astype(f32)
+
+    both = 2 * rows
+    inputs = x_all[:, :, :width].reshape(both, width).astype(f32)
+    grad_all = x_all[:, :, width : 2 * width].reshape(both, width)
+    meta_all = x_all[:, :, 2 * width :].reshape(both, 128)
+    pick_mine = jnp.where(side == 0, meta_all[:, :N_ROUTE], meta_all[:, N_ROUTE : 2 * N_ROUTE]).astype(f32)
+    tail = meta_all[:, 2 * N_ROUTE : 2 * N_ROUTE + 2].reshape(2, batches, local_len, 2)[:, :, 0]
+    starts = tail[..., 0] > 0
+    counts = tail[..., 1].astype(jnp.int32)
+
+    normed_one, unit_one, inv_one = norm_forward(inputs, gain_one, shift_one)
+    act_one = normed_one.astype(bf16)
+    front = jnp.dot(act_one, w_a, preferred_element_type=f32)
+    qk = front[:, :W_QK].astype(bf16)
+    parts = front[:, W_QK:MISC].reshape(both, EXPERTS, HALF_HEADS, PAD)
+    gates = jax.nn.sigmoid(front[:, MISC : MISC + N_ROUTE])
+    gated = (gates * pick_mine).reshape(both, 2, HALF_HEADS, EXPERTS)
+    value_gate = jnp.transpose(gated[:, 0], (0, 2, 1))[..., None]
+    output_gate = jnp.transpose(gated[:, 1], (0, 2, 1))[..., None]
+    values = jnp.sum(value_gate * parts, axis=1).reshape(both, HALF_HEADS * PAD).astype(bf16)
+    wide = HALF_HEADS * PAD
+    queries, keys_own = qk[:, :wide], qk[:, wide:]
+    cache = jnp.concatenate([keys_own, values], axis=1).reshape(2, batches, local_len, 2 * wide)
+    memory = shared_memory(cache, g_all.reshape(2, batches, MEM, 2 * wide), starts, levels)
+    window = jnp.concatenate([memory, cache], axis=2).reshape(2 * batches, MEM + local_len, 2, HALF_HEADS, PAD)
+    keys, vals = window[:, :, 0], window[:, :, 1]
+    queries = queries.reshape(2 * batches, local_len, HALF_HEADS, PAD)
+    raw = jnp.einsum("bqhd,bkhd->bhqk", queries, keys, preferred_element_type=f32) * SCALE
+    row_ids = jnp.arange(local_len, dtype=jnp.int32)[:, None]
+    own_ids = jnp.arange(MEM + local_len, dtype=jnp.int32)[None, :] - MEM
+    valid = jnp.logical_or(
+        own_ids[None, None] < 0,
+        jnp.logical_and((own_ids <= row_ids)[None, None], own_ids[None, None] < counts.reshape(-1)[:, None, None, None]))
+    scores = jnp.where(valid, raw + bias_of(table, local_len)[None], NEG)
+    top = jnp.max(scores, axis=-1, keepdims=True)
+    expo = jnp.exp(scores - top)
+    denom = jnp.sum(expo, axis=-1, keepdims=True)
+    probs = expo / denom
+    probs_b = probs.astype(bf16)
+    attended = jnp.einsum("bhqk,bkhd->bqhd", probs_b, vals, preferred_element_type=f32)
+    attended = attended.reshape(both, wide).astype(bf16)
+    attended_f = attended.astype(f32).reshape(both, 1, HALF_HEADS, PAD)
+    mixed = (output_gate * attended_f).reshape(both, W_O).astype(bf16)
+    branch = jnp.dot(mixed, w_o.T, preferred_element_type=f32).reshape(2, rows, width)
+
+    def mine(a):
+        return lax.dynamic_index_in_dim(a, side, 0, keepdims=False)
+
+    def other(a):
+        return lax.dynamic_index_in_dim(a, 1 - side, 0, keepdims=False)
+
+    def paired(own):
+        arrived = swap(own)
+        return jnp.where(side == 0, jnp.stack([own, arrived]), jnp.stack([arrived, own])).reshape(both, -1)
+
+    hidden = x_own.astype(f32) + mine(branch) + swap(other(branch))
+
+    normed_two, unit_two, inv_two = norm_forward(hidden, gain_two, shift_two)
+    act_two = paired(normed_two.astype(bf16))
+    pre_act = jnp.dot(act_two, w_i, preferred_element_type=f32)
+    activated = jax.nn.gelu(pre_act, approximate=False).astype(bf16)
+    ffn = jnp.dot(activated, w_f, preferred_element_type=f32).reshape(2, rows, width)
+    layer_out = (mask * (hidden + mine(ffn) + swap(other(ffn)))).astype(bf16).reshape(tokens.shape)
+    d_f = jnp.einsum("nf,nd->fd", activated, grad_all, preferred_element_type=f32).astype(bf16)
+    d_act = jnp.einsum("nd,fd->nf", grad_all, w_f, preferred_element_type=f32)
+    d_pre = (d_act * gelu_slope(pre_act)).astype(bf16)
+    d_i = jnp.einsum("nd,nf->df", act_two, d_pre, preferred_element_type=f32).astype(bf16)
+    d_two = jnp.einsum("nf,df->nd", d_pre, w_i, preferred_element_type=f32).reshape(2, rows, width)
+    d_two = mine(d_two) + swap(other(d_two))
+    d_from_two, d_gain_two, d_shift_two = norm_backward(d_two, unit_two, inv_two, gain_two)
+    upstream = cotangent.reshape(rows, width).astype(f32) * mask
+    d_hidden = upstream + d_from_two
+
+    d_branch = paired(d_hidden.astype(bf16))
+    d_o = jnp.einsum("nd,nk->dk", d_branch, mixed, preferred_element_type=f32).astype(bf16)
+    d_mixed = jnp.dot(d_branch, w_o, preferred_element_type=f32).astype(bf16)
+    d_mixed = d_mixed.astype(f32).reshape(both, EXPERTS, HALF_HEADS, PAD)
+    d_gate_out = jnp.sum(d_mixed * attended_f, axis=-1)
+    d_attended = jnp.sum(d_mixed * output_gate, axis=1).astype(bf16).reshape(2 * batches, local_len, HALF_HEADS, PAD)
+    d_probs = jnp.einsum("bqhd,bkhd->bhqk", d_attended, vals, preferred_element_type=f32)
+    delta = jnp.sum(d_probs * probs, axis=-1, keepdims=True)
+    d_scores = probs * (d_probs - delta)
+    d_table = bias_grad(jnp.sum(d_scores, axis=0), local_len)
+    d_scores_b = d_scores.astype(bf16)
+    d_queries = jnp.einsum("bhqk,bkhd->bqhd", d_scores_b, keys, preferred_element_type=f32) * SCALE
+    d_keys = jnp.einsum("bhqk,bqhd->bkhd", d_scores_b[..., MEM:], queries, preferred_element_type=f32) * SCALE
+    d_vals = jnp.einsum("bhqk,bqhd->bkhd", probs_b[..., MEM:], d_attended, preferred_element_type=f32)
+    d_values = d_vals.reshape(both, 1, HALF_HEADS, PAD).astype(bf16).astype(f32)
+    d_gate_val = jnp.sum(parts * d_values, axis=-1)
+    d_parts = (value_gate * d_values).reshape(both, W_VAL).astype(bf16)
+    d_gates = jnp.concatenate(
+        [jnp.transpose(g, (0, 2, 1)).reshape(both, HALF_HEADS * EXPERTS) for g in (d_gate_val, d_gate_out)], axis=1)
+    d_logits = d_gates * pick_mine * gates * (1.0 - gates)
+    d_front = jnp.concatenate(
+        [
+            d_queries.reshape(both, wide).astype(bf16),
+            d_keys.reshape(both, wide).astype(bf16),
+            d_parts,
+            pad_last(d_logits.astype(bf16), W_MISC),
+        ],
+        axis=1,
+    )
+    d_a = jnp.einsum("nd,nk->dk", act_one, d_front, preferred_element_type=f32).astype(bf16)
+    d_one = jnp.einsum("nk,dk->nd", d_front, w_a, preferred_element_type=f32).reshape(2, rows, width)
+    d_one = mine(d_one) + swap(other(d_one))
+    d_from_one, d_gain_one, d_shift_one = norm_backward(
+        d_one, mine(unit_one.reshape(2, rows, width)), mine(inv_one.reshape(2, rows, 1)), gain_one)
+    input_grad = (d_hidden + d_from_one).reshape(tokens.shape)
+    d_norms = jnp.stack([d_gain_one, d_shift_one, d_gain_two, d_shift_two], axis=1)
+    d_bias = jnp.pad(
+        d_table.T.reshape(4 * count, buckets, HALF_HEADS), ((0, 0), (0, shard - buckets), (0, 0))
+    ).reshape(width, HALF_HEADS)
+    d_misc = jnp.concatenate([d_norms, d_bias], axis=1).astype(bf16)
+    d_a = jnp.concatenate([d_a[:, : MISC + N_ROUTE], d_misc, d_a[:, MISC + N_ROUTE + 4 + HALF_HEADS :]], axis=1)
+
+    s_a, s_o, s_i, s_f = scatter(
+        levels,
+        (
+            d_a.reshape(4, levels, 2 * shard, W_A),
+            d_o.reshape(4, levels, 2 * shard, W_O),
+            d_i.reshape(4, levels, 2 * shard, -1),
+            d_f.reshape(4, levels, hidden_block, width),
+        ),
+    )
+    chip = jnp.concatenate([s_a, s_o, s_i], axis=1).reshape(2, shard, -1)
+    kept, arrived = mine(chip), swap(other(chip))
+    sides = jnp.where(side == 0, jnp.stack([kept, arrived]), jnp.stack([arrived, kept]))
+    qk_share = join_heads(sides[:, :, :W_QK], 2)
+    value_share = join_heads(sides[:, :, W_QK:MISC], EXPERTS)
+    output_share = join_heads(sides[:, :, W_A : W_A + W_O], EXPERTS).T
+    misc = sides[:, :, MISC:W_A]
+    router_share = jnp.transpose(
+        misc[:, :, :N_ROUTE].reshape(SIDE, shard, 2, HALF_HEADS * EXPERTS), (1, 2, 0, 3)
+    ).reshape(shard, 2 * HEADS * EXPERTS)
+    norm_share = misc[0, :, COL_NORM : COL_NORM + 4] + misc[1, :, COL_NORM : COL_NORM + 4]
+    bias_share = jnp.transpose(misc[:, :buckets, COL_BIAS : COL_BIAS + HALF_HEADS], (0, 2, 1)).reshape(HEADS, buckets)
+    in_share = jnp.transpose(
+        sides[:, :, W_A + W_O :].reshape(SIDE, shard, blocks, hidden_block), (1, 2, 0, 3)
+    ).reshape(shard, -1)
+    return (
+        layer_out, input_grad, norm_share[:, 0], norm_share[:, 1], qk_share, router_share, value_share,
+        output_share, bias_share, norm_share[:, 2], norm_share[:, 3], in_share, s_f,
+    )
+
+
+def by_size(*args):
+    thin = args[9].shape[0] % 16 != 0
+    paired = lax.axis_size("doc") == 4 and lax.axis_size("tm") % 2 == 0
+    return on_device(*args) if thin or not paired else on_chip(*args)
+
+
 def solution(mesh):
     return jax.shard_map(
-        on_device,
+        by_size,
         mesh=mesh,
         in_specs=(
             P(None, "doc", "tm", None),

time: 1640 us -> 825 us (0.50)
  waiting for transfers between devices: 998 us -> 103 us
  Pallas kernels: 0 us -> 344 us
  blocking collectives: 203 us -> 0 us
  starting transfers between devices: 142 us -> 21.2 us
  local copies, waits for them, and re-layouts: 135 us -> 196 us
  other arithmetic: 38.6 us -> 81.8 us
  matrix products: 91.2 us -> 61 us
    unnamed x7 -> x0, waiting for transfers between devices: 732 us -> none
    pallas_call x0 -> x2, Pallas kernels: none -> 344 us  [the longest x1 173 us: scatter(): pl.pallas_call(functools.partial(scatter_kernel, levels), out_shape=[jax....]
    ppermute x22 -> x12, waiting for transfers between devices: 267 us -> 103 us  [the longest x5 97.9 us: shared_memory(): arrived = lax.ppermute((odd, cache[1]), 'tm', up)]
    unnamed x2 -> x0, blocking collectives: 124 us -> none
    ppermute x22 -> x12, starting transfers between devices: 142 us -> 21.2 us  [the longest x5 19.9 us: shared_memory(): arrived = lax.ppermute((odd, cache[1]), 'tm', up)]
    all_gather x2 -> x0, blocking collectives: 78.8 us -> none  [the longest x1 40.6 us: on_device(): lax.all_gather(rel_bias, ('doc', 'tm'), axis=1, tiled=True)]
    dot_general x26 -> x19, matrix products: 91.2 us -> 55.1 us  [the longest x1 11.7 us: on_chip(): pre_act = jnp.dot(act_two, w_i, preferred_element_type=f32)]
    another operation x0 -> x11, local copies, waits for them, and re-layouts: none -> 35.6 us  [the longest x2 31.8 us: split_heads(): a = pad_last(a.reshape(rows, lead, SIDE, HALF_HEADS, HEAD_DIM), PAD)]
  transfers between devices with their start and end apart: 28 -> 12, of which waited for: 7 -> 8; matrix products, arithmetic and copies ran while one was open for 9% -> 12% of each run, Pallas kernels for 0% -> 0%
where the time goes in v1:
time: 825 us; the launch traced here: 810 us
  Pallas kernels  344 us (42%)
  local copies, waits for them, and re-layouts  196 us (24%)
  waiting for transfers between devices  103 us (12%)
  other arithmetic  81.8 us (10%)
  matrix products  61 us (7%)
  starting transfers between devices  21.2 us (3%)
    pallas_call x1, Pallas kernels, scatter(): pl.pallas_call(functools.partial(scatter_kernel, levels), out_shape=[jax....  173 us
    pallas_call x1, Pallas kernels, gather(): pl.pallas_call(functools.partial(gather_kernel, levels), out_shape=[jax.S...  172 us
    ppermute x5, waiting for transfers between devices, shared_memory(): arrived = lax.ppermute((odd, cache[1]), 'tm', up)  97.9 us
    another operation x2, local copies, waits for them, and re-layouts, split_heads(): a = pad_last(a.reshape(rows, lead, SIDE, HALF_HEADS, HEAD_DIM), PAD)  31.8 us
    unnamed x170, local copies, waits for them, and re-layouts  24.7 us
    ppermute x5, starting transfers between devices, shared_memory(): arrived = lax.ppermute((odd, cache[1]), 'tm', up)  19.9 us
  transfers between devices with their start and end apart: 12, of which 8 were waited for; matrix products, arithmetic and copies ran while one was open for 12% of the time, Pallas kernels for 0%

profile of v1, /device:TPU:0, one launch (start us, length us, event | category | flops | bytes accessed | tf_op | source)
XLA Modules:
  0.0 810.0 jit_solution(15001007282774752011)
XLA Ops:
  13.2 20.7 %reshape.762 = bf16[2048,2,2,2,112]{4,3,2,1,0:T(2,128)(2,1)} reshape(bf16[2,1,1024,896]{3,2,1,0:T(8,128)(2,1)} %param.20) | data formatting | bytes 7340032 | tf_op jit(solution)/shard_map/reshape;reshape | solution.py:791
  34.0 11.1 %copy.561 = bf16[2048,2,2,2,112]{0,4,3,2,1:T(8,128)(2,1)} copy(bf16[2048,2,2,2,112]{4,3,2,1,0:T(2,128)(2,1)} %reshape.762) | data formatting | bytes 7340032 | tf_op jit(solution)/shard_map/reshape;reshape | solution.py:791
  45.0 4.6 pad_bitcast_fusion
  49.6 11.2 %copy.502 = bf16[2,2048,2,2,128]{4,3,2,1,0:T(2,128)(2,1)} copy(bf16[2,2048,2,2,128]{1,4,3,0,2:T(8,128)(2,1)} %pad_bitcast_fusion) | data formatting | bytes 8388608 | tf_op jit(solution)/shard_map/transpose | solution.py:792
  60.8 7.3 reshape.708.g_in
  70.3 171.5 %shard_map.273 = (bf16[4,4,64,1920]{3,2,1,0:T(8,128)(2,1)}, bf16[4,4,64,1280]{3,2,1,0:T(8,128)(2,1)}, bf16[4,4,64,2048]{3,2,1,0:T(8,128)(2,1)}, bf16[4,4,128,102...) custom-call(bf16[2,32,1920]{2,1,0:T(8,128)(2,1)} %fusion.74.a_in, ...), custom_call_target="tpu_custom_call" | custom-call | tf_op jit(solution)/shard_map/pallas_call | solution.py:594
  241.8 3.9 fusion.111
  277.0 5.5 multiply_reduce_fusion.4
  301.4 4.4 collective-permute-start.2
  305.8 41.8 %collective-permute-done.2 = bf16[2,1024,512]{1,2,0:T(8,128)(2,1)S(1)} collective-permute-done((bf16[2,1024,512]{1,2,0:T(8,128)(2,1)S(1)}, bf16[2,1024,512]{1,2,0:T(8,128)(2,1)S(1)}, u32[]{:S(2)}, u32[]{:S(2)}) %collective-permute-start.2) | collective-permute-done | bytes 2097184 | tf_op jit(solution)/shard_map/ppermute | solution.py:812
  348.4 3.8 fusion.27
  352.2 5.7 collective-permute-start.3
  362.8 35.9 %collective-permute-done.3 = bf16[2,1024,512]{1,2,0:T(8,128)(2,1)} collective-permute-done((bf16[2,1024,512]{1,2,0:T(8,128)(2,1)}, bf16[2,1024,512]{1,2,0:T(8,128)(2,1)}, u32[]{:S(2)}, u32[]{:S(2)}) %collective-permute-start.3) | collective-permute-done | bytes 2097184 | tf_op jit(solution)/shard_map/ppermute | solution.py:812
  400.9 3.8 fusion.28
  404.7 5.7 collective-permute-start.4
  413.1 4.0 reshape.717
  419.8 3.9 copy.524
  423.7 3.9 copy.521
  434.4 15.9 %collective-permute-done.4 = bf16[2,1024,512]{1,2,0:T(8,128)(2,1)} collective-permute-done((bf16[2,1024,512]{1,2,0:T(8,128)(2,1)}, bf16[2,1024,512]{1,2,0:T(8,128)(2,1)}, u32[]{:S(2)}, u32[]{:S(2)}) %collective-permute-start.4) | collective-permute-done | bytes 2097184 | tf_op jit(solution)/shard_map/ppermute | solution.py:812
  457.7 6.4 copy.525
  464.2 5.9 exponential_reduce_fusion
  476.8 5.1 multiply_convert_fusion.1
  481.9 4.2 convert_element_type.325
  499.2 11.7 %fusion.6 = (bf16[512,2048]{1,0:T(8,128)(2,1)S(1)}, f32[512,2048]{1,0:T(8,128)S(1)}) fusion(bf16[512,1024]{1,0:T(8,128)(2,1)S(1)} %bitcast.351, bf16[1024,2048]{1,0:T(8,128)(2,1)S(1)} %bitcast.412), kind=kOutput, calls=%fused_computation.15 | convolution fusion | flops 2215641088 | bytes 11534336 | tf_op jit(solution)/shard_map/dot_general | solution.py:957
  524.1 4.4 convert_element_type.352
  534.3 4.3 convolution_convert_fusion.1
  538.6 4.4 convolution_convert_fusion.2
  549.2 4.3 reshape.753
  553.5 9.3 %multiply_reduce_fusion.3 = (bf16[512,2,128]{2,1,0:T(2,128)(2,1)S(1)}, f32[512,5,2]{2,1,0:T(8,128)}) fusion(f32[512,5,2,128]{3,2,1,0:T(2,128)} %reshape.753, f32[512,5,2]{2,1,0:T(8,128)S(1)} %copy-done.3, f32[512,2,128]{2,1,0:T(2,128)S(1)} %copy-done.15), kind=kLoop, calls=%fused_computation.57 | loop fusion | flops 2485248 | bytes 3448832 | tf_op jit(solution)/shard_map/reduce_sum | solution.py:976
  572.6 8.1 multiply_convert_fusion
  616.7 7.8 concatenate.114
  624.5 172.8 %shard_map.274 = (f32[64,1920]{1,0:T(8,128)}, f32[64,1280]{1,0:T(8,128)}, f32[64,2048]{1,0:T(8,128)}, f32[128,1024]{1,0:T(8,128)}) custom-call(bf16[4,4,64,1920]{3,2,1,0:T(8,128)(2,1)} %bitcast.323, bf16[4,4,64,1280]{3,2,1,0:T(8,128)(2,1)} %bitcast.333, bf16[4,4,64,2048]{3,2,1,0:T(8,128)(2,1)} %bitcast.332, bf16[4,4,128,1024]{3,2,1,0:T(8,128)(2,1)} %bitcast.331), custom_call_target="tpu_custom_call" | custom-call | tf_op jit(solution)/shard_map/pallas_call | solution.py:778
  (378 shorter events, 194.0 us)
Async XLA Ops:
  0.6 11.5 %copy-start.42 = (bf16[32,4096]{1,0:T(8,128)(2,1)S(1)}, bf16[32,4096]{1,0:T(8,128)(2,1)}, u32[]{:S(2)}) copy-start(bf16[32,4096]{1,0:T(8,128)(2,1)} %param.34) | copy-start | bytes 786436
  2.9 65.3 %copy-start.59 = (f32[256]{0:T(256)}, f32[256]{0:T(256)S(1)}, u32[]{:S(2)}) copy-start(f32[256]{0:T(256)S(1)} %fusion.93) | copy-start | bytes 3076
  60.8 7.4 copy-start.21
  60.8 8.3 %copy-start.27 = (bf16[2,1,128,1024]{3,2,1,0:T(8,128)(2,1)S(1)}, bf16[2,1,128,1024]{3,2,1,0:T(8,128)(2,1)}, u32[]{:S(2)}) copy-start(bf16[2,1,128,1024]{3,2,1,0:T(8,128)(2,1)} %param.18) | copy-start | bytes 1572868
  245.7 19.2 %copy-start.4 = (bf16[1,2048,512]{2,1,0:T(8,128)(2,1)}, bf16[1,2048,512]{2,1,0:T(8,128)(2,1)S(1)}, u32[]{:S(2)}) copy-start(bf16[1,2048,512]{2,1,0:T(8,128)(2,1)S(1)} %get-tuple-element.158) | copy-start | bytes 6291460
  248.5 47.1 %collective-permute-start = (bf16[2,1024,512]{1,2,0:T(8,128)(2,1)}, bf16[2,1024,512]{1,2,0:T(8,128)(2,1)}, u32[]{:S(2)}, u32[]{:S(2)}) collective-permute-start(bf16[2,1024,512]{1,2,0:T(8,128)(2,1)} %copy.520), channel_id=1, source_target_pairs={{0,2},{1,3},{2,4},{3,5},{4,6},{5,7},{8,10},{9,11},{10,12},{11,13},... | collective-permute-start | bytes 6291464 | tf_op jit(solution)/shard_map/ppermute | solution.py:812
  256.6 10.4 %copy-start.43 = (bf16[512,20]{0,1:T(8,128)(2,1)}, bf16[512,20]{0,1:T(8,128)(2,1)S(1)}, u32[]{:S(2)}) copy-start(bf16[512,20]{0,1:T(8,128)(2,1)S(1)} %copy.569) | copy-start | bytes 61444
  256.8 10.2 %copy-start.45 = (bf16[512,20]{0,1:T(8,128)(2,1)}, bf16[512,20]{0,1:T(8,128)(2,1)S(1)}, u32[]{:S(2)}) copy-start(bf16[512,20]{0,1:T(8,128)(2,1)S(1)} %copy.568) | copy-start | bytes 61444
  274.2 8.3 %copy-start = (f32[512,5,2,128]{3,2,1,0:T(2,128)}, f32[512,5,2,128]{3,2,1,0:T(2,128)S(1)}, u32[]{:S(2)}) copy-start(f32[512,5,2,128]{3,2,1,0:T(2,128)S(1)} %reshape.713) | copy-start | bytes 7864324
  284.7 13.7 %collective-permute-start.1 = (bf16[2,128,512]{1,2,0:T(8,128)(2,1)}, bf16[2,128,512]{1,2,0:T(8,128)(2,1)S(1)}, u32[]{:S(2)}, u32[]{:S(2)}) collective-permute-start(bf16[2,128,512]{1,2,0:T(8,128)(2,1)} %copy.511), channel_id=1, source_target_pairs={{0,2},{1,3},{2,4},{3,5},{4,6},{5,7},{8,10},{9,11},{10,12},{11,13},... | collective-permute-start | bytes 786440 | tf_op jit(solution)/shard_map/ppermute | solution.py:812
  292.4 107.9 %copy-start.49 = (pred[2]{0:T(512)(128)(4,1)}, pred[2]{0:T(512)(128)(4,1)S(1)}, u32[]{:S(2)}) copy-start(pred[2]{0:T(512)(128)(4,1)S(1)} %get-tuple-element.148) | copy-start | bytes 10
  292.4 108.5 %copy-start.53 = (pred[2]{0:T(512)(128)(4,1)}, pred[2]{0:T(512)(128)(4,1)S(1)}, u32[]{:S(2)}) copy-start(pred[2]{0:T(512)(128)(4,1)S(1)} %get-tuple-element.147) | copy-start | bytes 10
  301.4 46.2 %collective-permute-start.2 = (bf16[2,1024,512]{1,2,0:T(8,128)(2,1)S(1)}, bf16[2,1024,512]{1,2,0:T(8,128)(2,1)S(1)}, u32[]{:S(2)}, u32[]{:S(2)}) collective-permute-start(bf16[2,1024,512]{1,2,0:T(8,128)(2,1)S(1)} %fusion.26), channel_id=1, source_target_pairs={{0,2},{1,3},{2,4},{3,5},{4,6},{5,7},{8,10},{9,11},{10,12},{11,13},... | collective-permute-start | bytes 6291464 | tf_op jit(solution)/shard_map/ppermute | solution.py:812
  352.2 46.4 %collective-permute-start.3 = (bf16[2,1024,512]{1,2,0:T(8,128)(2,1)}, bf16[2,1024,512]{1,2,0:T(8,128)(2,1)}, u32[]{:S(2)}, u32[]{:S(2)}) collective-permute-start(bf16[2,1024,512]{1,2,0:T(8,128)(2,1)} %fusion.27), channel_id=1, source_target_pairs={{0,2},{1,3},{2,4},{3,5},{4,6},{5,7},{8,10},{9,11},{10,12},{11,13},... | collective-permute-start | bytes 6291464 | tf_op jit(solution)/shard_map/ppermute | solution.py:812
  404.7 45.6 %collective-permute-start.4 = (bf16[2,1024,512]{1,2,0:T(8,128)(2,1)}, bf16[2,1024,512]{1,2,0:T(8,128)(2,1)}, u32[]{:S(2)}, u32[]{:S(2)}) collective-permute-start(bf16[2,1024,512]{1,2,0:T(8,128)(2,1)} %fusion.28), channel_id=1, source_target_pairs={{0,2},{1,3},{2,4},{3,5},{4,6},{5,7},{8,10},{9,11},{10,12},{11,13},... | collective-permute-start | bytes 6291464 | tf_op jit(solution)/shard_map/ppermute | solution.py:812
  434.4 17.7 %copy-start.11 = (bf16[1,2,1024,512]{2,3,1,0:T(8,128)(2,1)S(1)}, bf16[1,2,1024,512]{2,3,1,0:T(8,128)(2,1)}, u32[]{:S(2)}) copy-start(bf16[1,2,1024,512]{2,3,1,0:T(8,128)(2,1)} %copy.521) | copy-start | bytes 6291460
  434.4 17.7 %copy-start.50 = (pred[2]{0:T(512)(128)(4,1)S(1)}, pred[2]{0:T(512)(128)(4,1)}, u32[]{:S(2)}) copy-start(pred[2]{0:T(512)(128)(4,1)} %copy-done.49) | copy-start | bytes 10
  491.3 2.9 collective-permute-start.5
  496.6 2.0 collective-permute-start.6
  497.0 14.0 %copy-start.37 = (bf16[2,256,1024]{2,1,0:T(8,128)(2,1)}, bf16[2,256,1024]{2,1,0:T(8,128)(2,1)S(1)}, u32[]{:S(2)}) copy-start(bf16[2,256,1024]{2,1,0:T(8,128)(2,1)S(1)} %slice.257) | copy-start | bytes 3145732
  498.8 12.2 %copy-start.34 = (bf16[2,256,1024]{2,1,0:T(8,128)(2,1)}, bf16[2,256,1024]{2,1,0:T(8,128)(2,1)S(1)}, u32[]{:S(2)}) copy-start(bf16[2,256,1024]{2,1,0:T(8,128)(2,1)S(1)} %maximum_select_fusion.3) | copy-start | bytes 3145732
  499.2 11.8 %copy-start.62 = (bf16[4,4,128,1024]{3,2,1,0:T(8,128)(2,1)S(1)}, bf16[4,4,128,1024]{3,2,1,0:T(8,128)(2,1)}, u32[]{:S(2)}) copy-start(bf16[4,4,128,1024]{3,2,1,0:T(8,128)(2,1)} %get-tuple-element.28) | copy-start | bytes 12582916
  510.9 7.3 copy-start.67
  518.1 10.5 %collective-permute-start.8 = (f32[256,1024]{1,0:T(8,128)}, f32[256,1024]{1,0:T(8,128)}, u32[]{:S(2)}, u32[]{:S(2)}) collective-permute-start(f32[256,1024]{1,0:T(8,128)} %dynamic-slice_bitcast_fusion.1), channel_id=1, source_target_pairs={{0,1},{1,0},{2,3},{3,2},{4,5},{5,4},{6,7},{7,6},{8,9},{9,8},{10,11... | collective-permute-start | bytes 3145736 | tf_op jit(solution)/shard_map/ppermute | solution.py:386
  522.3 8.6 %collective-permute-start.7 = (f32[256,1024]{1,0:T(8,128)}, f32[256,1024]{1,0:T(8,128)}, u32[]{:S(2)}, u32[]{:S(2)}) collective-permute-start(f32[256,1024]{1,0:T(8,128)} %dynamic-slice_bitcast_fusion.2), channel_id=1, source_target_pairs={{0,1},{1,0},{2,3},{3,2},{4,5},{5,4},{6,7},{7,6},{8,9},{9,8},{10,11... | collective-permute-start | bytes 3145736 | tf_op jit(solution)/shard_map/ppermute | solution.py:386
  534.1 10.7 %collective-permute-start.9 = (bf16[256,1024]{1,0:T(8,128)(2,1)S(1)}, bf16[256,1024]{1,0:T(8,128)(2,1)S(1)}, u32[]{:S(2)}, u32[]{:S(2)}) collective-permute-start(bf16[256,1024]{1,0:T(8,128)(2,1)S(1)} %get-tuple-element.150), channel_id=1, source_target_pairs={{0,1},{1,0},{2,3},{3,2},{4,5},{5,4},{6,7},{7,6},{8,9},{9,8},{10,11... | collective-permute-start | bytes 1572872 | tf_op jit(solution)/shard_map/ppermute | solution.py:386
  549.2 15.0 %slice-start = ((s8[4718592]{0:T(1024)(128)(4,1)}), s8[524288]{0:T(1024)(128)(4,1)S(1)}, s32[]{:S(2)}) async-start(s8[4718592]{0:T(1024)(128)(4,1)} %bitcast.316), calls=%async_computation | async-start | bytes 1048576
  553.5 10.7 %slice-start.1 = ((s8[4718592]{0:T(1024)(128)(4,1)}), s8[4194304]{0:T(1024)(128)(4,1)S(1)}, s32[]{:S(2)}) async-start(s8[4718592]{0:T(1024)(128)(4,1)} %bitcast.316), calls=%async_computation.1 | async-start | bytes 8388608
  553.5 10.7 %copy-start.7 = (bf16[4,1024,2,2,128]{4,1,3,0,2:T(8,128)(2,1)S(1)}, bf16[4,1024,2,2,128]{4,1,3,0,2:T(8,128)(2,1)}, u32[]{:S(2)}) copy-start(bf16[4,1024,2,2,128]{4,1,3,0,2:T(8,128)(2,1)} %copy.525) | copy-start | bytes 12582916
  553.5 10.7 %copy-start.29 = (bf16[4,128,2,2,128]{4,1,3,0,2:T(8,128)(2,1)S(1)}, bf16[4,128,2,2,128]{4,1,3,0,2:T(8,128)(2,1)}, u32[]{:S(2)}) copy-start(bf16[4,128,2,2,128]{4,1,3,0,2:T(8,128)(2,1)} %copy.526) | copy-start | bytes 1572868
  605.4 7.7 collective-permute-start.10
  798.9 2.2 collective-permute-start.11
  (51 other events, 166.9 us)

commit v2 on v1

--- a/solution.py
+++ b/solution.py
@@ -528,81 +528,428 @@
                 self.along(z + k - 1, k, "down").wait_send()
 
 
-def gather_kernel(
-    levels, a_in, o_in, i_in, f_in, x_in, g_in,
-    a_all, o_all, i_all, f_all, x_all, g_all,
-    send, recv, csend, crecv, lsem,
+def selector(side):
+    inner = HEADS * HEAD_DIM
+    wide = HALF_HEADS * PAD
+    src = lax.broadcasted_iota(jnp.int32, (2 * inner, 2 * wide), 0)
+    dst = lax.broadcasted_iota(jnp.int32, (2 * inner, 2 * wide), 1)
+    kind, head, feature = dst // wide, (dst // PAD) % HALF_HEADS, dst % PAD
+    wanted = kind * inner + (side * HALF_HEADS + head) * HEAD_DIM + feature
+    hit = jnp.logical_and(src == wanted, feature < HEAD_DIM)
+    return jnp.where(hit, 1.0, 0.0).astype(jnp.bfloat16)
+
+
+def table_by_offset(w_a, per_device, shard, local_len, spread):
+    distance = MEM + local_len - 1 - lax.broadcasted_iota(jnp.int32, (1, spread), 1)
+    bucket = bucket_index(distance)
+    wanted = (bucket // per_device) * shard + bucket % per_device
+    step = 128
+
+    def body(i, total):
+        at = pl.ds(pl.multiple_of(i * step, step), step)
+        ids = lax.broadcasted_iota(jnp.int32, (step, spread), 0) + i * step
+        one_hot = jnp.where(ids == wanted, 1.0, 0.0).astype(jnp.bfloat16)
+        return total + dot_f32(w_a[at, MISC:W_A], one_hot, TN)
+
+    return lax.fori_loop(0, w_a.shape[0] // step, body, jnp.zeros((W_MISC, spread), jnp.float32))
+
+
+NT = (((1,), (1,)), ((), ()))
+TN = (((0,), (0,)), ((), ()))
+
+
+def dot_f32(a, b, dims=(((1,), (0,)), ((), ()))):
+    return lax.dot_general(a, b, dims, preferred_element_type=jnp.float32)
+
+
+def forward_kernel(
+    levels, batches, local_len, per_device,
+    a_in, o_in, i_in, f_in, x_in, g_in,
+    a_out, o_out, i_all, f_all, xs_out, act_out, front_out, gates_out, win_out, probs_out, att_out,
+    mixed_out, hidden_out, n2_out,
+    a_all, o_all, xs, graw, win, cr, sel, unit, act, front, gates, vec, bias, probs, att, mixed,
+    branch, arrived, hidden, n2,
+    send, recv, csend, crecv, lsem, gsend, grecv, msend, mrecv, esend, erecv, osem,
 ):
+    bf16, f32 = jnp.bfloat16, jnp.float32
     d, t = lax.axis_index("doc"), lax.axis_index("tm")
     z, c = t // 2, t % 2
     nb = neighbours(2 * levels)
-    rows = a_in.shape[1]
-    own = pl.ds(pl.multiple_of(c * rows, 16), rows)
-    locals_, remotes = [], []
-
-    def place(index, src_mine, src_other, dst):
-        locals_.append(pltpu.make_async_copy(src_mine, dst, lsem.at[index]))
-        if src_other is not None:
-            remotes.append(pltpu.make_async_remote_copy(
-                src_ref=src_other, dst_ref=dst, send_sem=csend.at[index], recv_sem=crecv.at[index],
-                device_id=nb["c"], device_id_type=MESH))
-
-    place(0, a_in.at[c], a_in.at[1 - c], a_all.at[d, z, own])
-    place(1, o_in.at[c], o_in.at[1 - c], o_all.at[d, z, own])
-    place(2, i_in.at[c], i_in.at[1 - c], i_all.at[d, z, own])
-    place(3, x_in, x_in, x_all.at[c])
-    place(4, g_in.at[c], g_in.at[1 - c], g_all.at[c])
-    place(5, f_in, None, f_all.at[d, z])
-    for cp in locals_:
+    shard = a_in.shape[1]
+    width = f_in.shape[1]
+    rows = batches * local_len
+    both = 2 * rows
+    wide = HALF_HEADS * PAD
+    own = pl.ds(pl.multiple_of(c * shard, 16), shard)
+    reach = cr.shape[0]
+
+    def local(src, dst, index):
+        cp = pltpu.make_async_copy(src, dst, lsem.at[index])
         cp.start()
+        return cp
+
+    def sibling(src, dst, index):
+        return pltpu.make_async_remote_copy(
+            src_ref=src, dst_ref=dst, send_sem=csend.at[index], recv_sem=crecv.at[index],
+            device_id=nb["c"], device_id_type=MESH)
+
+    loc_a = local(a_in.at[c], a_all.at[d, z, own], 0)
+    loc_x = local(x_in, xs.at[c], 1)
+    loc_g = local(g_in, graw.at[c], 2)
+    loc_o = local(o_in.at[c], o_all.at[d, z, own], 3)
+    loc_i = local(i_in.at[c], i_all.at[d, z, own], 4)
+    loc_f = local(f_in, f_all.at[d, z], 5)
     enter(nb, z, levels)
-    for cp in remotes:
+    rem_a = sibling(a_in.at[1 - c], a_all.at[d, z, own], 0)
+    rem_x = sibling(x_in, xs.at[c], 1)
+    rem_g = sibling(g_in, graw.at[c], 2)
+    rem_o = sibling(o_in.at[1 - c], o_all.at[d, z, own], 3)
+    rem_i = sibling(i_in.at[1 - c], i_all.at[d, z, own], 4)
+    for cp in (rem_a, rem_x, rem_g, rem_o, rem_i):
         cp.start()
-    groups = [
+    ga, go, gi, gf = [
         Gather(ref, (send.at[i], recv.at[i]), nb, d, z, levels)
         for i, ref in enumerate((a_all, o_all, i_all, f_all))
     ]
-    for i, group in enumerate(groups):
-        if i < 3:
-            locals_[i].wait()
-            remotes[i].wait()
-        else:
-            locals_[5].wait()
-        group.begin()
-        for k in range(1, levels):
-            group.line(k)
-        if i:
-            for k in range(levels):
-                groups[i - 1].turn(k)
+    loc_a.wait()
+    rem_a.wait()
+    ga.begin()
+    sel[...] = selector(c)
+
+    loc_x.wait()
+    rem_x.wait()
+    step = 64
+
+    def stats(i, carry):
+        at = pl.ds(pl.multiple_of((i % (rows // step)) * step, step), step)
+        block = i // (rows // step)
+        values = xs[block, at, :width].astype(f32)
+        centered = values - jnp.mean(values, axis=-1, keepdims=True)
+        inverse = lax.rsqrt(jnp.mean(centered * centered, axis=-1, keepdims=True) + EPS)
+        unit[pl.ds(pl.multiple_of(i * step, step), step)] = centered * inverse
+        return carry
+
+    lax.fori_loop(0, both // step, stats, 0)
+    ga.line(1)
+
+    def slot(s):
+        return pl.ds(s * local_len, local_len)
+
+    def starts_of(block, batch):
+        column = xs[block, pl.ds(batch * local_len, local_len), 2 * width : 2 * width + 128]
+        return column[:, 40:41].astype(f32)
+
+    def place(block, s, follow):
+        for batch in range(batches):
+            at = block * batches + batch
+            mine = dot_f32(graw[block, batch, slot(s)], sel[...]).astype(bf16)
+            if follow:
+                moved = win[at, slot(s)] if block == 0 else win[batch, slot(s + 1)]
+                first = jnp.broadcast_to(starts_of(block, batch), mine.shape) > 0.5
+                mine = jnp.where(first, mine.astype(f32), moved.astype(f32)).astype(bf16)
+            win[at, slot(s)] = mine
+
+    slots = MEM // local_len
+
+    def chain(k):
+        count = min(2, slots - 1 - 2 * k)
+        top = slots - 2 * k
+        src = win.at[pl.ds(batches, batches), pl.ds((top - count) * local_len, count * local_len)]
+        dst = win.at[pl.ds(0, batches), pl.ds((top - count - 1) * local_len, count * local_len)]
+        return pltpu.make_async_remote_copy(
+            src_ref=src, dst_ref=dst, send_sem=gsend.at[k], recv_sem=grecv.at[k],
+            device_id=nb["up"], device_id_type=MESH)
+
+    rounds = slots // 2
+    has_up, has_down = z < levels - 1, z > 0
+
+    def chain_start(k):
+        pl.when(has_up)(lambda: chain(k).start())
+
+    def chain_round(k):
+        pl.when(has_down)(lambda: chain(k).wait_recv())
+        for s in (slots - 2 - 2 * k, slots - 3 - 2 * k):
+            if s >= 0:
+                place(0, s, True)
+        for s in (slots - 3 - 2 * k, slots - 4 - 2 * k):
+            if s >= 0:
+                place(1, s, True)
+        if k + 1 < rounds:
+            chain_start(k + 1)
+
+    loc_g.wait()
+    rem_g.wait()
+    place(0, slots - 1, False)
+    place(1, slots - 1, False)
+    place(1, slots - 2, True)
+    chain_start(0)
+    ga.turn(0)
+    ga.line(2)
+    ga.turn(1)
+    chain_round(0)
+    ga.line(3) if levels > 3 else None
+    for k in range(4, levels):
+        ga.line(k)
+    loc_o.wait()
+    rem_o.wait()
+    go.begin()
+    for k in range(2, levels):
+        ga.turn(k)
+    chain_round(1)
     for k in range(levels):
-        groups[-1].turn(k)
-    for group in groups:
+        ga.finish(k)
+    out_a = pltpu.make_async_copy(a_all, a_out, osem.at[0])
+    out_a.start()
+    go.line(1)
+
+    w_a = a_all.reshape(4 * levels * 2 * shard, W_A)
+    vec[...] = w_a[:, MISC:W_A].astype(f32).T
+
+    def norm(i, carry):
+        at = pl.ds(pl.multiple_of(i * step, step), step)
+        act[at] = (unit[at] * vec[COL_NORM : COL_NORM + 1] + vec[COL_NORM + 1 : COL_NORM + 2]).astype(bf16)
+        return carry
+
+    lax.fori_loop(0, both // step, norm, 0)
+
+    def project(i, carry):
+        at = pl.ds(pl.multiple_of(i * 256, 256), 256)
+        front[:, at] = dot_f32(act[...], w_a[:, at])
+        return carry
+
+    lax.fori_loop(0, MISC // 256, project, 0)
+    front[:, MISC:W_A] = dot_f32(act[...], w_a[:, MISC:W_A])
+    go.line(2)
+    go.turn(0)
+    meta_at = pl.ds(pl.multiple_of(2 * width + c * 128, 128), 128)
+
+    def gate(i, carry):
+        at = pl.ds(pl.multiple_of(i * local_len, local_len), local_len)
+        gated = jax.nn.sigmoid(front[at, MISC:W_A])
+        gates[at] = gated
+        picks = xs[i // batches, pl.ds(pl.multiple_of((i % batches) * local_len, local_len), local_len), meta_at]
+        gated = gated * picks.astype(f32)
+        for h in range(HALF_HEADS):
+            total = jnp.zeros((local_len, PAD), f32)
+            for e in range(EXPERTS):
+                lane = h * EXPERTS + e
+                col = W_QK + (e * HALF_HEADS + h) * PAD
+                total = total + gated[:, lane : lane + 1] * front[at, col : col + PAD]
+            win[i, pl.ds(MEM, local_len), wide + h * PAD : wide + (h + 1) * PAD] = total.astype(bf16)
+        win[i, pl.ds(MEM, local_len), :wide] = front[at, wide : 2 * wide].astype(bf16)
+        return carry
+
+    lax.fori_loop(0, 2 * batches, gate, 0)
+
+    def hop(k):
+        src = win.at[:, pl.ds(MEM, local_len)] if k == 1 else cr.at[k - 2]
+        return pltpu.make_async_remote_copy(
+            src_ref=src, dst_ref=cr.at[k - 1], send_sem=msend.at[k - 1], recv_sem=mrecv.at[k - 1],
+            device_id=nb["up"], device_id_type=MESH)
+
+    def hop_start(k):
+        pl.when(jnp.logical_and(has_up, z >= k - 1))(lambda: hop(k).start())
+
+    def hop_arrived(k):
+        pl.when(z >= k)(lambda: hop(k).wait_recv())
+
+    hop_start(1)
+    go.line(3) if levels > 3 else None
+    for k in range(4, levels):
+        go.line(k)
+    go.turn(1)
+    chain_round(2)
+    chain_round(3)
+    for k in range(4, rounds):
+        chain_round(k)
+
+    spread = MEM + 2 * local_len
+    table = table_by_offset(w_a, per_device, shard, local_len, spread)
+    for h in range(HALF_HEADS):
+        line = jnp.broadcast_to(table[COL_BIAS + h : COL_BIAS + h + 1], (local_len, spread))
+        turned = pltpu.roll(line, spread - local_len + 1, 1, stride=1, stride_axis=0)
+        bias[h] = turned[:, : MEM + local_len]
+    loc_i.wait()
+    rem_i.wait()
+    gi.begin()
+    for k in range(2, levels):
+        go.turn(k)
+    for k in range(1, reach + 1):
+        hop_arrived(k)
+        if k < reach:
+            hop_start(k + 1)
+    gi.line(1)
+
+    for k in range(rounds):
+        pl.when(has_up)(lambda: chain(k).wait_send())
+    for batch in range(batches):
+        seen = []
+        for back in range(slots + 1):
+            block = jnp.maximum(t - c + 1 - back, 0) + d * 2 * levels
+            tile = w_a[pl.ds(pl.multiple_of(block * shard, 16), 16), MISC:W_A].astype(f32)
+            col = COL_BIAS + HALF_HEADS + batch
+            seen.append(tile[0:1, col : col + 1])
+        for block in range(2):
+            stopped = jnp.zeros((1, 1), f32)
+            for n in range(1, slots + 1):
+                stopped = jnp.maximum(stopped, seen[n - 1 if block else n])
+                if block:
+                    k, which = n // 2, 1 - n % 2
+                else:
+                    k, which = (n + 1) // 2, n % 2
+                if k > reach:
+                    continue
+                at = which * batches + batch
+                source = win[at, pl.ds(MEM, local_len)] if k == 0 else cr[k - 1, at]
+                into = block * batches + batch
+                held = win[into, slot(slots - n)]
+                stop = jnp.broadcast_to(stopped, held.shape) > 0.5
+                win[into, slot(slots - n)] = jnp.where(stop, held.astype(f32), source.astype(f32)).astype(bf16)
+    out_w = pltpu.make_async_copy(win, win_out, osem.at[1])
+    out_w.start()
+
+    key_ids = lax.broadcasted_iota(jnp.int32, (local_len, local_len), 1)
+    row_ids = lax.broadcasted_iota(jnp.int32, (local_len, local_len), 0)
+
+    def attend(i, carry):
+        at = pl.ds(pl.multiple_of(i * local_len, local_len), local_len)
+        block, batch = i // batches, i % batches
+        rows_at = pl.ds(pl.multiple_of(batch * local_len, local_len), local_len)
+        count = xs[block, rows_at, 2 * width : 2 * width + 128][:, 41:42].astype(f32)
+        seen = jnp.logical_and(key_ids <= row_ids, key_ids.astype(f32) < count)
+        picks = xs[block, rows_at, meta_at].astype(f32) * gates[at]
+        for h in range(HALF_HEADS):
+            cols = slice(h * PAD, (h + 1) * PAD)
+            q = front[at, cols].astype(bf16)
+            s = dot_f32(q, win[i, :, cols], NT) * SCALE + bias[h]
+            s = jnp.concatenate([s[:, :MEM], jnp.where(seen, s[:, MEM:], NEG)], axis=1)
+            top = jnp.max(s, axis=-1, keepdims=True)
+            expo = jnp.exp(s - top)
+            p = (expo * (1.0 / jnp.sum(expo, axis=-1, keepdims=True))).astype(bf16)
+            probs[i, h] = p
+            got = dot_f32(p, win[i, :, wide + h * PAD : wide + (h + 1) * PAD]).astype(bf16)
+            att[at, cols] = got
+            got = got.astype(f32)
+            for e in range(EXPERTS):
+                lane = HALF_HEADS * EXPERTS + h * EXPERTS + e
+                col = (e * HALF_HEADS + h) * PAD
+                mixed[at, col : col + PAD] = (picks[:, lane : lane + 1] * got).astype(bf16)
+        return carry
+
+    lax.fori_loop(0, 2 * batches, attend, 0)
+    gi.line(2)
+    gi.turn(0)
+    for k in range(levels):
+        go.finish(k)
+
+    w_o = o_all.reshape(4 * levels * 2 * shard, W_O)
+    far = pl.ds(pl.multiple_of((1 - c) * rows, rows), rows)
+    near = pl.ds(pl.multiple_of(c * rows, rows), rows)
+
+    def out_project(at):
+        def body(i, carry):
+            cols = pl.ds(pl.multiple_of(i * 256, 256), 256)
+            branch[at, cols] = dot_f32(mixed[at], w_o[cols], NT)
+            return carry
+
+        lax.fori_loop(0, width // 256, body, 0)
+
+    def exchange(src, dst, index):
+        return pltpu.make_async_remote_copy(
+            src_ref=src, dst_ref=dst, send_sem=esend.at[index], recv_sem=erecv.at[index],
+            device_id=nb["c"], device_id_type=MESH)
+
+    out_project(far)
+    give = exchange(branch.at[far], arrived, 0)
+    give.start()
+    out_project(near)
+    out_o = pltpu.make_async_copy(o_all, o_out, osem.at[2])
+    out_o.start()
+    give.wait_recv()
+
+    def second(i, carry):
+        at = pl.ds(pl.multiple_of(i * step, step), step)
+        total_at = pl.ds(pl.multiple_of(c * rows + i * step, step), step)
+        values = xs[c, at, :width].astype(f32) + branch[total_at] + arrived[at]
+        hidden[at] = values
+        centered = values - jnp.mean(values, axis=-1, keepdims=True)
+        inverse = lax.rsqrt(jnp.mean(centered * centered, axis=-1, keepdims=True) + EPS)
+        normed = centered * inverse * vec[COL_NORM + 2 : COL_NORM + 3] + vec[COL_NORM + 3 : COL_NORM + 4]
+        n2[total_at] = normed.astype(bf16)
+        return carry
+
+    lax.fori_loop(0, rows // step, second, 0)
+    pair = exchange(n2.at[near], n2.at[near], 1)
+    pair.start()
+    gi.line(3) if levels > 3 else None
+    for k in range(4, levels):
+        gi.line(k)
+    loc_f.wait()
+    gf.begin()
+    for k in range(1, levels):
+        gi.turn(k)
+        gf.line(k)
+    for k in range(levels):
+        gf.turn(k)
+    pair.wait_recv()
+    outs = [
+        pltpu.make_async_copy(src, dst, osem.at[3 + i])
+        for i, (src, dst) in enumerate((
+            (xs, xs_out), (act, act_out), (front, front_out), (gates, gates_out), (probs, probs_out),
+            (att, att_out), (mixed, mixed_out), (hidden, hidden_out), (n2, n2_out)))
+    ]
+    for cp in outs:
+        cp.start()
+    for group in (gi, gf):
         for k in range(levels):
             group.finish(k)
+    for group in (ga, go, gi, gf):
         group.drain()
-    locals_[3].wait()
-    locals_[4].wait()
-    remotes[3].wait()
-    remotes[4].wait()
-
-
-def gather(levels, packs):
+    for cp in (give, pair):
+        cp.wait_send()
+    for k in range(1, reach + 1):
+        pl.when(jnp.logical_and(has_up, z >= k - 1))(lambda: hop(k).wait_send())
+    out_a.wait()
+    out_w.wait()
+    out_o.wait()
+    for cp in outs:
+        cp.wait()
+
+
+def forward(levels, batches, local_len, per_device, packs):
     a, o, i, f, x, g = packs
+    bf16, f32 = jnp.bfloat16, jnp.float32
+    width = f.shape[1]
+    rows = batches * local_len
+    both = 2 * rows
+    wide = HALF_HEADS * PAD
     two = lambda v: (4, levels, 2 * v.shape[1], v.shape[2])
-    shapes = [two(a), two(o), two(i), (4, levels) + f.shape, (2,) + x.shape, (2,) + g.shape[1:]]
+    window = (2 * batches, MEM + local_len, 2 * wide)
+    probs = (2 * batches, HALF_HEADS, local_len, MEM + local_len)
+    outs = [
+        (two(a), bf16), (two(o), bf16), (two(i), bf16), ((4, levels) + f.shape, bf16),
+        ((2,) + x.shape, bf16), ((both, width), bf16), ((both, W_A), f32), ((both, W_MISC), f32),
+        (window, bf16), (probs, bf16), ((both, wide), bf16), ((both, W_O), bf16),
+        ((rows, width), f32), ((both, width), bf16),
+    ]
+    reach = min(MEM // local_len // 2, levels - 1)
+    scratch = [
+        (two(a), bf16), (two(o), bf16), ((2,) + x.shape, bf16), ((2,) + g.shape, bf16), (window, bf16),
+        ((reach, 2 * batches, local_len, 2 * wide), bf16), ((g.shape[2], 2 * wide), bf16),
+        ((both, width), f32), ((both, width), bf16), ((both, W_A), f32), ((both, W_MISC), f32),
+        ((W_MISC, width), f32), ((HALF_HEADS, local_len, MEM + local_len), f32), (probs, bf16),
+        ((both, wide), bf16), ((both, W_O), bf16), ((both, width), f32), ((rows, width), f32),
+        ((rows, width), f32), ((both, width), bf16),
+    ]
+    rounds = MEM // local_len // 2
+    sems = [(4, 6 * levels), (4, 6 * levels), (6,), (6,), (6,), (rounds,), (rounds,), (reach,), (reach,), (2,), (2,), (12,)]
     hbm = pl.BlockSpec(memory_space=pl.ANY)
     return pl.pallas_call(
-        functools.partial(gather_kernel, levels),
-        out_shape=[jax.ShapeDtypeStruct(s, jnp.bfloat16) for s in shapes],
+        functools.partial(forward_kernel, levels, batches, local_len, per_device),
+        out_shape=[jax.ShapeDtypeStruct(s, k) for s, k in outs],
         in_specs=[hbm] * 6,
-        out_specs=[hbm] * 6,
-        scratch_shapes=[
-            pltpu.SemaphoreType.DMA((4, 6 * levels)),
-            pltpu.SemaphoreType.DMA((4, 6 * levels)),
-            pltpu.SemaphoreType.DMA((6,)),
-            pltpu.SemaphoreType.DMA((6,)),
-            pltpu.SemaphoreType.DMA((6,)),
-        ],
+        out_specs=[hbm] * len(outs),
+        scratch_shapes=[pltpu.VMEM(s, k) for s, k in scratch] + [pltpu.SemaphoreType.DMA(s) for s in sems],
         compiler_params=pltpu.CompilerParams(
             collective_id=1, has_side_effects=True, vmem_limit_bytes=VMEM_BYTES),
     )(a, o, i, f, x, g)
@@ -798,33 +1145,6 @@
     return jnp.transpose(a, (1, 2, 0, 3, 4)).reshape(rows, lead * HEADS * HEAD_DIM)
 
 
-def shared_memory(cache, given, starts, levels):
-    count = 2 * levels
-    up = [(i, i + 2) for i in range(count - 2)]
-    local_len = cache.shape[2]
-
-    def follow(before, block):
-        moved = jnp.concatenate([before[0][:, local_len:], before[1]], axis=1)
-        return jnp.where(starts[block][:, None, None], given[block], moved)
-
-    odd = given[1]
-    for _ in range(levels):
-        arrived = lax.ppermute((odd, cache[1]), "tm", up)
-        even = follow(arrived, 0)
-        odd = follow((even, cache[0]), 1)
-    return jnp.stack([even, odd])
-
-
-def bias_of(table, local_len):
-    spread = MEM + 2 * local_len - 1
-    window = MEM + local_len
-    by_distance = jnp.einsum("hc,kc->hk", table, bucket_matrix(local_len), precision=HIGH)
-    heads = table.shape[0]
-    turned = jnp.concatenate([by_distance[:, ::-1], jnp.zeros((heads, 1), jnp.float32)], axis=1)
-    tiled = jnp.tile(turned, (1, local_len))[:, : local_len * spread].reshape(heads, local_len, spread)
-    return tiled[:, :, local_len - 1 : local_len - 1 + window]
-
-
 def bias_grad(score_sum, local_len):
     heads = score_sum.shape[0]
     spread = MEM + 2 * local_len - 1
@@ -860,7 +1180,9 @@
     bias_cols = jnp.pad(
         jnp.transpose(rel_bias.reshape(SIDE, HALF_HEADS, buckets), (0, 2, 1)),
         ((0, 0), (0, shard - buckets), (0, 0)))
-    misc = pad_last(jnp.concatenate([route, norms, bias_cols], axis=2), W_MISC)
+    starts_cols = jnp.broadcast_to(
+        doc_starts.reshape(1, 1, batches).astype(bf16), (SIDE, shard, batches))
+    misc = pad_last(jnp.concatenate([route, norms, bias_cols, starts_cols], axis=2), W_MISC)
     a_pack = jnp.concatenate([a_qk, a_v, misc], axis=2)
     hidden_block = ffn_out.shape[0]
     i_pack = jnp.transpose(
@@ -877,15 +1199,14 @@
     ]
     starts_col = jnp.repeat(doc_starts.reshape(batches), local_len).reshape(rows, 1).astype(bf16)
     counts_col = jnp.repeat(valid_counts.reshape(batches), local_len).reshape(rows, 1).astype(bf16)
-    meta = pad_last(
-        jnp.concatenate(
-            [picks[0][0], picks[1][0], picks[0][1], picks[1][1], starts_col, counts_col], axis=1).astype(bf16),
-        128)
-    x_pack = jnp.concatenate([x_own, grad_own, meta], axis=1)
-    given = given_cache.reshape(batches * MEM, 2 * HEADS * HEAD_DIM)
-    g_pack = split_heads(given, 2)
-
-    a_all, o_all, i_all, f_all, x_all, g_all = gather(levels, (a_pack, a_o, i_pack, ffn_out, x_pack, g_pack))
+    metas = [
+        pad_last(jnp.concatenate([picks[0][s], picks[1][s]], axis=1).astype(bf16), 40) for s in range(SIDE)]
+    metas = [pad_last(jnp.concatenate([m, starts_col, counts_col], axis=1), 128) for m in metas]
+    x_pack = jnp.concatenate([x_own, grad_own] + metas, axis=1)
+    g_pack = given_cache.reshape(batches, MEM, 2 * HEADS * HEAD_DIM)
+
+    (a_all, o_all, i_all, f_all, x_all, act_one, front, gates, window, probs_b, attended, mixed, hidden, act_two
+     ) = forward(levels, batches, local_len, buckets, (a_pack, a_o, i_pack, ffn_out, x_pack, g_pack))
     w_a = a_all.reshape(width, W_A)
     w_o = o_all.reshape(width, W_O)
     w_i = i_all.reshape(width, -1)
@@ -893,52 +1214,21 @@
 
     vectors = w_a[:, MISC + COL_NORM : MISC + COL_NORM + 4].T.astype(f32)
     gain_one, shift_one, gain_two, shift_two = [v.reshape(1, width) for v in vectors]
-    table = w_a[:, MISC + COL_BIAS : MISC + COL_BIAS + HALF_HEADS].reshape(4 * count, shard, HALF_HEADS)
-    table = jnp.transpose(table[:, :buckets].reshape(BUCKETS, HALF_HEADS)).astype(f32)
-
     both = 2 * rows
-    inputs = x_all[:, :, :width].reshape(both, width).astype(f32)
+    wide = HALF_HEADS * PAD
     grad_all = x_all[:, :, width : 2 * width].reshape(both, width)
-    meta_all = x_all[:, :, 2 * width :].reshape(both, 128)
-    pick_mine = jnp.where(side == 0, meta_all[:, :N_ROUTE], meta_all[:, N_ROUTE : 2 * N_ROUTE]).astype(f32)
-    tail = meta_all[:, 2 * N_ROUTE : 2 * N_ROUTE + 2].reshape(2, batches, local_len, 2)[:, :, 0]
-    starts = tail[..., 0] > 0
-    counts = tail[..., 1].astype(jnp.int32)
-
-    normed_one, unit_one, inv_one = norm_forward(inputs, gain_one, shift_one)
-    act_one = normed_one.astype(bf16)
-    front = jnp.dot(act_one, w_a, preferred_element_type=f32)
-    qk = front[:, :W_QK].astype(bf16)
-    parts = front[:, W_QK:MISC].reshape(both, EXPERTS, HALF_HEADS, PAD)
-    gates = jax.nn.sigmoid(front[:, MISC : MISC + N_ROUTE])
+    meta_all = x_all[:, :, 2 * width :].reshape(both, 2, 128)
+    pick_mine = jnp.where(side == 0, meta_all[:, 0, :N_ROUTE], meta_all[:, 1, :N_ROUTE]).astype(f32)
+    gates = gates[:, :N_ROUTE]
     gated = (gates * pick_mine).reshape(both, 2, HALF_HEADS, EXPERTS)
     value_gate = jnp.transpose(gated[:, 0], (0, 2, 1))[..., None]
     output_gate = jnp.transpose(gated[:, 1], (0, 2, 1))[..., None]
-    values = jnp.sum(value_gate * parts, axis=1).reshape(both, HALF_HEADS * PAD).astype(bf16)
-    wide = HALF_HEADS * PAD
-    queries, keys_own = qk[:, :wide], qk[:, wide:]
-    cache = jnp.concatenate([keys_own, values], axis=1).reshape(2, batches, local_len, 2 * wide)
-    memory = shared_memory(cache, g_all.reshape(2, batches, MEM, 2 * wide), starts, levels)
-    window = jnp.concatenate([memory, cache], axis=2).reshape(2 * batches, MEM + local_len, 2, HALF_HEADS, PAD)
+    parts = front[:, W_QK:MISC].reshape(both, EXPERTS, HALF_HEADS, PAD)
+    window = window.reshape(2 * batches, MEM + local_len, 2, HALF_HEADS, PAD)
     keys, vals = window[:, :, 0], window[:, :, 1]
-    queries = queries.reshape(2 * batches, local_len, HALF_HEADS, PAD)
-    raw = jnp.einsum("bqhd,bkhd->bhqk", queries, keys, preferred_element_type=f32) * SCALE
-    row_ids = jnp.arange(local_len, dtype=jnp.int32)[:, None]
-    own_ids = jnp.arange(MEM + local_len, dtype=jnp.int32)[None, :] - MEM
-    valid = jnp.logical_or(
-        own_ids[None, None] < 0,
-        jnp.logical_and((own_ids <= row_ids)[None, None], own_ids[None, None] < counts.reshape(-1)[:, None, None, None]))
-    scores = jnp.where(valid, raw + bias_of(table, local_len)[None], NEG)
-    top = jnp.max(scores, axis=-1, keepdims=True)
-    expo = jnp.exp(scores - top)
-    denom = jnp.sum(expo, axis=-1, keepdims=True)
-    probs = expo / denom
-    probs_b = probs.astype(bf16)
-    attended = jnp.einsum("bhqk,bkhd->bqhd", probs_b, vals, preferred_element_type=f32)
-    attended = attended.reshape(both, wide).astype(bf16)
+    queries = front[:, :wide].astype(bf16).reshape(2 * batches, local_len, HALF_HEADS, PAD)
+    probs = probs_b.astype(f32)
     attended_f = attended.astype(f32).reshape(both, 1, HALF_HEADS, PAD)
-    mixed = (output_gate * attended_f).reshape(both, W_O).astype(bf16)
-    branch = jnp.dot(mixed, w_o.T, preferred_element_type=f32).reshape(2, rows, width)
 
     def mine(a):
         return lax.dynamic_index_in_dim(a, side, 0, keepdims=False)
@@ -950,10 +1240,9 @@
         arrived = swap(own)
         return jnp.where(side == 0, jnp.stack([own, arrived]), jnp.stack([arrived, own])).reshape(both, -1)
 
-    hidden = x_own.astype(f32) + mine(branch) + swap(other(branch))
-
-    normed_two, unit_two, inv_two = norm_forward(hidden, gain_two, shift_two)
-    act_two = paired(normed_two.astype(bf16))
+    unused, unit_one, inv_one = norm_forward(x_own.astype(f32), gain_one, shift_one)
+
+    unused, unit_two, inv_two = norm_forward(hidden, gain_two, shift_two)
     pre_act = jnp.dot(act_two, w_i, preferred_element_type=f32)
     activated = jax.nn.gelu(pre_act, approximate=False).astype(bf16)
     ffn = jnp.dot(activated, w_f, preferred_element_type=f32).reshape(2, rows, width)
@@ -1001,7 +1290,7 @@
     d_one = jnp.einsum("nk,dk->nd", d_front, w_a, preferred_element_type=f32).reshape(2, rows, width)
     d_one = mine(d_one) + swap(other(d_one))
     d_from_one, d_gain_one, d_shift_one = norm_backward(
-        d_one, mine(unit_one.reshape(2, rows, width)), mine(inv_one.reshape(2, rows, 1)), gain_one)
+        d_one, unit_one, inv_one, gain_one)
     input_grad = (d_hidden + d_from_one).reshape(tokens.shape)
     d_norms = jnp.stack([d_gain_one, d_shift_one, d_gain_two, d_shift_two], axis=1)
     d_bias = jnp.pad(

time: 825 us -> 558 us (0.68)
  waiting for transfers between devices: 103 us -> 0.72 us
  local copies, waits for them, and re-layouts: 196 us -> 97.1 us
  other arithmetic: 81.8 us -> 41.4 us
  starting transfers between devices: 21.2 us -> 1.1 us
    ppermute x5 -> x0, waiting for transfers between devices: 97.9 us -> none  [shared_memory(): arrived = lax.ppermute((odd, cache[1]), 'tm', up)]
    another operation x5 -> x2, local copies, waits for them, and re-layouts: 31.8 us -> 0.02 us  [the longest x2 31.8 us: split_heads(): a = pad_last(a.reshape(rows, lead, SIDE, HALF_HEADS, HEAD_DIM), PAD)]
    ppermute x5 -> x0, starting transfers between devices: 19.9 us -> none  [shared_memory(): arrived = lax.ppermute((odd, cache[1]), 'tm', up)]
    transpose x5 -> x3, local copies, waits for them, and re-layouts: 16.2 us -> 0.43 us  [split_heads(): jnp.transpose(a, (2, 0, 1, 3, 4))]
    select_n x8 -> x0, other arithmetic: 13.5 us -> none  [follow(): return jnp.where(starts[block][:, None, None], given[block], moved)]
    squeeze x5 -> x0, local copies, waits for them, and re-layouts: 11.6 us -> none  [the longest x3 10.6 us: follow(): return jnp.where(starts[block][:, None, None], given[block], moved)]
    convert_element_type x6 -> x1, other arithmetic: 11.2 us -> 0.66 us  [on_chip(): doc_starts.reshape(1, 1, batches).astype(bf16)]
    convert_element_type x6 -> x1, local copies, waits for them, and re-layouts: 9.73 us -> 0.01 us  [on_chip(): jnp.repeat(valid_counts.reshape(batches), local_len).reshape(rows, 1)]
  transfers between devices with their start and end apart: 12 -> 5, of which waited for: 8 -> 1; matrix products, arithmetic and copies ran while one was open for 12% -> 14% of each run, Pallas kernels for 0% -> 0%
where the time goes in v2:
time: 558 us; the launch traced here: 547 us
  Pallas kernels  347 us (62%)
  local copies, waits for them, and re-layouts  97.1 us (17%)
  matrix products  57.1 us (10%)
  other arithmetic  41.4 us (7%)
    pallas_call x1, Pallas kernels, scatter(): pl.pallas_call(functools.partial(scatter_kernel, levels), out_shape=[jax....  177 us
    pallas_call x1, Pallas kernels, forward(): pl.pallas_call(functools.partial(forward_kernel, levels, batches, local_l...  170 us
    unnamed x100, local copies, waits for them, and re-layouts  17.3 us
    dot_general x1, matrix products, on_chip(): pre_act = jnp.dot(act_two, w_i, preferred_element_type=f32)  14.5 us
  transfers between devices with their start and end apart: 5, of which 1 were waited for; matrix products, arithmetic and copies ran while one was open for 14% of the time, Pallas kernels for 0%

profile of v2, /device:TPU:0, one launch (start us, length us, event | category | flops | bytes accessed | tf_op | source)
XLA Modules:
  0.0 546.7 jit_solution(13131514320910474451)
XLA Ops:
  13.5 170.1 %shard_map.273 = (bf16[4,4,64,1920]{3,2,1,0:T(8,128)(2,1)}, bf16[4,4,64,1280]{3,2,1,0:T(8,128)(2,1)}, bf16[4,4,64,2048]{3,2,1,0:T(8,128)(2,1)}, bf16[4,4,128,102...) custom-call(bf16[2,32,1920]{2,1,0:T(8,128)(2,1)} %fusion.60.a_in, ...), custom_call_target="tpu_custom_call" | custom-call | tf_op jit(solution)/shard_map/pallas_call | solution.py:947
  184.9 14.5 %fusion.3 = (bf16[512,2048]{1,0:T(8,128)(2,1)}, f32[512,2048]{1,0:T(8,128)S(1)}) fusion(bf16[512,1024]{1,0:T(8,128)(2,1)} %get-tuple-element.32, bf16[1024,2048]{1,0:T(8,128)(2,1)} %bitcast.295), kind=kOutput, calls=%fused_computation.7 | convolution fusion | flops 2215641088 | bytes 11534336 | tf_op jit(solution)/shard_map/dot_general | solution.py:1246
  199.5 4.0 fusion.9
  204.8 2.4 fusion.99
  208.3 5.2 fusion.98
  216.8 6.4 %convolution_convert_fusion.2 = bf16[1024,2048]{1,0:T(8,128)(2,1)} fusion(bf16[512,1024]{1,0:T(8,128)(2,1)} %get-tuple-element.32, bf16[512,2048]{1,0:T(8,128)(2,1)} %copy-done.41), kind=kOutput, calls=%fused_computation.33 | convolution fusion | flops 2149580800 | bytes 7340032 | tf_op jit(solution)/shard_map/nd,nf->df/dot_general | solution.py:1253
  225.6 7.7 %reshape.413 = bf16[4,1152,2,2,128]{4,3,2,1,0:T(2,128)(2,1)} reshape(bf16[4,1152,512]{2,1,0:T(8,128)(2,1)} %get-tuple-element.37) | data formatting | bytes 9437184 | tf_op jit(solution)/shard_map/reshape | solution.py:1227
  233.4 7.1 %fusion.91 = (bf16[4,1152,1,2,128]{4,3,2,1,0:T(2,128)(2,1)}, bf16[4,1152,1,2,128]{4,3,2,1,0:T(2,128)(2,1)}) fusion(bf16[4,1152,2,2,128]{4,3,2,1,0:T(2,128)(2,1)} %reshape.413), kind=kLoop, calls=%fused_computation.197 | loop fusion | bytes 9437184 | tf_op jit(solution)/shard_map/slice | solution.py:1228
  241.4 2.7 multiply_reduce_fusion.3
  244.1 3.4 fusion.89
  248.3 2.7 copy.282
  251.0 2.0 reshape.450
  253.0 2.8 copy.289
  255.9 2.6 reshape.420
  259.3 6.8 %copy.319 = bf16[4,1152,1,2,128]{1,4,3,0,2:T(8,128)(2,1)} copy(bf16[4,1152,1,2,128]{4,3,2,1,0:T(2,128)(2,1)} %get-tuple-element.145) | data formatting | bytes 4718592
  266.1 6.1 %convolution_convert_fusion.1 = bf16[2048,1024]{1,0:T(8,128)(2,1)} fusion(bf16[512,2048]{1,0:T(8,128)(2,1)} %get-tuple-element.172, bf16[512,1024]{1,0:T(8,128)(2,1)S(1)} %bitcast.260), kind=kOutput, calls=%fused_computation.32 | convolution fusion | flops 2149580800 | bytes 7340032 | tf_op jit(solution)/shard_map/nf,nd->fd/dot_general | solution.py:1250
  277.5 2.5 reshape.447
  280.0 9.6 %multiply_reduce_fusion.2 = (bf16[512,2,128]{2,1,0:T(2,128)(2,1)}, f32[512,5,2]{2,1,0:T(8,128)}) fusion(f32[512,5,2,128]{3,2,1,0:T(2,128)} %reshape.447, f32[512,5,2]{2,1,0:T(8,128)} %copy.282, f32[512,2,128]{2,1,0:T(2,128)} %reshape.450), kind=kLoop, calls=%fused_computation.44 | loop fusion | flops 2485248 | bytes 3448832 | tf_op jit(solution)/shard_map/reduce_sum | solution.py:1265
  289.5 2.2 copy.295
  294.3 9.3 %multiply_convert_fusion = (bf16[512,5,2,128]{3,2,1,0:T(2,128)(2,1)}, f32[512,5,2]{2,1,0:T(8,128)}) fusion(f32[512,2,128]{2,1,0:T(2,128)S(1)} %copy.293, f32[512,5,2]{2,1,0:T(8,128)} %copy.289, f32[512,5,2,128]{3,2,1,0:T(2,128)S(1)} %copy-done.3), kind=kLoop, calls=%fused_computation.43 | loop fusion | flops 2616320 | bytes 4497408 | tf_op jit(solution)/shard_map/convert_element_type | solution.py:1276
  303.6 2.8 copy.294
  310.9 4.4 convert_element_type.242
  315.3 2.6 fusion
  321.7 3.5 fusion.40
  325.7 1.9 copy-done.32
  327.7 2.4 fusion.100
  332.2 3.0 reshape.424
  339.5 3.8 convolution_convert_fusion
  343.5 3.0 convolution_convert_fusion.3
  346.7 1.9 multiply_reduce_fusion.4
  349.0 7.7 %concatenate.47 = bf16[1024,1920]{1,0:T(8,128)(2,1)} concatenate(bf16[1024,1812]{1,0:T(8,128)(2,1)} %bitcast.244, bf16[1024,1]{1,0:T(8,128)(2,1)S(1)} %stack.73, bf16[1024,1]{1,0:T(8,128)(2,1)S(1)} %stack.74, bf16[1024,1]{1,0:T(8,128)(2,1)S(1)} %stack.75, bf16[1024,1]{1,0:T(8,128)(2,1)S(1)} %copy-done.18, bf16[1024,2]{1,0:T(8,128)(2,1)S(1)} %bitcast.256, ...), dimensions={1} | concatenate | bytes 7864320 | tf_op jit(solution)/shard_map/concatenate | solution.py:1300
  356.6 177.3 %shard_map.274 = (f32[64,1920]{1,0:T(8,128)}, f32[64,1280]{1,0:T(8,128)}, f32[64,2048]{1,0:T(8,128)}, f32[128,1024]{1,0:T(8,128)}) custom-call(bf16[4,4,64,1920]{3,2,1,0:T(8,128)(2,1)} %bitcast.238, bf16[4,4,64,1280]{3,2,1,0:T(8,128)(2,1)} %bitcast.250, bf16[4,4,64,2048]{3,2,1,0:T(8,128)(2,1)} %bitcast.245, bf16[4,4,128,1024]{3,2,1,0:T(8,128)(2,1)} %bitcast.246), custom_call_target="tpu_custom_call" | custom-call | tf_op jit(solution)/shard_map/pallas_call | solution.py:1125
  (235 shorter events, 60.4 us)
Async XLA Ops:
  0.6 10.0 %copy-start.40 = (s32[2,1,1]{0,2,1:T(1,128)S(1)}, s32[2,1,1]{0,2,1:T(1,128)}, u32[]{:S(2)}) copy-start(s32[2,1,1]{0,2,1:T(1,128)} %param.23) | copy-start | bytes 28
  0.7 10.1 %copy-start.34 = (s32[2,1,128,4,2]{2,4,3,1,0:T(2,128)S(1)}, s32[2,1,128,4,2]{2,4,3,1,0:T(2,128)}, u32[]{:S(2)}) copy-start(s32[2,1,128,4,2]{2,4,3,1,0:T(2,128)} %param.22) | copy-start | bytes 24580
  0.7 10.2 %copy-start.35 = (s32[2,1,128,4,2]{2,4,3,1,0:T(2,128)S(1)}, s32[2,1,128,4,2]{2,4,3,1,0:T(2,128)}, u32[]{:S(2)}) copy-start(s32[2,1,128,4,2]{2,4,3,1,0:T(2,128)} %param.21) | copy-start | bytes 24580
  0.7 10.8 %copy-start.13 = (bf16[2,1,128,1024]{3,2,1,0:T(8,128)(2,1)S(1)}, bf16[2,1,128,1024]{3,2,1,0:T(8,128)(2,1)}, u32[]{:S(2)}) copy-start(bf16[2,1,128,1024]{3,2,1,0:T(8,128)(2,1)} %param.19) | copy-start | bytes 1572868
  0.7 11.7 %copy-start.2 = (bf16[2,1,128,1024]{3,2,1,0:T(8,128)(2,1)S(1)}, bf16[2,1,128,1024]{3,2,1,0:T(8,128)(2,1)}, u32[]{:S(2)}) copy-start(bf16[2,1,128,1024]{3,2,1,0:T(8,128)(2,1)} %param.18) | copy-start | bytes 1572868
  184.9 14.6 %copy-start.20 = (bf16[2,256,1024]{2,1,0:T(8,128)(2,1)}, bf16[2,256,1024]{2,1,0:T(8,128)(2,1)S(1)}, u32[]{:S(2)}) copy-start(bf16[2,256,1024]{2,1,0:T(8,128)(2,1)S(1)} %slice.122) | copy-start | bytes 3145732
  184.9 14.6 %copy-start.36 = (bf16[4,4,128,1024]{3,2,1,0:T(8,128)(2,1)S(1)}, bf16[4,4,128,1024]{3,2,1,0:T(8,128)(2,1)}, u32[]{:S(2)}) copy-start(bf16[4,4,128,1024]{3,2,1,0:T(8,128)(2,1)} %get-tuple-element.34) | copy-start | bytes 12582916
  199.5 5.3 copy-start.37
  207.1 6.3 %copy-start.10 = (f32[2,256,1024]{2,1,0:T(8,128)}, f32[2,256,1024]{2,1,0:T(8,128)S(1)}, u32[]{:S(2)}) copy-start(f32[2,256,1024]{2,1,0:T(8,128)S(1)} %fusion.99) | copy-start | bytes 6291460
  208.3 33.1 %collective-permute-start.1 = (f32[256,1024]{1,0:T(8,128)}, f32[256,1024]{1,0:T(8,128)}, u32[]{:S(2)}, u32[]{:S(2)}) collective-permute-start(f32[256,1024]{1,0:T(8,128)} %dynamic-slice_bitcast_fusion.1), channel_id=1, source_target_pairs={{0,1},{1,0},{2,3},{3,2},{4,5},{5,4},{6,7},{7,6},{8,9},{9,8},{10,11... | collective-permute-start | bytes 3145736 | tf_op jit(solution)/shard_map/ppermute | solution.py:386
  215.1 28.9 %collective-permute-start = (f32[256,1024]{1,0:T(8,128)}, f32[256,1024]{1,0:T(8,128)}, u32[]{:S(2)}, u32[]{:S(2)}) collective-permute-start(f32[256,1024]{1,0:T(8,128)} %dynamic-slice_bitcast_fusion.2), channel_id=1, source_target_pairs={{0,1},{1,0},{2,3},{3,2},{4,5},{5,4},{6,7},{7,6},{8,9},{9,8},{10,11... | collective-permute-start | bytes 3145736 | tf_op jit(solution)/shard_map/ppermute | solution.py:386
  216.8 6.4 %copy-start = (f32[256,1024]{1,0:T(8,128)S(1)}, f32[256,1024]{1,0:T(8,128)}, u32[]{:S(2)}) copy-start(f32[256,1024]{1,0:T(8,128)} %get-tuple-element.31) | copy-start | bytes 3145732
  225.6 7.7 %copy-start.22 = (f32[512,128]{1,0:T(8,128)S(1)}, f32[512,128]{1,0:T(8,128)}, u32[]{:S(2)}) copy-start(f32[512,128]{1,0:T(8,128)} %get-tuple-element.40) | copy-start | bytes 786436
  244.1 4.0 copy-start.9
  247.5 25.7 %collective-permute-start.2 = (bf16[256,1024]{1,0:T(8,128)(2,1)}, bf16[256,1024]{1,0:T(8,128)(2,1)}, u32[]{:S(2)}, u32[]{:S(2)}) collective-permute-start(bf16[256,1024]{1,0:T(8,128)(2,1)} %get-tuple-element.140), channel_id=1, source_target_pairs={{0,1},{1,0},{2,3},{3,2},{4,5},{5,4},{6,7},{7,6},{8,9},{9,8},{10,11... | collective-permute-start | bytes 1572872 | tf_op jit(solution)/shard_map/ppermute | solution.py:386
  258.5 7.6 %copy-start.21 = (bf16[2,256,1024]{2,1,0:T(8,128)(2,1)S(1)}, bf16[2,256,1024]{2,1,0:T(8,128)(2,1)}, u32[]{:S(2)}) copy-start(bf16[2,256,1024]{2,1,0:T(8,128)(2,1)} %copy-done.20) | copy-start | bytes 3145732
  266.0 6.1 %copy-start.33 = (bf16[1024]{0:T(1024)(128)(2,1)S(1)}, bf16[1024]{0:T(1024)(128)(2,1)}, u32[]{:S(2)}) copy-start(bf16[1024]{0:T(1024)(128)(2,1)} %get-tuple-element.129) | copy-start | bytes 6148
  266.0 9.9 %copy-start.38 = (bf16[4,4,64,1280]{3,2,1,0:T(8,128)(2,1)S(1)}, bf16[4,4,64,1280]{3,2,1,0:T(8,128)(2,1)}, u32[]{:S(2)}) copy-start(bf16[4,4,64,1280]{3,2,1,0:T(8,128)(2,1)} %get-tuple-element.39) | copy-start | bytes 7864324
  280.0 13.6 %copy-start.1 = (bf16[4,2,128,1152]{3,2,1,0:T(8,128)(2,1)S(1)}, bf16[4,2,128,1152]{3,2,1,0:T(8,128)(2,1)}, u32[]{:S(2)}) copy-start(bf16[4,2,128,1152]{3,2,1,0:T(8,128)(2,1)} %get-tuple-element.38) | copy-start | bytes 7077892
  321.2 4.3 copy-start.19
  321.2 4.3 copy-start.23
  321.5 4.1 copy-start.5
  321.7 4.0 copy-start.24
  325.5 4.6 copy-start.26
  325.6 4.5 copy-start.29
  327.7 4.1 copy-start.6
  331.3 15.3 %collective-permute-start.3 = (f32[256,1024]{1,0:T(8,128)}, f32[256,1024]{1,0:T(8,128)}, u32[]{:S(2)}, u32[]{:S(2)}) collective-permute-start(f32[256,1024]{1,0:T(8,128)} %dynamic-slice_bitcast_fusion), channel_id=1, source_target_pairs={{0,1},{1,0},{2,3},{3,2},{4,5},{5,4},{6,7},{7,6},{8,9},{9,8},{10,11... | collective-permute-start | bytes 3145736 | tf_op jit(solution)/shard_map/ppermute | solution.py:386
  332.2 7.3 %copy-start.30 = (bf16[512,20]{1,0:T(8,128)(2,1)S(1)}, bf16[512,20]{1,0:T(8,128)(2,1)}, u32[]{:S(2)}) copy-start(bf16[512,20]{1,0:T(8,128)(2,1)} %copy-done.29) | copy-start | bytes 61444
  335.2 4.3 copy-start.25
  335.2 4.3 copy-start.27
  535.5 2.2 collective-permute-start.4
  540.7 4.9 copy-start.28
  (15 other events, 36.4 us)

commit v3 on v2

--- a/solution.py
+++ b/solution.py
@@ -381,11 +381,6 @@
     return jnp.pad(a, [(0, 0)] * (a.ndim - 1) + [(0, width - a.shape[-1])])
 
 
-def swap(a):
-    count = lax.axis_size("tm")
-    return lax.ppermute(a, "tm", [(i, i ^ 1) for i in range(count)])
-
-
 def neighbours(count):
     d, t = lax.axis_index("doc"), lax.axis_index("tm")
     z, c = t // 2, t % 2
@@ -565,11 +560,11 @@
 def forward_kernel(
     levels, batches, local_len, per_device,
     a_in, o_in, i_in, f_in, x_in, g_in,
-    a_out, o_out, i_all, f_all, xs_out, act_out, front_out, gates_out, win_out, probs_out, att_out,
-    mixed_out, hidden_out, n2_out,
-    a_all, o_all, xs, graw, win, cr, sel, unit, act, front, gates, vec, bias, probs, att, mixed,
-    branch, arrived, hidden, n2,
-    send, recv, csend, crecv, lsem, gsend, grecv, msend, mrecv, esend, erecv, osem,
+    a_out, o_out, i_out, f_all, xs_out, act_out, front_out, gates_out, win_out, probs_out, att_out,
+    mixed_out, hidden_out, n2_out, vec_out, ffn_out, slope_out,
+    a_all, o_all, i_all, xs, graw, win, cr, sel, unit, act, front, gates, vec, bias, probs, att, mixed,
+    arrived, hidden, n2, ffn, slope,
+    send, recv, csend, crecv, lsem, gsend, grecv, msend, mrecv, esend, erecv, osem, psem,
 ):
     bf16, f32 = jnp.bfloat16, jnp.float32
     d, t = lax.axis_index("doc"), lax.axis_index("tm")
@@ -811,6 +806,9 @@
     key_ids = lax.broadcasted_iota(jnp.int32, (local_len, local_len), 1)
     row_ids = lax.broadcasted_iota(jnp.int32, (local_len, local_len), 0)
 
+    def probs_copy(i, slot_of):
+        return pltpu.make_async_copy(probs.at[slot_of], probs_out.at[i], psem.at[slot_of])
+
     def attend(i, carry):
         at = pl.ds(pl.multiple_of(i * local_len, local_len), local_len)
         block, batch = i // batches, i % batches
@@ -818,6 +816,8 @@
         count = xs[block, rows_at, 2 * width : 2 * width + 128][:, 41:42].astype(f32)
         seen = jnp.logical_and(key_ids <= row_ids, key_ids.astype(f32) < count)
         picks = xs[block, rows_at, meta_at].astype(f32) * gates[at]
+        slot_of = lax.rem(i, 2)
+        pl.when(i >= 2)(lambda: probs_copy(i - 2, slot_of).wait())
         for h in range(HALF_HEADS):
             cols = slice(h * PAD, (h + 1) * PAD)
             q = front[at, cols].astype(bf16)
@@ -825,8 +825,9 @@
             s = jnp.concatenate([s[:, :MEM], jnp.where(seen, s[:, MEM:], NEG)], axis=1)
             top = jnp.max(s, axis=-1, keepdims=True)
             expo = jnp.exp(s - top)
-            p = (expo * (1.0 / jnp.sum(expo, axis=-1, keepdims=True))).astype(bf16)
-            probs[i, h] = p
+            p = expo * (1.0 / jnp.sum(expo, axis=-1, keepdims=True))
+            probs[slot_of, h] = p
+            p = p.astype(bf16)
             got = dot_f32(p, win[i, :, wide + h * PAD : wide + (h + 1) * PAD]).astype(bf16)
             att[at, cols] = got
             got = got.astype(f32)
@@ -834,15 +835,19 @@
                 lane = HALF_HEADS * EXPERTS + h * EXPERTS + e
                 col = (e * HALF_HEADS + h) * PAD
                 mixed[at, col : col + PAD] = (picks[:, lane : lane + 1] * got).astype(bf16)
+        probs_copy(i, slot_of).start()
         return carry
 
     lax.fori_loop(0, 2 * batches, attend, 0)
+    for i in range(2 * batches - 2, 2 * batches):
+        probs_copy(i, i % 2).wait()
     gi.line(2)
     gi.turn(0)
     for k in range(levels):
         go.finish(k)
 
     w_o = o_all.reshape(4 * levels * 2 * shard, W_O)
+    branch = unit
     far = pl.ds(pl.multiple_of((1 - c) * rows, rows), rows)
     near = pl.ds(pl.multiple_of(c * rows, rows), rows)
 
@@ -889,20 +894,42 @@
     for k in range(1, levels):
         gi.turn(k)
         gf.line(k)
-    for k in range(levels):
-        gf.turn(k)
+    gf.turn(0)
     pair.wait_recv()
     outs = [
         pltpu.make_async_copy(src, dst, osem.at[3 + i])
         for i, (src, dst) in enumerate((
-            (xs, xs_out), (act, act_out), (front, front_out), (gates, gates_out), (probs, probs_out),
-            (att, att_out), (mixed, mixed_out), (hidden, hidden_out), (n2, n2_out)))
+            (xs, xs_out), (act, act_out), (front, front_out), (gates, gates_out),
+            (att, att_out), (mixed, mixed_out), (hidden, hidden_out), (n2, n2_out), (vec, vec_out)))
     ]
     for cp in outs:
         cp.start()
-    for group in (gi, gf):
-        for k in range(levels):
-            group.finish(k)
+    for k in range(levels):
+        gi.finish(k)
+    out_i = pltpu.make_async_copy(i_all, i_out, osem.at[13])
+    out_i.start()
+
+    w_i = i_all.reshape(4 * levels * 2 * shard, i_all.shape[3])
+
+    def activate(i, carry):
+        at = pl.ds(pl.multiple_of(i * 256, 256), 256)
+        pre = dot_f32(n2[...], w_i[:, at])
+        below = 0.5 * (1.0 + lax.erf(pre * 0.7071067811865476))
+        ffn[:, at] = (pre * below).astype(bf16)
+        slope[:, at] = (below + pre * jnp.exp(-0.5 * pre * pre) * 0.3989422804014327).astype(bf16)
+        return carry
+
+    steps = ffn.shape[1] // 256
+    lax.fori_loop(0, steps // 2, activate, 0)
+    gf.turn(1)
+    lax.fori_loop(steps // 2, steps, activate, 0)
+    outs += [pltpu.make_async_copy(ffn, ffn_out, osem.at[14]), pltpu.make_async_copy(slope, slope_out, osem.at[15])]
+    outs[-2].start()
+    outs[-1].start()
+    for k in range(2, levels):
+        gf.turn(k)
+    for k in range(levels):
+        gf.finish(k)
     for group in (ga, go, gi, gf):
         group.drain()
     for cp in (give, pair):
@@ -912,6 +939,7 @@
     out_a.wait()
     out_w.wait()
     out_o.wait()
+    out_i.wait()
     for cp in outs:
         cp.wait()
 
@@ -929,20 +957,21 @@
     outs = [
         (two(a), bf16), (two(o), bf16), (two(i), bf16), ((4, levels) + f.shape, bf16),
         ((2,) + x.shape, bf16), ((both, width), bf16), ((both, W_A), f32), ((both, W_MISC), f32),
-        (window, bf16), (probs, bf16), ((both, wide), bf16), ((both, W_O), bf16),
-        ((rows, width), f32), ((both, width), bf16),
+        (window, bf16), (probs, f32), ((both, wide), bf16), ((both, W_O), bf16),
+        ((rows, width), f32), ((both, width), bf16), ((W_MISC, width), f32), ((both, i.shape[2]), bf16),
+        ((both, i.shape[2]), bf16),
     ]
     reach = min(MEM // local_len // 2, levels - 1)
     scratch = [
-        (two(a), bf16), (two(o), bf16), ((2,) + x.shape, bf16), ((2,) + g.shape, bf16), (window, bf16),
-        ((reach, 2 * batches, local_len, 2 * wide), bf16), ((g.shape[2], 2 * wide), bf16),
+        (two(a), bf16), (two(o), bf16), (two(i), bf16), ((2,) + x.shape, bf16), ((2,) + g.shape, bf16),
+        (window, bf16), ((reach, 2 * batches, local_len, 2 * wide), bf16), ((g.shape[2], 2 * wide), bf16),
         ((both, width), f32), ((both, width), bf16), ((both, W_A), f32), ((both, W_MISC), f32),
-        ((W_MISC, width), f32), ((HALF_HEADS, local_len, MEM + local_len), f32), (probs, bf16),
-        ((both, wide), bf16), ((both, W_O), bf16), ((both, width), f32), ((rows, width), f32),
-        ((rows, width), f32), ((both, width), bf16),
+        ((W_MISC, width), f32), ((HALF_HEADS, local_len, MEM + local_len), f32), ((2,) + probs[1:], f32),
+        ((both, wide), bf16), ((both, W_O), bf16), ((rows, width), f32),
+        ((rows, width), f32), ((both, width), bf16), ((both, i.shape[2]), bf16), ((both, i.shape[2]), bf16),
     ]
     rounds = MEM // local_len // 2
-    sems = [(4, 6 * levels), (4, 6 * levels), (6,), (6,), (6,), (rounds,), (rounds,), (reach,), (reach,), (2,), (2,), (12,)]
+    sems = [(4, 6 * levels), (4, 6 * levels), (6,), (6,), (6,), (rounds,), (rounds,), (reach,), (reach,), (2,), (2,), (16,), (2,)]
     hbm = pl.BlockSpec(memory_space=pl.ANY)
     return pl.pallas_call(
         functools.partial(forward_kernel, levels, batches, local_len, per_device),
@@ -978,6 +1007,10 @@
         self.half = src.shape[2] // 2
         self.by_x, self.by_y = d + 1 - 2 * (d % 2), (d + 2) % 4
         self.low, self.high = pl.ds(0, self.half), pl.ds(self.half, self.half)
+        self.columns = (3 - d, self.by_x, self.by_y, d)
+        self.order = []
+        for k in range((levels + 1) // 2):
+            self.order += [levels - 1 - k, k] if levels - 1 - k != k else [k]
 
     def copy(self, src, dst, slot, to):
         return pltpu.make_async_remote_copy(
@@ -1005,13 +1038,15 @@
         buf = self.up if to == "up" else self.down
         return self.copy(buf.at[j], buf.at[j], (6 if to == "up" else 7) * self.levels + j, to)
 
-    def begin(self):
-        for j in range(self.levels):
-            self.corner(j, "x").start()
-            self.corner(j, "y").start()
-        for j in range(self.levels):
-            self.direct(j, "x").start()
-            self.direct(j, "y").start()
+    def begin(self, place):
+        for j in self.order:
+            if place == 0:
+                self.corner(j, "x").start()
+                self.corner(j, "y").start()
+            elif place == 1:
+                self.direct(j, "x").start()
+            elif place == 2:
+                self.direct(j, "y").start()
 
     def turn(self, j):
         self.corner(j, "x").wait_recv()
@@ -1086,51 +1121,510 @@
             pl.when(self.z > j)(lambda: self.along(j, "down").wait_send())
 
 
-def scatter_kernel(levels, *refs):
+def scatter_scratch(levels, shapes):
+    out = []
+    for rows, width in shapes:
+        out.append(((4, levels, rows, width), jnp.bfloat16))
+        for r in (rows // 2, rows // 2, rows, rows, rows, rows):
+            out.append(((levels, r, width), jnp.bfloat16))
+    return out
+
+
+def norm_rows(values):
+    centered = values - jnp.mean(values, axis=-1, keepdims=True)
+    inverse = lax.rsqrt(jnp.mean(centered * centered, axis=-1, keepdims=True) + EPS)
+    return centered * inverse, inverse
+
+
+def norm_rows_backward(upstream, normed, inverse, gain):
+    scaled = upstream * gain
+    inside = (
+        scaled
+        - jnp.mean(scaled, axis=-1, keepdims=True)
+        - normed * jnp.mean(scaled * normed, axis=-1, keepdims=True)
+    )
+    return inside * inverse
+
+
+def middle_kernel(
+    levels, batches, local_len, per_device, shard,
+    wf_in, wi_in, wo_in, act_in, slope_in, xs_in, n2_in, hidden_in, vec_in, att_in, gates_in, front_in,
+    win_in, probs_in,
+    f_out, i_out, layer_out, dfront_out, db_out, dhid_out, dnorm_out, mbias_out,
+    w_f, w_i, w_o, act, slope, grad, meta, n2, hidden, vec, att, gates, front, win, probs,
+    branch, arrived, dhid, db, dmix, dfront, dsum, datt, dnorm, result, mbias, f_total, i_total,
+    *rest,
+):
+    bf16, f32 = jnp.bfloat16, jnp.float32
+    f_bufs, i_bufs = rest[:7], rest[7:14]
+    send, recv, lsem, tsem, esend, erecv, osem = rest[14:]
     d, t = lax.axis_index("doc"), lax.axis_index("tm")
-    z = t // 2
+    z, c = t // 2, t % 2
     nb = neighbours(2 * levels)
-    count = 4
-    srcs, dsts = refs[:count], refs[count : 2 * count]
-    bufs = refs[2 * count : -2]
-    send, recv = refs[-2:]
+    width = w_f.shape[1]
+    rows = batches * local_len
+    both = 2 * rows
+    wide = HALF_HEADS * PAD
+    ff = act.shape[1]
+    far = pl.ds(pl.multiple_of((1 - c) * rows, rows), rows)
+    near = pl.ds(pl.multiple_of(c * rows, rows), rows)
+
+    def load(src, dst, index):
+        cp = pltpu.make_async_copy(src, dst, lsem.at[index])
+        cp.start()
+        return cp
+
+    meta_at = pl.ds(pl.multiple_of(2 * width + c * 128, 128), 128)
+    l_act = load(act_in, act, 0)
+    l_grad = load(xs_in.at[:, :, pl.ds(width, width)], grad, 1)
+    l_wf = load(wf_in, w_f, 2)
+    l_slope = load(slope_in, slope, 3)
+    l_n2 = load(n2_in, n2, 4)
+    l_wi = load(wi_in, w_i, 5)
+    l_hid = load(hidden_in, hidden, 6)
+    l_vec = load(vec_in, vec, 7)
+    l_meta = load(xs_in.at[:, :, meta_at], meta, 8)
+    l_att = load(att_in, att, 9)
+    l_gates = load(gates_in, gates, 10)
+    l_wo = load(wo_in, w_o, 11)
+
+    def tiles(i, slot):
+        at = pl.ds(pl.multiple_of(i * local_len, local_len), local_len)
+        return [
+            pltpu.make_async_copy(win_in.at[i], win.at[slot], tsem.at[0, slot]),
+            pltpu.make_async_copy(probs_in.at[i], probs.at[slot], tsem.at[1, slot]),
+            pltpu.make_async_copy(front_in.at[at], front.at[slot], tsem.at[2, slot]),
+        ]
+
+    for cp in tiles(0, 0):
+        cp.start()
     enter(nb, z, levels)
-    groups = [
-        Scatter(srcs[i], bufs[6 * i : 6 * i + 6], (send.at[i], recv.at[i]), nb, d, z, levels)
-        for i in range(count)
+    sf = Scatter(f_bufs[0], f_bufs[1:], (send.at[0], recv.at[0]), nb, d, z, levels)
+    si = Scatter(i_bufs[0], i_bufs[1:], (send.at[1], recv.at[1]), nb, d, z, levels)
+
+    l_act.wait()
+    l_grad.wait()
+    g_all = grad.reshape(both, width)
+    f_rows = f_bufs[0].shape[2]
+    span = levels * f_rows
+    for place, column in enumerate(sf.columns):
+        at = pl.ds(pl.multiple_of(column * span, span), span)
+        got = dot_f32(act[:, at], g_all[...], TN).astype(bf16)
+        f_bufs[0][column] = got.reshape(levels, f_rows, width)
+        sf.begin(place)
+
+    l_wf.wait()
+    l_slope.wait()
+
+    def back(i, carry):
+        at = pl.ds(pl.multiple_of(i * 256, 256), 256)
+        slope[:, at] = (dot_f32(g_all[...], w_f[at], NT) * slope[:, at].astype(f32)).astype(bf16)
+        return carry
+
+    lax.fori_loop(0, ff // 256, back, 0)
+    l_n2.wait()
+    i_rows = i_bufs[0].shape[2]
+    span = levels * i_rows
+    for place, column in enumerate(si.columns):
+        at = pl.ds(pl.multiple_of(column * span, span), span)
+
+        def weights(i, carry):
+            cols = pl.ds(pl.multiple_of(i * 512, 512), 512)
+            got = dot_f32(n2[:, at], slope[:, cols], TN).astype(bf16)
+            i_bufs[0][column, :, :, cols] = got.reshape(levels, i_rows, 512)
+            return carry
+
+        lax.fori_loop(0, ff // 512, weights, 0)
+        si.begin(place)
+
+    def exchange(src, dst, index):
+        return pltpu.make_async_remote_copy(
+            src_ref=src, dst_ref=dst, send_sem=esend.at[index], recv_sem=erecv.at[index],
+            device_id=nb["c"], device_id_type=MESH)
+
+    l_wi.wait()
+
+    def input_side(at):
+        def body(i, carry):
+            cols = pl.ds(pl.multiple_of(i * 256, 256), 256)
+            branch[at, cols] = dot_f32(slope[at], w_i[cols], NT)
+            return carry
+
+        lax.fori_loop(0, width // 256, body, 0)
+
+    input_side(far)
+    give = exchange(branch.at[far], arrived, 0)
+    give.start()
+    input_side(near)
+    for j in sf.order:
+        sf.turn(j)
+    l_hid.wait()
+    l_vec.wait()
+    give.wait()
+    dnorm[...] = jnp.zeros_like(dnorm)
+    step = 64
+
+    def second(i, carry):
+        at = pl.ds(pl.multiple_of(i * step, step), step)
+        total_at = pl.ds(pl.multiple_of(c * rows + i * step, step), step)
+        normed, inverse = norm_rows(hidden[at])
+        up = branch[total_at] + arrived[at]
+        dnorm[0:1] += jnp.sum(up * normed, axis=0, keepdims=True)
+        dnorm[1:2] += jnp.sum(up, axis=0, keepdims=True)
+        got = norm_rows_backward(up, normed, inverse, vec[COL_NORM + 2 : COL_NORM + 3])
+        got = got + grad[c, at].astype(f32)
+        dhid[at] = got
+        db[total_at] = got.astype(bf16)
+        return carry
+
+    lax.fori_loop(0, rows // step, second, 0)
+    pair = exchange(db.at[near], db.at[near], 1)
+    pair.start()
+
+    def output_side(at):
+        def body(i, carry):
+            cols = pl.ds(pl.multiple_of(i * 256, 256), 256)
+            branch[at, cols] = dot_f32(act[at], w_f[:, cols])
+            return carry
+
+        lax.fori_loop(0, width // 256, body, 0)
+
+    output_side(far)
+    pair.wait()
+    last = exchange(branch.at[far], arrived, 2)
+    last.start()
+    l_wo.wait()
+
+    def mix(i, carry):
+        cols = pl.ds(pl.multiple_of(i * wide, wide), wide)
+        dmix[:, cols] = dot_f32(db[...], w_o[:, cols]).astype(bf16)
+        return carry
+
+    lax.fori_loop(0, EXPERTS, mix, 0)
+    l_meta.wait()
+    l_att.wait()
+    l_gates.wait()
+    dsum[...] = jnp.zeros_like(dsum)
+    lanes = lax.broadcasted_iota(jnp.int32, (local_len, W_MISC), 1)
+
+    def attend(i, carry):
+        slot = lax.rem(i, 2)
+
+        @pl.when(i + 1 < 2 * batches)
+        def _():
+            for cp in tiles(i + 1, 1 - slot):
+                cp.start()
+
+        for cp in tiles(i, slot):
+            cp.wait()
+        at = pl.ds(pl.multiple_of(i * local_len, local_len), local_len)
+        block, batch = i // batches, i % batches
+        rows_at = pl.ds(pl.multiple_of(batch * local_len, local_len), local_len)
+        gate = gates[at]
+        picks = meta[block, rows_at].astype(f32)
+        gated = gate * picks
+        d_gates = jnp.zeros((local_len, W_MISC), f32)
+        for h in range(HALF_HEADS):
+            cols = slice(h * PAD, (h + 1) * PAD)
+            v_cols = slice(wide + h * PAD, wide + (h + 1) * PAD)
+            got = att[at, cols].astype(f32)
+            d_att = jnp.zeros((local_len, PAD), f32)
+            for e in range(EXPERTS):
+                lane = HALF_HEADS * EXPERTS + h * EXPERTS + e
+                col = (e * HALF_HEADS + h) * PAD
+                part = dmix[at, col : col + PAD].astype(f32)
+                d_att = d_att + gated[:, lane : lane + 1] * part
+                d_gates = jnp.where(lanes == lane, jnp.sum(part * got, axis=-1, keepdims=True), d_gates)
+            d_att = d_att.astype(bf16)
+            p = probs[slot, h]
+            d_p = dot_f32(d_att, win[slot, :, v_cols], NT)
+            delta = jnp.sum(d_p * p, axis=-1, keepdims=True)
+            d_s = p * (d_p - delta)
+            dsum[h] += d_s
+            d_s = d_s.astype(bf16)
+            q = front[slot, :, cols].astype(bf16)
+            d_q = dot_f32(d_s, win[slot, :, cols]) * SCALE
+            d_k = dot_f32(d_s[:, MEM:], q, TN) * SCALE
+            d_v = dot_f32(p[:, MEM:].astype(bf16), d_att, TN).astype(bf16).astype(f32)
+            dfront[at, cols] = d_q.astype(bf16)
+            dfront[at, wide + h * PAD : wide + (h + 1) * PAD] = d_k.astype(bf16)
+            for e in range(EXPERTS):
+                lane = h * EXPERTS + e
+                col = W_QK + (e * HALF_HEADS + h) * PAD
+                part = front[slot, :, col : col + PAD]
+                d_gates = jnp.where(lanes == lane, jnp.sum(part * d_v, axis=-1, keepdims=True), d_gates)
+                dfront[at, col : col + PAD] = (gated[:, lane : lane + 1] * d_v).astype(bf16)
+        d_logits = jnp.where(lanes < N_ROUTE, d_gates * picks * gate * (1.0 - gate), 0.0)
+        dfront[at, MISC:W_A] = d_logits.astype(bf16)
+        return carry
+
+    lax.fori_loop(0, batches, attend, 0)
+    for j in sf.order:
+        sf.column(j)
+    for j in sf.order:
+        sf.line(j)
+    for j in si.order:
+        si.turn(j)
+    lax.fori_loop(batches, 2 * batches, attend, 0)
+    outs = [
+        pltpu.make_async_copy(src, dst, osem.at[i])
+        for i, (src, dst) in enumerate(((dfront, dfront_out), (db, db_out), (dhid, dhid_out), (dnorm, dnorm_out)))
     ]
-    for group in groups:
-        group.begin()
-    for group in groups:
-        for j in range(levels):
-            group.turn(j)
-    for group in groups:
-        for j in range(levels):
-            group.column(j)
-        for j in range(levels):
-            group.line(j)
-    for group, dst in zip(groups, dsts):
-        group.total(dst)
-    for group in groups:
-        group.drain()
-
-
-def scatter(levels, parts):
-    scratch = []
-    for p in parts:
-        rows, width = p.shape[2:]
-        for r in (rows // 2, rows // 2, rows, rows, rows, rows):
-            scratch.append(pltpu.VMEM((levels, r, width), jnp.bfloat16))
-    vmem = pl.BlockSpec(memory_space=pltpu.VMEM)
+    for cp in outs:
+        cp.start()
+    output_side(near)
+    last.wait()
+
+    def final(i, carry):
+        at = pl.ds(pl.multiple_of(i * step, step), step)
+        total_at = pl.ds(pl.multiple_of(c * rows + i * step, step), step)
+        tail = meta[c, at].astype(f32)
+        position = lax.broadcasted_iota(jnp.int32, (step, 1), 0) + (i * step) % local_len
+        keep = position.astype(f32) < tail[:, 41:42]
+        total = hidden[at] + branch[total_at] + arrived[at]
+        result[at] = jnp.where(keep, total, 0.0).astype(bf16)
+        return carry
+
+    lax.fori_loop(0, rows // step, final, 0)
+    out_r = pltpu.make_async_copy(result, layer_out, osem.at[4])
+    out_r.start()
+    for j in si.order:
+        si.column(j)
+    for j in si.order:
+        si.line(j)
+    sf.total(f_total)
+    out_f = pltpu.make_async_copy(f_total, f_out, osem.at[5])
+    out_f.start()
+
+    spread = MEM + 2 * local_len
+    ids = lax.broadcasted_iota(jnp.int32, (local_len, 1), 0)
+    lines = []
+    for h in range(HALF_HEADS):
+        turned = jnp.concatenate([dsum[h], jnp.zeros((local_len, local_len), f32)], axis=1)
+        bit = 1
+        while bit < local_len:
+            moved = pltpu.roll(turned, bit, 1)
+            turned = jnp.where(((local_len - 1 - ids) // bit) % 2 == 1, moved, turned)
+            bit *= 2
+        lines.append(jnp.sum(turned, axis=0, keepdims=True))
+    row_of = lax.broadcasted_iota(jnp.int32, (W_MISC, spread), 0)
+    table = jnp.zeros((W_MISC, spread), f32)
+    for h in range(HALF_HEADS):
+        table = jnp.where(row_of == COL_BIAS + h, lines[h], table)
+    high = table.astype(bf16)
+    low = (table - high.astype(f32)).astype(bf16)
+    distance = MEM + local_len - 1 - lax.broadcasted_iota(jnp.int32, (1, spread), 1)
+    bucket = bucket_index(distance)
+    wanted = (bucket // per_device) * shard + bucket % per_device
+
+    def by_bucket(i, carry):
+        at = pl.ds(pl.multiple_of(i * 128, 128), 128)
+        row_ids = lax.broadcasted_iota(jnp.int32, (128, spread), 0) + i * 128
+        one_hot = jnp.where(row_ids == wanted, 1.0, 0.0).astype(bf16)
+        mbias[at] = dot_f32(one_hot, high, NT) + dot_f32(one_hot, low, NT)
+        return carry
+
+    lax.fori_loop(0, mbias.shape[0] // 128, by_bucket, 0)
+    out_m = pltpu.make_async_copy(mbias, mbias_out, osem.at[6])
+    out_m.start()
+    si.total(i_total)
+    mine, other = [pl.ds(pl.multiple_of(k * shard, 16), shard) for k in (c, 1 - c)]
+    keep = pltpu.make_async_copy(i_total.at[mine], i_out.at[c], osem.at[7])
+    keep.start()
+    swap_i = exchange(i_total.at[other], i_out.at[c], 3)
+    swap_i.start()
+    sf.drain()
+    si.drain()
+    for cp in outs + [out_r, out_f, out_m, keep, swap_i]:
+        cp.wait()
+
+
+def kernel_call(body, ins, outs, scratch, sems, collective):
+    hbm = pl.BlockSpec(memory_space=pl.ANY)
     return pl.pallas_call(
-        functools.partial(scatter_kernel, levels),
-        out_shape=[jax.ShapeDtypeStruct(p.shape[2:], jnp.float32) for p in parts],
-        in_specs=[vmem] * 4,
-        out_specs=[vmem] * 4,
-        scratch_shapes=scratch + [pltpu.SemaphoreType.DMA((4, 8 * levels))] * 2,
+        body,
+        out_shape=[jax.ShapeDtypeStruct(s, k) for s, k in outs],
+        in_specs=[hbm] * len(ins),
+        out_specs=[hbm] * len(outs),
+        scratch_shapes=[pltpu.VMEM(s, k) for s, k in scratch] + [pltpu.SemaphoreType.DMA(s) for s in sems],
         compiler_params=pltpu.CompilerParams(
-            collective_id=2, has_side_effects=True, vmem_limit_bytes=VMEM_BYTES),
-    )(*parts)
+            collective_id=collective, has_side_effects=True, vmem_limit_bytes=VMEM_BYTES),
+    )(*ins)
+
+
+def middle(levels, batches, local_len, per_device, shard, ins):
+    bf16, f32 = jnp.bfloat16, jnp.float32
+    w_f, w_i, w_o, act, slope, xs, n2, hidden, vec, att, gates, front, win, probs = ins
+    ff, width = w_f.shape
+    rows = batches * local_len
+    both = 2 * rows
+    f_rows = ff // (4 * levels)
+    i_rows = width // (4 * levels)
+    outs = [
+        ((f_rows, width), f32), ((SIDE, shard, ff), f32), ((rows, width), bf16), ((both, W_A), bf16),
+        ((both, width), bf16), ((rows, width), f32), ((8, width), f32), ((width, W_MISC), f32),
+    ]
+    scratch = [(v.shape, v.dtype) for v in (w_f, w_i, w_o, act, slope)]
+    scratch += [((2, rows, width), bf16), ((2, rows, 128), bf16)]
+    scratch += [(v.shape, v.dtype) for v in (n2, hidden, vec, att, gates)]
+    scratch += [((2, local_len, W_A), f32), ((2,) + win.shape[1:], bf16), ((2,) + probs.shape[1:], f32)]
+    scratch += [
+        ((both, width), f32), ((rows, width), f32), ((rows, width), f32), ((both, width), bf16),
+        ((both, W_O), bf16), ((both, W_A), bf16), ((HALF_HEADS, local_len, MEM + local_len), f32),
+        ((8, 128), f32), ((8, width), f32), ((rows, width), bf16), ((width, W_MISC), f32),
+        ((f_rows, width), f32), ((i_rows, ff), f32),
+    ]
+    scratch += scatter_scratch(levels, [(f_rows, width), (i_rows, ff)])
+    sems = [(2, 8 * levels), (2, 8 * levels), (12,), (3, 2), (4,), (4,), (8,)]
+    body = functools.partial(middle_kernel, levels, batches, local_len, per_device, shard)
+    return kernel_call(body, ins, outs, scratch, sems, 2)
+
+
+def last_kernel(
+    levels, batches, local_len, shard,
+    db_in, mixed_in, act_in, dfront_in, wa_in, mbias_in, dnorm_in, dhid_in, xs_in, vec_in,
+    a_out, o_out, m_out, grad_out,
+    db, mixed, act, dfront, w_a, mbias, dnorm, dhid, x_own, vec, branch, arrived, result, norms,
+    a_total, o_total, m_total, *rest,
+):
+    bf16, f32 = jnp.bfloat16, jnp.float32
+    a_bufs, o_bufs, m_bufs = rest[:7], rest[7:14], rest[14:21]
+    send, recv, lsem, esend, erecv, osem = rest[21:]
+    d, t = lax.axis_index("doc"), lax.axis_index("tm")
+    z, c = t // 2, t % 2
+    nb = neighbours(2 * levels)
+    width = db.shape[1]
+    rows = batches * local_len
+    far = pl.ds(pl.multiple_of((1 - c) * rows, rows), rows)
+    near = pl.ds(pl.multiple_of(c * rows, rows), rows)
+    pairs = (
+        (db_in, db), (mixed_in, mixed), (act_in, act), (dfront_in, dfront), (wa_in, w_a), (mbias_in, mbias),
+        (dnorm_in, dnorm), (dhid_in, dhid), (xs_in.at[c, :, pl.ds(0, width)], x_own), (vec_in, vec))
+    loads = [pltpu.make_async_copy(src, dst, lsem.at[i]) for i, (src, dst) in enumerate(pairs)]
+    for cp in loads:
+        cp.start()
+    enter(nb, z, levels)
+    so, sa, sm = [
+        Scatter(bufs[0], bufs[1:], (send.at[i], recv.at[i]), nb, d, z, levels)
+        for i, bufs in enumerate((o_bufs, a_bufs, m_bufs))
+    ]
+    block_rows = o_bufs[0].shape[2]
+    span = levels * block_rows
+
+    def weight_grad(scatter, left, right, chunk):
+        total = right.shape[1] if scatter is so else MISC
+        for place, column in enumerate(scatter.columns):
+            at = pl.ds(pl.multiple_of(column * span, span), span)
+
+            def body(i, carry):
+                cols = pl.ds(pl.multiple_of(i * chunk, chunk), chunk)
+                got = dot_f32(left[:, at], right[:, cols], TN).astype(bf16)
+                scatter.src[column, :, :, cols] = got.reshape(levels, block_rows, chunk)
+                return carry
+
+            lax.fori_loop(0, total // chunk, body, 0)
+            scatter.begin(place)
+
+    loads[0].wait()
+    loads[1].wait()
+    weight_grad(so, db, mixed, 640)
+    loads[2].wait()
+    loads[3].wait()
+    weight_grad(sa, act, dfront, 896)
+    for j in so.order:
+        so.turn(j)
+    loads[4].wait()
+
+    def exchange(src, dst, index):
+        return pltpu.make_async_remote_copy(
+            src_ref=src, dst_ref=dst, send_sem=esend.at[index], recv_sem=erecv.at[index],
+            device_id=nb["c"], device_id_type=MESH)
+
+    def input_side(at):
+        def body(i, carry):
+            cols = pl.ds(pl.multiple_of(i * 256, 256), 256)
+            branch[at, cols] = dot_f32(dfront[at], w_a[cols], NT)
+            return carry
+
+        lax.fori_loop(0, width // 256, body, 0)
+
+    input_side(far)
+    give = exchange(branch.at[far], arrived, 0)
+    give.start()
+    input_side(near)
+    for cp in loads[5:]:
+        cp.wait()
+    give.wait()
+    norms[...] = jnp.zeros_like(norms)
+    norms[COL_NORM + 2 : COL_NORM + 4] = dnorm[0:2]
+    step = 64
+
+    def first(i, carry):
+        at = pl.ds(pl.multiple_of(i * step, step), step)
+        total_at = pl.ds(pl.multiple_of(c * rows + i * step, step), step)
+        normed, inverse = norm_rows(x_own[at].astype(f32))
+        up = branch[total_at] + arrived[at]
+        norms[COL_NORM : COL_NORM + 1] += jnp.sum(up * normed, axis=0, keepdims=True)
+        norms[COL_NORM + 1 : COL_NORM + 2] += jnp.sum(up, axis=0, keepdims=True)
+        got = norm_rows_backward(up, normed, inverse, vec[COL_NORM : COL_NORM + 1])
+        result[at] = dhid[at] + got
+        return carry
+
+    lax.fori_loop(0, rows // step, first, 0)
+    out_g = pltpu.make_async_copy(result, grad_out, osem.at[0])
+    out_g.start()
+    misc = dot_f32(act[...], dfront[:, MISC:W_A], TN) + mbias[...] + norms[...].T
+    misc = misc.astype(bf16).reshape(4, levels, block_rows, W_MISC)
+    for column in range(4):
+        m_bufs[0][column] = misc[column]
+    for place in range(3):
+        sm.begin(place)
+    for j in sa.order:
+        sa.turn(j)
+    for j in so.order:
+        so.column(j)
+    for j in so.order:
+        so.line(j)
+    for j in sm.order:
+        sm.turn(j)
+    for j in sa.order:
+        sa.column(j)
+    for j in sa.order:
+        sa.line(j)
+    for j in sm.order:
+        sm.column(j)
+    for j in sm.order:
+        sm.line(j)
+    mine, other = [pl.ds(pl.multiple_of(k * shard, 16), shard) for k in (c, 1 - c)]
+    ends = []
+    for i, (scatter, total, out) in enumerate(((so, o_total, o_out), (sa, a_total, a_out), (sm, m_total, m_out))):
+        scatter.total(total)
+        keep = pltpu.make_async_copy(total.at[mine], out.at[c], osem.at[1 + i])
+        keep.start()
+        move = exchange(total.at[other], out.at[c], 1 + i)
+        move.start()
+        ends += [keep, move]
+    for scatter in (so, sa, sm):
+        scatter.drain()
+    for cp in ends + [out_g]:
+        cp.wait()
+
+
+def last(levels, batches, local_len, shard, ins):
+    bf16, f32 = jnp.bfloat16, jnp.float32
+    db, mixed, act, dfront, w_a, mbias, dnorm, dhid, xs, vec = ins
+    both, width = db.shape
+    rows = both // 2
+    block_rows = width // (4 * levels)
+    outs = [((SIDE, shard, w), f32) for w in (MISC, W_O, W_MISC)] + [((rows, width), f32)]
+    scratch = [(v.shape, v.dtype) for v in (db, mixed, act, dfront, w_a, mbias, dnorm, dhid)]
+    scratch += [((rows, width), bf16), (vec.shape, f32), ((both, width), f32), ((rows, width), f32)]
+    scratch += [((rows, width), f32), ((W_MISC, width), f32)]
+    scratch += [((block_rows, w), f32) for w in (MISC, W_O, W_MISC)]
+    scratch += scatter_scratch(levels, [(block_rows, w) for w in (MISC, W_O, W_MISC)])
+    sems = [(3, 8 * levels), (3, 8 * levels), (10,), (4,), (4,), (4,)]
+    body = functools.partial(last_kernel, levels, batches, local_len, shard)
+    return kernel_call(body, ins, outs, scratch, sems, 3)
 
 
 def split_heads(a, lead):
@@ -1143,15 +1637,6 @@
     rows = a.shape[1]
     a = a.reshape(SIDE, rows, lead, HALF_HEADS, PAD)[..., :HEAD_DIM]
     return jnp.transpose(a, (1, 2, 0, 3, 4)).reshape(rows, lead * HEADS * HEAD_DIM)
-
-
-def bias_grad(score_sum, local_len):
-    heads = score_sum.shape[0]
-    spread = MEM + 2 * local_len - 1
-    padded = jnp.pad(score_sum, ((0, 0), (0, 0), (local_len - 1, 0))).reshape(heads, local_len * spread)
-    padded = jnp.pad(padded, ((0, 0), (0, local_len))).reshape(heads, local_len, spread + 1)
-    by_distance = jnp.sum(padded, axis=1)[:, :spread][:, ::-1]
-    return jnp.einsum("hk,kc->hc", by_distance, bucket_matrix(local_len), precision=HIGH)
 
 
 def on_chip(
@@ -1205,127 +1690,34 @@
     x_pack = jnp.concatenate([x_own, grad_own] + metas, axis=1)
     g_pack = given_cache.reshape(batches, MEM, 2 * HEADS * HEAD_DIM)
 
-    (a_all, o_all, i_all, f_all, x_all, act_one, front, gates, window, probs_b, attended, mixed, hidden, act_two
-     ) = forward(levels, batches, local_len, buckets, (a_pack, a_o, i_pack, ffn_out, x_pack, g_pack))
+    (a_all, o_all, i_all, f_all, xs, act_one, front, gates, win, probs, attended, mixed, hidden, n2, vec, act,
+     slope) = forward(levels, batches, local_len, buckets, (a_pack, a_o, i_pack, ffn_out, x_pack, g_pack))
     w_a = a_all.reshape(width, W_A)
     w_o = o_all.reshape(width, W_O)
     w_i = i_all.reshape(width, -1)
     w_f = f_all.reshape(-1, width)
-
-    vectors = w_a[:, MISC + COL_NORM : MISC + COL_NORM + 4].T.astype(f32)
-    gain_one, shift_one, gain_two, shift_two = [v.reshape(1, width) for v in vectors]
-    both = 2 * rows
-    wide = HALF_HEADS * PAD
-    grad_all = x_all[:, :, width : 2 * width].reshape(both, width)
-    meta_all = x_all[:, :, 2 * width :].reshape(both, 2, 128)
-    pick_mine = jnp.where(side == 0, meta_all[:, 0, :N_ROUTE], meta_all[:, 1, :N_ROUTE]).astype(f32)
-    gates = gates[:, :N_ROUTE]
-    gated = (gates * pick_mine).reshape(both, 2, HALF_HEADS, EXPERTS)
-    value_gate = jnp.transpose(gated[:, 0], (0, 2, 1))[..., None]
-    output_gate = jnp.transpose(gated[:, 1], (0, 2, 1))[..., None]
-    parts = front[:, W_QK:MISC].reshape(both, EXPERTS, HALF_HEADS, PAD)
-    window = window.reshape(2 * batches, MEM + local_len, 2, HALF_HEADS, PAD)
-    keys, vals = window[:, :, 0], window[:, :, 1]
-    queries = front[:, :wide].astype(bf16).reshape(2 * batches, local_len, HALF_HEADS, PAD)
-    probs = probs_b.astype(f32)
-    attended_f = attended.astype(f32).reshape(both, 1, HALF_HEADS, PAD)
-
-    def mine(a):
-        return lax.dynamic_index_in_dim(a, side, 0, keepdims=False)
-
-    def other(a):
-        return lax.dynamic_index_in_dim(a, 1 - side, 0, keepdims=False)
-
-    def paired(own):
-        arrived = swap(own)
-        return jnp.where(side == 0, jnp.stack([own, arrived]), jnp.stack([arrived, own])).reshape(both, -1)
-
-    unused, unit_one, inv_one = norm_forward(x_own.astype(f32), gain_one, shift_one)
-
-    unused, unit_two, inv_two = norm_forward(hidden, gain_two, shift_two)
-    pre_act = jnp.dot(act_two, w_i, preferred_element_type=f32)
-    activated = jax.nn.gelu(pre_act, approximate=False).astype(bf16)
-    ffn = jnp.dot(activated, w_f, preferred_element_type=f32).reshape(2, rows, width)
-    layer_out = (mask * (hidden + mine(ffn) + swap(other(ffn)))).astype(bf16).reshape(tokens.shape)
-    d_f = jnp.einsum("nf,nd->fd", activated, grad_all, preferred_element_type=f32).astype(bf16)
-    d_act = jnp.einsum("nd,fd->nf", grad_all, w_f, preferred_element_type=f32)
-    d_pre = (d_act * gelu_slope(pre_act)).astype(bf16)
-    d_i = jnp.einsum("nd,nf->df", act_two, d_pre, preferred_element_type=f32).astype(bf16)
-    d_two = jnp.einsum("nf,df->nd", d_pre, w_i, preferred_element_type=f32).reshape(2, rows, width)
-    d_two = mine(d_two) + swap(other(d_two))
-    d_from_two, d_gain_two, d_shift_two = norm_backward(d_two, unit_two, inv_two, gain_two)
-    upstream = cotangent.reshape(rows, width).astype(f32) * mask
-    d_hidden = upstream + d_from_two
-
-    d_branch = paired(d_hidden.astype(bf16))
-    d_o = jnp.einsum("nd,nk->dk", d_branch, mixed, preferred_element_type=f32).astype(bf16)
-    d_mixed = jnp.dot(d_branch, w_o, preferred_element_type=f32).astype(bf16)
-    d_mixed = d_mixed.astype(f32).reshape(both, EXPERTS, HALF_HEADS, PAD)
-    d_gate_out = jnp.sum(d_mixed * attended_f, axis=-1)
-    d_attended = jnp.sum(d_mixed * output_gate, axis=1).astype(bf16).reshape(2 * batches, local_len, HALF_HEADS, PAD)
-    d_probs = jnp.einsum("bqhd,bkhd->bhqk", d_attended, vals, preferred_element_type=f32)
-    delta = jnp.sum(d_probs * probs, axis=-1, keepdims=True)
-    d_scores = probs * (d_probs - delta)
-    d_table = bias_grad(jnp.sum(d_scores, axis=0), local_len)
-    d_scores_b = d_scores.astype(bf16)
-    d_queries = jnp.einsum("bhqk,bkhd->bqhd", d_scores_b, keys, preferred_element_type=f32) * SCALE
-    d_keys = jnp.einsum("bhqk,bqhd->bkhd", d_scores_b[..., MEM:], queries, preferred_element_type=f32) * SCALE
-    d_vals = jnp.einsum("bhqk,bqhd->bkhd", probs_b[..., MEM:], d_attended, preferred_element_type=f32)
-    d_values = d_vals.reshape(both, 1, HALF_HEADS, PAD).astype(bf16).astype(f32)
-    d_gate_val = jnp.sum(parts * d_values, axis=-1)
-    d_parts = (value_gate * d_values).reshape(both, W_VAL).astype(bf16)
-    d_gates = jnp.concatenate(
-        [jnp.transpose(g, (0, 2, 1)).reshape(both, HALF_HEADS * EXPERTS) for g in (d_gate_val, d_gate_out)], axis=1)
-    d_logits = d_gates * pick_mine * gates * (1.0 - gates)
-    d_front = jnp.concatenate(
-        [
-            d_queries.reshape(both, wide).astype(bf16),
-            d_keys.reshape(both, wide).astype(bf16),
-            d_parts,
-            pad_last(d_logits.astype(bf16), W_MISC),
-        ],
-        axis=1,
-    )
-    d_a = jnp.einsum("nd,nk->dk", act_one, d_front, preferred_element_type=f32).astype(bf16)
-    d_one = jnp.einsum("nk,dk->nd", d_front, w_a, preferred_element_type=f32).reshape(2, rows, width)
-    d_one = mine(d_one) + swap(other(d_one))
-    d_from_one, d_gain_one, d_shift_one = norm_backward(
-        d_one, unit_one, inv_one, gain_one)
-    input_grad = (d_hidden + d_from_one).reshape(tokens.shape)
-    d_norms = jnp.stack([d_gain_one, d_shift_one, d_gain_two, d_shift_two], axis=1)
-    d_bias = jnp.pad(
-        d_table.T.reshape(4 * count, buckets, HALF_HEADS), ((0, 0), (0, shard - buckets), (0, 0))
-    ).reshape(width, HALF_HEADS)
-    d_misc = jnp.concatenate([d_norms, d_bias], axis=1).astype(bf16)
-    d_a = jnp.concatenate([d_a[:, : MISC + N_ROUTE], d_misc, d_a[:, MISC + N_ROUTE + 4 + HALF_HEADS :]], axis=1)
-
-    s_a, s_o, s_i, s_f = scatter(
-        levels,
-        (
-            d_a.reshape(4, levels, 2 * shard, W_A),
-            d_o.reshape(4, levels, 2 * shard, W_O),
-            d_i.reshape(4, levels, 2 * shard, -1),
-            d_f.reshape(4, levels, hidden_block, width),
-        ),
-    )
-    chip = jnp.concatenate([s_a, s_o, s_i], axis=1).reshape(2, shard, -1)
-    kept, arrived = mine(chip), swap(other(chip))
-    sides = jnp.where(side == 0, jnp.stack([kept, arrived]), jnp.stack([arrived, kept]))
-    qk_share = join_heads(sides[:, :, :W_QK], 2)
-    value_share = join_heads(sides[:, :, W_QK:MISC], EXPERTS)
-    output_share = join_heads(sides[:, :, W_A : W_A + W_O], EXPERTS).T
-    misc = sides[:, :, MISC:W_A]
+    out_share, i_sides, layer_out, d_front, d_branch, d_hidden, d_norm, d_bias = middle(
+        levels, batches, local_len, buckets, shard,
+        (w_f, w_i, w_o, act, slope, xs, n2, hidden, vec, attended, gates, front, win, probs))
+    a_sides, o_sides, misc, input_grad = last(
+        levels, batches, local_len, shard,
+        (d_branch, mixed, act_one, d_front, w_a, d_bias, d_norm, d_hidden, xs, vec))
+    layer_out = layer_out.reshape(tokens.shape)
+    input_grad = input_grad.reshape(tokens.shape)
+    qk_share = join_heads(a_sides[:, :, :W_QK], 2)
+    value_share = join_heads(a_sides[:, :, W_QK:], EXPERTS)
+    output_share = join_heads(o_sides, EXPERTS).T
     router_share = jnp.transpose(
         misc[:, :, :N_ROUTE].reshape(SIDE, shard, 2, HALF_HEADS * EXPERTS), (1, 2, 0, 3)
     ).reshape(shard, 2 * HEADS * EXPERTS)
     norm_share = misc[0, :, COL_NORM : COL_NORM + 4] + misc[1, :, COL_NORM : COL_NORM + 4]
     bias_share = jnp.transpose(misc[:, :buckets, COL_BIAS : COL_BIAS + HALF_HEADS], (0, 2, 1)).reshape(HEADS, buckets)
     in_share = jnp.transpose(
-        sides[:, :, W_A + W_O :].reshape(SIDE, shard, blocks, hidden_block), (1, 2, 0, 3)
+        i_sides.reshape(SIDE, shard, blocks, hidden_block), (1, 2, 0, 3)
     ).reshape(shard, -1)
     return (
         layer_out, input_grad, norm_share[:, 0], norm_share[:, 1], qk_share, router_share, value_share,
-        output_share, bias_share, norm_share[:, 2], norm_share[:, 3], in_share, s_f,
+        output_share, bias_share, norm_share[:, 2], norm_share[:, 3], in_share, out_share,
     )
 
 

time: 558 us -> 409 us (0.73); the launches traced: 547 us -> 406 us
  local copies, waits for them, and re-layouts: 97.1 us -> 22 us
  matrix products: 57.1 us -> 0 us
  other arithmetic: 41.4 us -> 5.85 us
  Pallas kernels: 347 us -> 377 us
    dot_general x15 -> x0, matrix products: 57.1 us -> none  [the longest x1 14.5 us: on_chip(): pre_act = jnp.dot(act_two, w_i, preferred_element_type=f32)]
    pallas_call x1 -> x2, Pallas kernels: 177 us -> 206 us  [kernel_call(): pl.pallas_call(body, out_shape=[jax.ShapeDtypeStruct(s, k) for s, k in ou...]
    reshape x10 -> x1, local copies, waits for them, and re-layouts: 19.9 us -> 1.21 us  [on_chip(): in_share = jnp.transpose(i_sides.reshape(SIDE, shard, blocks, hidden_bloc...]
    reduce_sum x9 -> x0, other arithmetic: 16.9 us -> none  [the longest x1 9.56 us: on_chip(): jnp.sum(d_mixed * output_gate, axis=1).astype(bf16)]
    convert_element_type x4 -> x0, other arithmetic: 13.9 us -> none  [the longest x1 9.34 us: on_chip(): d_parts = (value_gate * d_values).reshape(both, W_VAL).astype(bf16)]
    unnamed x100 -> x30, local copies, waits for them, and re-layouts: 17.3 us -> 5.73 us
    transpose x7 -> x2, local copies, waits for them, and re-layouts: 11.7 us -> 0.44 us  [on_chip(): jnp.transpose(i_sides.reshape(SIDE, shard, blocks, hidden_block), (1, 2,...]
    concatenate x2 -> x0, local copies, waits for them, and re-layouts: 9.31 us -> none  [the longest x1 7.67 us: on_chip(): jnp.concatenate([d_a[:, :MISC + N_ROUTE], d_misc, d_a[:, MISC + N_ROUTE +...]
  transfers between devices with their start and end apart: 5 -> 0, of which waited for: 1 -> 0; matrix products, arithmetic and copies ran while one was open for 14% -> 0% of each run, Pallas kernels for 0% -> 0%
where the time goes in v3:
time: 409 us; the launch traced here: 406 us
  Pallas kernels  377 us (92%)
  local copies, waits for them, and re-layouts  22 us (5%)
  other arithmetic  5.85 us (1%)
    pallas_call x2, Pallas kernels, kernel_call(): pl.pallas_call(body, out_shape=[jax.ShapeDtypeStruct(s, k) for s, k in ou...  206 us
    pallas_call x1, Pallas kernels, forward(): pl.pallas_call(functools.partial(forward_kernel, levels, batches, local_l...  171 us

profile of v3, /device:TPU:0, one launch (start us, length us, event | category | flops | bytes accessed | tf_op | source)
XLA Modules:
  0.0 405.9 jit_solution(18413182136760596956)
XLA Ops:
  0.7 0.7 convert_bitcast_fusion
  1.5 0.7 bitcast_convert_fusion
  2.3 0.7 pad_maximum_fusion.4
  3.0 0.7 fusion.20
  3.7 0.8 copy.160
  4.6 0.7 copy.164
  5.4 0.7 copy.167
  6.2 0.8 copy.157
  7.6 0.9 reshape.187
  8.7 1.1 reshape.189
  10.1 0.7 fusion.7.a_in
  11.2 0.7 reshape.195.o_in
  12.2 0.8 reshape.197.i_in
  13.2 1.1 fusion.4.x_in
  14.3 171.1 %shard_map.273 = (bf16[4,4,64,1920]{3,2,1,0:T(8,128)(2,1)}, bf16[4,4,64,1280]{3,2,1,0:T(8,128)(2,1)}, bf16[4,4,64,2048]{3,2,1,0:T(8,128)(2,1)}, bf16[4,4,128,102...) custom-call(bf16[2,32,1920]{2,1,0:T(8,128)(2,1)} %fusion.7.a_in, ...), custom_call_target="tpu_custom_call" | custom-call | tf_op jit(solution)/shard_map/pallas_call | solution.py:976
  185.3 112.0 %shard_map.274 = (f32[128,1024]{1,0:T(8,128)}, f32[2,32,2048]{2,1,0:T(8,128)}, bf16[256,1024]{1,0:T(8,128)(2,1)}, bf16[512,1920]{1,0:T(8,128)(2,1)}, bf16[512,10...) custom-call(bf16[2048,1024]{1,0:T(8,128)(2,1)} %bitcast.107, ...), custom_call_target="tpu_custom_call" | custom-call | tf_op jit(solution)/shard_map/pallas_call | solution.py:1444
  297.4 93.8 %shard_map.275 = (f32[2,32,1792]{2,1,0:T(8,128)}, f32[2,32,1280]{2,1,0:T(8,128)}, f32[2,32,128]{2,1,0:T(8,128)}, f32[256,1024]{1,0:T(8,128)}) custom-call(bf16[512,1024]{1,0:T(8,128)(2,1)} %get-tuple-element.57.db_in, bf16[512,1280]{1,0:T(8,128)(2,1)} %get-tuple-element.58.mixed_in, bf16[512,1024]{1,0:T(8,128)(2,1)} %get-tuple-element.59.act_in, ...), custom_call_target="tpu_custom_call" | custom-call | tf_op jit(solution)/shard_map/pallas_call | solution.py:1444
  391.2 0.8 slice_bitcast_fusion.3
  392.0 0.7 copy.178
  392.6 0.8 slice_add_fusion
  393.5 0.5 slice_bitcast_fusion.4
  394.1 0.9 copy.174
  395.0 0.7 copy.182
  395.6 0.9 slice.63
  396.6 1.0 slice.66
  397.9 1.0 reshape.213
  399.1 0.8 reshape.209
  400.3 1.0 reshape.215
  401.9 1.2 reshape.218
  403.1 0.8 copy.211
  403.9 1.0 copy.212
  404.9 0.8 copy.213
  (67 shorter events, 3.7 us)
Async XLA Ops:
  0.6 11.3 %copy-start.7 = (bf16[32,4096]{1,0:T(8,128)(2,1)S(1)}, bf16[32,4096]{1,0:T(8,128)(2,1)}, u32[]{:S(2)}) copy-start(bf16[32,4096]{1,0:T(8,128)(2,1)} %param.34) | copy-start | bytes 786436
  0.7 10.2 %copy-start.8 = (bf16[2240,32]{0,1:T(8,128)(2,1)S(1)}, bf16[2240,32]{0,1:T(8,128)(2,1)}, u32[]{:S(2)}) copy-start(bf16[2240,32]{0,1:T(8,128)(2,1)} %param.30) | copy-start | bytes 430084
  7.3 5.7 %copy-start.1 = (bf16[2,1,128,1024]{3,2,1,0:T(8,128)(2,1)S(1)}, bf16[2,1,128,1024]{3,2,1,0:T(8,128)(2,1)}, u32[]{:S(2)}) copy-start(bf16[2,1,128,1024]{3,2,1,0:T(8,128)(2,1)} %param.19) | copy-start | bytes 1572868
  9.8 3.4 copy-start.5
  394.1 5.9 %copy-start.6 = (f32[2,32,1280]{2,1,0:T(8,128)S(1)}, f32[2,32,1280]{2,1,0:T(8,128)}, u32[]{:S(2)}) copy-start(f32[2,32,1280]{2,1,0:T(8,128)} %get-tuple-element.68) | copy-start | bytes 983044
  397.8 3.5 copy-start.4
  400.3 2.8 copy-start.3
  401.4 2.5 copy-start
  401.9 3.0 copy-start.2

commit v4 on v3

--- a/solution.py
+++ b/solution.py
@@ -373,7 +373,7 @@
 N_ROUTE = 2 * HALF_HEADS * EXPERTS
 COL_NORM = N_ROUTE
 COL_BIAS = N_ROUTE + 4
-VMEM_BYTES = 60 * 1024 * 1024
+VMEM_BYTES = 63 * 1024 * 1024
 SCALE = HEAD_DIM ** (-0.5)
 
 
@@ -1000,17 +1000,13 @@
 
 
 class Scatter:
-    def __init__(self, src, bufs, sems, nb, d, z, levels):
-        self.src, self.nb, self.d, self.z, self.levels = src, nb, d, z, levels
-        self.cx, self.cy, self.rx, self.ry, self.up, self.down = bufs
+    def __init__(self, src, view, sems, nb, d, z, levels, total):
+        self.src, self.view, self.nb, self.d, self.z, self.levels = src, view, nb, d, z, levels
         self.send, self.recv = sems
+        self.sum = total
         self.half = src.shape[2] // 2
         self.by_x, self.by_y = d + 1 - 2 * (d % 2), (d + 2) % 4
         self.low, self.high = pl.ds(0, self.half), pl.ds(self.half, self.half)
-        self.columns = (3 - d, self.by_x, self.by_y, d)
-        self.order = []
-        for k in range((levels + 1) // 2):
-            self.order += [levels - 1 - k, k] if levels - 1 - k != k else [k]
 
     def copy(self, src, dst, slot, to):
         return pltpu.make_async_remote_copy(
@@ -1018,98 +1014,68 @@
             device_id=self.nb[to], device_id_type=MESH)
 
     def corner(self, j, to):
-        part = self.low if to == "x" else self.high
-        buf = self.cx if to == "x" else self.cy
-        return self.copy(self.src.at[3 - self.d, j, part], buf.at[j], (0 if to == "x" else self.levels) + j, to)
+        part, name, base = (self.low, "cx", 0) if to == "x" else (self.high, "cy", self.levels)
+        return self.copy(self.src.at[3 - self.d, j, part], self.view(name, j), base + j, to)
 
     def direct(self, j, to):
-        part = self.low if to == "x" else self.high
-        column = self.by_x if to == "x" else self.by_y
-        buf = self.rx if to == "x" else self.ry
-        return self.copy(self.src.at[column, j, part], buf.at[j, part], (2 if to == "x" else 3) * self.levels + j, to)
+        if to == "x":
+            column, part, name, base = self.by_x, self.low, "rx", 2 * self.levels
+        else:
+            column, part, name, base = self.by_y, self.high, "ry", 3 * self.levels
+        return self.copy(self.src.at[column, j, part], self.view(name, j).at[part], base + j, to)
 
     def relay(self, j, to):
-        part = self.high if to == "x" else self.low
-        held = self.cy if to == "x" else self.cx
-        buf = self.rx if to == "x" else self.ry
-        return self.copy(held.at[j], buf.at[j, part], (4 if to == "x" else 5) * self.levels + j, to)
-
-    def along(self, j, to):
-        buf = self.up if to == "up" else self.down
-        return self.copy(buf.at[j], buf.at[j], (6 if to == "up" else 7) * self.levels + j, to)
-
-    def begin(self, place):
-        for j in self.order:
-            if place == 0:
-                self.corner(j, "x").start()
-                self.corner(j, "y").start()
-            elif place == 1:
-                self.direct(j, "x").start()
-            elif place == 2:
-                self.direct(j, "y").start()
+        if to == "x":
+            held, part, name, base = "cy", self.high, "rx", 4 * self.levels
+        else:
+            held, part, name, base = "cx", self.low, "ry", 5 * self.levels
+        return self.copy(self.view(held, j), self.view(name, j).at[part], base + j, to)
+
+    def along(self, j, to, first=False):
+        base = (6 if to == "up" else 7) * self.levels
+        return self.copy(self.view("rx" if first else to, j), self.view(to, j), base + j, to)
+
+    def issue(self, j):
+        self.corner(j, "x").start()
+        self.corner(j, "y").start()
+        self.direct(j, "x").start()
+        self.direct(j, "y").start()
 
     def turn(self, j):
         self.corner(j, "x").wait_recv()
-        add_rows(self.cx.at[j], [self.cx.at[j], self.src.at[self.by_y, j, self.low]])
+        add_rows(self.view("cx", j), [self.view("cx", j), self.src.at[self.by_y, j, self.low]])
         self.relay(j, "y").start()
         self.corner(j, "y").wait_recv()
-        add_rows(self.cy.at[j], [self.cy.at[j], self.src.at[self.by_x, j, self.high]])
+        add_rows(self.view("cy", j), [self.view("cy", j), self.src.at[self.by_x, j, self.high]])
         self.relay(j, "x").start()
 
     def column(self, j):
-        self.direct(j, "x").wait_recv()
-        self.direct(j, "y").wait_recv()
-        self.relay(j, "x").wait_recv()
-        self.relay(j, "y").wait_recv()
-        add_rows(self.rx.at[j], [self.rx.at[j], self.ry.at[j], self.src.at[self.d, j]])
-
-    def line(self, j):
-        z, levels = self.z, self.levels
-
-        @pl.when(z < j)
+        for to in ("x", "y"):
+            self.direct(j, to).wait_recv()
+            self.relay(j, to).wait_recv()
+        add_rows(self.view("rx", j), [self.view("rx", j), self.view("ry", j), self.src.at[self.d, j]])
+
+    def lift(self, j, stage):
+        def hop(to):
+            if stage:
+                self.along(j, to).wait_recv()
+                add_rows(self.view(to, j), [self.view(to, j), self.view("rx", j)])
+            self.along(j, to, first=stage == 0).start()
+
+        if stage < j:
+            pl.when(self.z == stage)(lambda: hop("up"))
+        if self.levels - 1 - stage > j:
+            pl.when(self.z == self.levels - 1 - stage)(lambda: hop("down"))
+
+    def total(self, j):
+        @pl.when(self.z == j)
         def _():
-            @pl.when(z > 0)
-            def _():
-                self.along(j, "up").wait_recv()
-                add_rows(self.up.at[j], [self.up.at[j], self.rx.at[j]])
-
-            @pl.when(z == 0)
-            def _():
-                add_rows(self.up.at[j], [self.rx.at[j]])
-
-            self.along(j, "up").start()
-
-        @pl.when(z > j)
-        def _():
-            @pl.when(z < levels - 1)
-            def _():
-                self.along(j, "down").wait_recv()
-                add_rows(self.down.at[j], [self.down.at[j], self.rx.at[j]])
-
-            @pl.when(z == levels - 1)
-            def _():
-                add_rows(self.down.at[j], [self.rx.at[j]])
-
-            self.along(j, "down").start()
-
-    def total(self, dst):
-        z, levels = self.z, self.levels
-
-        @pl.when(z == 0)
-        def _():
-            self.along(z, "down").wait_recv()
-            add_rows(dst, [self.rx.at[z], self.down.at[z]])
-
-        @pl.when(z == levels - 1)
-        def _():
-            self.along(z, "up").wait_recv()
-            add_rows(dst, [self.rx.at[z], self.up.at[z]])
-
-        @pl.when(jnp.logical_and(z > 0, z < levels - 1))
-        def _():
-            self.along(z, "up").wait_recv()
-            self.along(z, "down").wait_recv()
-            add_rows(dst, [self.rx.at[z], self.up.at[z], self.down.at[z]])
+            terms = [self.view("rx", j)]
+            for to, there in (("up", j > 0), ("down", j < self.levels - 1)):
+                if there:
+                    self.along(j, to).wait_recv()
+                    terms.append(self.view(to, j))
+            add_rows(self.sum, terms)
 
     def drain(self):
         for j in range(self.levels):
@@ -1121,13 +1087,32 @@
             pl.when(self.z > j)(lambda: self.along(j, "down").wait_send())
 
 
-def scatter_scratch(levels, shapes):
-    out = []
-    for rows, width in shapes:
-        out.append(((4, levels, rows, width), jnp.bfloat16))
-        for r in (rows // 2, rows // 2, rows, rows, rows, rows):
-            out.append(((levels, r, width), jnp.bfloat16))
-    return out
+class Pipeline:
+    def __init__(self, units, levels, ahead):
+        self.units, self.levels, self.ahead, self.now = units, levels, ahead, 0
+
+    def each(self, n, act):
+        if 0 <= n < len(self.units):
+            for scatter, j in self.units[n]:
+                act(scatter, j)
+
+    def begin(self):
+        for n in range(self.ahead):
+            self.each(n, lambda s, j: s.issue(j))
+
+    def step(self):
+        n = self.now
+        self.each(n, lambda s, j: s.turn(j))
+        self.each(n + self.ahead, lambda s, j: s.issue(j))
+        self.each(n - 1, lambda s, j: s.column(j))
+        for stage in range(self.levels - 1):
+            self.each(n - 2 - stage, lambda s, j: s.lift(j, stage))
+        self.each(n - 1 - self.levels, lambda s, j: s.total(j))
+        self.now += 1
+
+    def finish(self):
+        while self.now < len(self.units) + self.levels + 1:
+            self.step()
 
 
 def norm_rows(values):
@@ -1146,18 +1131,23 @@
     return inside * inverse
 
 
-def middle_kernel(
+VEC_ROW = COL_NORM // 8 * 8
+VEC_GAIN = COL_NORM - VEC_ROW
+
+
+def backward_kernel(
     levels, batches, local_len, per_device, shard,
-    wf_in, wi_in, wo_in, act_in, slope_in, xs_in, n2_in, hidden_in, vec_in, att_in, gates_in, front_in,
-    win_in, probs_in,
-    f_out, i_out, layer_out, dfront_out, db_out, dhid_out, dnorm_out, mbias_out,
-    w_f, w_i, w_o, act, slope, grad, meta, n2, hidden, vec, att, gates, front, win, probs,
-    branch, arrived, dhid, db, dmix, dfront, dsum, datt, dnorm, result, mbias, f_total, i_total,
-    *rest,
+    wf_in, wi_in, wo_in, wa_in, ffn_in, slope_in, xs_in, n2_in, hidden_in, vec_in, att_in, gates_in, front_in,
+    win_in, probs_in, mixed_in, act_in,
+    f_out, i_out, o_out, a_out, m_out, layer_out, grad_out,
+    w_f, w_i, ffn, slope, grad, meta, n2, hidden, vec, att, gates, front, win, probs,
+    branch, arrived, dhid, db, dmix, dfront, dsum, norms,
+    f_total, i_total, o_total, a_total, m_total, *rest,
 ):
     bf16, f32 = jnp.bfloat16, jnp.float32
-    f_bufs, i_bufs = rest[:7], rest[7:14]
-    send, recv, lsem, tsem, esend, erecv, osem = rest[14:]
+    f_bufs, i_bufs, m_bufs = rest[:7], rest[7:14], rest[14:21]
+    o_src, o_cx, o_cy, a_src, a_cx, a_cy = rest[21:27]
+    send, recv, lsem, tsem, esend, erecv, osem, ready, freed = rest[27:]
     d, t = lax.axis_index("doc"), lax.axis_index("tm")
     z, c = t // 2, t % 2
     nb = neighbours(2 * levels)
@@ -1165,7 +1155,7 @@
     rows = batches * local_len
     both = 2 * rows
     wide = HALF_HEADS * PAD
-    ff = act.shape[1]
+    ff = ffn.shape[1]
     far = pl.ds(pl.multiple_of((1 - c) * rows, rows), rows)
     near = pl.ds(pl.multiple_of(c * rows, rows), rows)
 
@@ -1175,43 +1165,91 @@
         return cp
 
     meta_at = pl.ds(pl.multiple_of(2 * width + c * 128, 128), 128)
-    l_act = load(act_in, act, 0)
+    l_ffn = load(ffn_in, ffn, 0)
     l_grad = load(xs_in.at[:, :, pl.ds(width, width)], grad, 1)
     l_wf = load(wf_in, w_f, 2)
     l_slope = load(slope_in, slope, 3)
     l_n2 = load(n2_in, n2, 4)
     l_wi = load(wi_in, w_i, 5)
     l_hid = load(hidden_in, hidden, 6)
-    l_vec = load(vec_in, vec, 7)
-    l_meta = load(xs_in.at[:, :, meta_at], meta, 8)
-    l_att = load(att_in, att, 9)
-    l_gates = load(gates_in, gates, 10)
-    l_wo = load(wo_in, w_o, 11)
-
-    def tiles(i, slot):
-        at = pl.ds(pl.multiple_of(i * local_len, local_len), local_len)
+    l_vec = load(vec_in.at[pl.ds(VEC_ROW, 8)], vec, 7)
+    l_mixed = load(mixed_in, dmix, 8)
+    l_meta = load(xs_in.at[:, :, meta_at], meta, 9)
+    l_att = load(att_in, att, 10)
+    l_gates = load(gates_in, gates, 11)
+    w_o = a_src.at[:, :, :, pl.ds(0, W_O)]
+    l_wo = load(wo_in, w_o, 12)
+
+    def tiles(i):
+        at = pl.ds(i * local_len, local_len)
         return [
-            pltpu.make_async_copy(win_in.at[i], win.at[slot], tsem.at[0, slot]),
-            pltpu.make_async_copy(probs_in.at[i], probs.at[slot], tsem.at[1, slot]),
-            pltpu.make_async_copy(front_in.at[at], front.at[slot], tsem.at[2, slot]),
+            pltpu.make_async_copy(win_in.at[i], win.at[i % 2], tsem.at[0, i % 2]),
+            pltpu.make_async_copy(probs_in.at[i], probs.at[i % 2], tsem.at[1, i % 2]),
+            pltpu.make_async_copy(front_in.at[at, pl.ds(0, MISC)], front.at[i % 2], tsem.at[2, i % 2]),
         ]
 
-    for cp in tiles(0, 0):
+    for cp in tiles(0):
         cp.start()
     enter(nb, z, levels)
-    sf = Scatter(f_bufs[0], f_bufs[1:], (send.at[0], recv.at[0]), nb, d, z, levels)
-    si = Scatter(i_bufs[0], i_bufs[1:], (send.at[1], recv.at[1]), nb, d, z, levels)
-
-    l_act.wait()
+
+    names = ("cx", "cy", "rx", "ry", "up", "down")
+
+    def plain(bufs):
+        return lambda name, j: bufs[1 + names.index(name)].at[j]
+
+    block_rows = shard * SIDE
+
+    def within(held, cx, cy, cols):
+        def view(name, j):
+            if name in ("cx", "cy"):
+                return (cx if name == "cx" else cy).at[j]
+            ref, base = held[name]
+            return ref.at[pl.ds(base + j * block_rows, block_rows), pl.ds(0, cols)]
+
+        return view
+
+    span = levels * block_rows
+    o_view = within(dict(rx=(ffn, 0), ry=(ffn, span), up=(slope, 0), down=(slope, span)), o_cx, o_cy, W_O)
+    a_view = within(dict(rx=(w_i, 0), ry=(w_i, span), up=(w_i, 2 * span), down=(w_i, 3 * span)), a_cx, a_cy, MISC)
+    sums = [
+        Scatter(src, view, (send.at[i], recv.at[i]), nb, d, z, levels, total)
+        for i, (src, view, total) in enumerate((
+            (f_bufs[0], plain(f_bufs), f_total), (i_bufs[0], plain(i_bufs), i_total),
+            (o_src, o_view, o_total), (a_src, a_view, a_total), (m_bufs[0], plain(m_bufs), m_total)))
+    ]
+    sf, si, so, sa, sm = sums
+    order = []
+    for k in range((levels + 1) // 2):
+        order += [levels - 1 - k, k] if levels - 1 - k != k else [k]
+    units = [[(s, j)] for s in (sf, si, so, sa) for j in order]
+    units[-1] = units[-1] + [(sm, j) for j in order]
+    line = Pipeline(units, levels, 2)
+
+    def exchange(src, dst, index):
+        return pltpu.make_async_remote_copy(
+            src_ref=src, dst_ref=dst, send_sem=esend.at[index], recv_sem=erecv.at[index],
+            device_id=nb["c"], device_id_type=MESH)
+
+    def weight_grad(dst, left, right, chunk, total, column):
+        at = pl.ds(pl.multiple_of(column * span, span), span)
+
+        def body(i, carry):
+            cols = pl.ds(pl.multiple_of(i * chunk, chunk), chunk)
+            got = dot_f32(left[:, at], right[:, cols], TN).astype(bf16)
+            dst[column, :, :, cols] = got.reshape(levels, block_rows, chunk)
+            return carry
+
+        lax.fori_loop(0, total // chunk, body, 0)
+
+    l_ffn.wait()
     l_grad.wait()
     g_all = grad.reshape(both, width)
     f_rows = f_bufs[0].shape[2]
-    span = levels * f_rows
-    for place, column in enumerate(sf.columns):
-        at = pl.ds(pl.multiple_of(column * span, span), span)
-        got = dot_f32(act[:, at], g_all[...], TN).astype(bf16)
-        f_bufs[0][column] = got.reshape(levels, f_rows, width)
-        sf.begin(place)
+    f_span = levels * f_rows
+    for column in (3 - d, sf.by_x, sf.by_y, d):
+        at = pl.ds(pl.multiple_of(column * f_span, f_span), f_span)
+        f_bufs[0][column] = dot_f32(ffn[:, at], g_all[...], TN).astype(bf16).reshape(levels, f_rows, width)
+    line.begin()
 
     l_wf.wait()
     l_slope.wait()
@@ -1223,45 +1261,33 @@
 
     lax.fori_loop(0, ff // 256, back, 0)
     l_n2.wait()
-    i_rows = i_bufs[0].shape[2]
-    span = levels * i_rows
-    for place, column in enumerate(si.columns):
-        at = pl.ds(pl.multiple_of(column * span, span), span)
-
-        def weights(i, carry):
-            cols = pl.ds(pl.multiple_of(i * 512, 512), 512)
-            got = dot_f32(n2[:, at], slope[:, cols], TN).astype(bf16)
-            i_bufs[0][column, :, :, cols] = got.reshape(levels, i_rows, 512)
-            return carry
-
-        lax.fori_loop(0, ff // 512, weights, 0)
-        si.begin(place)
-
-    def exchange(src, dst, index):
-        return pltpu.make_async_remote_copy(
-            src_ref=src, dst_ref=dst, send_sem=esend.at[index], recv_sem=erecv.at[index],
-            device_id=nb["c"], device_id_type=MESH)
+    for column in range(4):
+        weight_grad(i_bufs[0], n2, slope, 512, ff, column)
+    line.step()
 
     l_wi.wait()
 
-    def input_side(at):
-        def body(i, carry):
-            cols = pl.ds(pl.multiple_of(i * 256, 256), 256)
-            branch[at, cols] = dot_f32(slope[at], w_i[cols], NT)
-            return carry
-
-        lax.fori_loop(0, width // 256, body, 0)
-
-    input_side(far)
+    def times(src, weights, dims):
+        def run(at):
+            def body(i, carry):
+                cols = pl.ds(pl.multiple_of(i * 256, 256), 256)
+                branch[at, cols] = dot_f32(src[at], weights(cols), dims)
+                return carry
+
+            lax.fori_loop(0, width // 256, body, 0)
+
+        return run
+
+    through_in = times(slope, lambda cols: w_i[cols], NT)
+    through_in(far)
     give = exchange(branch.at[far], arrived, 0)
     give.start()
-    input_side(near)
-    for j in sf.order:
-        sf.turn(j)
+    through_in(near)
+    line.step()
     l_hid.wait()
     l_vec.wait()
     give.wait()
-    dnorm[...] = jnp.zeros_like(dnorm)
+    norms[...] = jnp.zeros_like(norms)
     step = 64
 
     def second(i, carry):
@@ -1269,9 +1295,9 @@
         total_at = pl.ds(pl.multiple_of(c * rows + i * step, step), step)
         normed, inverse = norm_rows(hidden[at])
         up = branch[total_at] + arrived[at]
-        dnorm[0:1] += jnp.sum(up * normed, axis=0, keepdims=True)
-        dnorm[1:2] += jnp.sum(up, axis=0, keepdims=True)
-        got = norm_rows_backward(up, normed, inverse, vec[COL_NORM + 2 : COL_NORM + 3])
+        norms[COL_NORM + 2 : COL_NORM + 3] += jnp.sum(up * normed, axis=0, keepdims=True)
+        norms[COL_NORM + 3 : COL_NORM + 4] += jnp.sum(up, axis=0, keepdims=True)
+        got = norm_rows_backward(up, normed, inverse, vec[VEC_GAIN + 2 : VEC_GAIN + 3])
         got = got + grad[c, at].astype(f32)
         dhid[at] = got
         db[total_at] = got.astype(bf16)
@@ -1280,24 +1306,37 @@
     lax.fori_loop(0, rows // step, second, 0)
     pair = exchange(db.at[near], db.at[near], 1)
     pair.start()
-
-    def output_side(at):
-        def body(i, carry):
-            cols = pl.ds(pl.multiple_of(i * 256, 256), 256)
-            branch[at, cols] = dot_f32(act[at], w_f[:, cols])
-            return carry
-
-        lax.fori_loop(0, width // 256, body, 0)
-
-    output_side(far)
+    l_act = load(act_in, grad, 13)
+
+    through_out = times(ffn, lambda cols: w_f[:, cols], (((1,), (0,)), ((), ())))
+    through_out(far)
     pair.wait()
     last = exchange(branch.at[far], arrived, 2)
     last.start()
+    line.step()
+    through_out(near)
+
+    for name in ("x", "y"):
+        pl.semaphore_signal(ready, inc=1, device_id=nb[name], device_id_type=MESH)
+    for name, there in (("up", z < levels - 1), ("down", z > 0)):
+
+        @pl.when(there)
+        def _():
+            pl.semaphore_signal(ready, inc=1, device_id=nb[name], device_id_type=MESH)
+
+    l_wa = [
+        load(wa_in.at[:, pl.ds(0, width)], w_f.at[pl.ds(0, width)], 14),
+        load(wa_in.at[:, pl.ds(width, W_A - width)], w_f.at[pl.ds(width, width), pl.ds(0, W_A - width)], 15),
+    ]
+    l_mixed.wait()
+    for column in range(4):
+        weight_grad(o_src, db, dmix, 640, W_O, column)
+    line.step()
     l_wo.wait()
 
     def mix(i, carry):
         cols = pl.ds(pl.multiple_of(i * wide, wide), wide)
-        dmix[:, cols] = dot_f32(db[...], w_o[:, cols]).astype(bf16)
+        dmix[:, cols] = dot_f32(db[...], a_src[:, :, :, cols].reshape(width, wide)).astype(bf16)
         return carry
 
     lax.fori_loop(0, EXPERTS, mix, 0)
@@ -1307,21 +1346,17 @@
     dsum[...] = jnp.zeros_like(dsum)
     lanes = lax.broadcasted_iota(jnp.int32, (local_len, W_MISC), 1)
 
-    def attend(i, carry):
-        slot = lax.rem(i, 2)
-
-        @pl.when(i + 1 < 2 * batches)
-        def _():
-            for cp in tiles(i + 1, 1 - slot):
+    def attend(i):
+        slot = i % 2
+        if i + 1 < 2 * batches:
+            for cp in tiles(i + 1):
                 cp.start()
-
-        for cp in tiles(i, slot):
+        for cp in tiles(i):
             cp.wait()
-        at = pl.ds(pl.multiple_of(i * local_len, local_len), local_len)
+        at = pl.ds(i * local_len, local_len)
         block, batch = i // batches, i % batches
-        rows_at = pl.ds(pl.multiple_of(batch * local_len, local_len), local_len)
         gate = gates[at]
-        picks = meta[block, rows_at].astype(f32)
+        picks = meta[block, pl.ds(batch * local_len, local_len)].astype(f32)
         gated = gate * picks
         d_gates = jnp.zeros((local_len, W_MISC), f32)
         for h in range(HALF_HEADS):
@@ -1356,23 +1391,13 @@
                 dfront[at, col : col + PAD] = (gated[:, lane : lane + 1] * d_v).astype(bf16)
         d_logits = jnp.where(lanes < N_ROUTE, d_gates * picks * gate * (1.0 - gate), 0.0)
         dfront[at, MISC:W_A] = d_logits.astype(bf16)
-        return carry
-
-    lax.fori_loop(0, batches, attend, 0)
-    for j in sf.order:
-        sf.column(j)
-    for j in sf.order:
-        sf.line(j)
-    for j in si.order:
-        si.turn(j)
-    lax.fori_loop(batches, 2 * batches, attend, 0)
-    outs = [
-        pltpu.make_async_copy(src, dst, osem.at[i])
-        for i, (src, dst) in enumerate(((dfront, dfront_out), (db, db_out), (dhid, dhid_out), (dnorm, dnorm_out)))
-    ]
-    for cp in outs:
-        cp.start()
-    output_side(near)
+
+    for i in range(2 * batches):
+        attend(i)
+        if line.now + line.ahead == 2 * levels:
+            ends = jnp.where(z < levels - 1, 1, 0) + jnp.where(z > 0, 1, 0)
+            pl.semaphore_wait(ready, 2 + ends)
+        line.step()
     last.wait()
 
     def final(i, carry):
@@ -1382,19 +1407,39 @@
         position = lax.broadcasted_iota(jnp.int32, (step, 1), 0) + (i * step) % local_len
         keep = position.astype(f32) < tail[:, 41:42]
         total = hidden[at] + branch[total_at] + arrived[at]
-        result[at] = jnp.where(keep, total, 0.0).astype(bf16)
+        db[total_at] = jnp.where(keep, total, 0.0).astype(bf16)
         return carry
 
     lax.fori_loop(0, rows // step, final, 0)
-    out_r = pltpu.make_async_copy(result, layer_out, osem.at[4])
-    out_r.start()
-    for j in si.order:
-        si.column(j)
-    for j in si.order:
-        si.line(j)
-    sf.total(f_total)
-    out_f = pltpu.make_async_copy(f_total, f_out, osem.at[5])
-    out_f.start()
+    pl.semaphore_signal(freed, inc=1, device_id=nb["c"], device_id_type=MESH)
+    outs = [pltpu.make_async_copy(db.at[near], layer_out, osem.at[0])]
+    outs[0].start()
+
+    l_act.wait()
+    one_all = grad.reshape(both, width)
+    for column in range(4):
+        weight_grad(a_src, one_all, dfront, 896, MISC, column)
+    line.step()
+    for cp in l_wa:
+        cp.wait()
+
+    def through_front(at):
+        def body(i, carry):
+            cols = pl.ds(pl.multiple_of(i * 256, 256), 256)
+            below = pl.ds(pl.multiple_of(width + i * 256, 256), 256)
+            branch[at, cols] = (
+                dot_f32(dfront[at, :width], w_f[cols], NT)
+                + dot_f32(dfront[at, width:], w_f[below, : W_A - width], NT))
+            return carry
+
+        lax.fori_loop(0, width // 256, body, 0)
+
+    through_front(far)
+    hand = exchange(branch.at[far], arrived, 3)
+    pl.semaphore_wait(freed, 1)
+    hand.start()
+    through_front(near)
+    line.step()
 
     spread = MEM + 2 * local_len
     ids = lax.broadcasted_iota(jnp.int32, (local_len, 1), 0)
@@ -1416,215 +1461,87 @@
     distance = MEM + local_len - 1 - lax.broadcasted_iota(jnp.int32, (1, spread), 1)
     bucket = bucket_index(distance)
     wanted = (bucket // per_device) * shard + bucket % per_device
-
-    def by_bucket(i, carry):
-        at = pl.ds(pl.multiple_of(i * 128, 128), 128)
-        row_ids = lax.broadcasted_iota(jnp.int32, (128, spread), 0) + i * 128
+    hand.wait()
+
+    def first(i, carry):
+        at = pl.ds(pl.multiple_of(i * step, step), step)
+        total_at = pl.ds(pl.multiple_of(c * rows + i * step, step), step)
+        normed, inverse = norm_rows(n2[at].astype(f32))
+        up = branch[total_at] + arrived[at]
+        norms[COL_NORM : COL_NORM + 1] += jnp.sum(up * normed, axis=0, keepdims=True)
+        norms[COL_NORM + 1 : COL_NORM + 2] += jnp.sum(up, axis=0, keepdims=True)
+        dhid[at] += norm_rows_backward(up, normed, inverse, vec[VEC_GAIN : VEC_GAIN + 1])
+        return carry
+
+    l_x = load(xs_in.at[c, :, pl.ds(0, width)], n2.at[pl.ds(0, rows)], 16)
+    l_x.wait()
+    lax.fori_loop(0, rows // step, first, 0)
+    outs.append(pltpu.make_async_copy(dhid, grad_out, osem.at[1]))
+    outs[1].start()
+    line.step()
+    columns = norms[...].T
+
+    for column in range(4):
+        at = pl.ds(column * span, span)
+        row_ids = lax.broadcasted_iota(jnp.int32, (span, spread), 0) + column * span
         one_hot = jnp.where(row_ids == wanted, 1.0, 0.0).astype(bf16)
-        mbias[at] = dot_f32(one_hot, high, NT) + dot_f32(one_hot, low, NT)
-        return carry
-
-    lax.fori_loop(0, mbias.shape[0] // 128, by_bucket, 0)
-    out_m = pltpu.make_async_copy(mbias, mbias_out, osem.at[6])
-    out_m.start()
-    si.total(i_total)
+        misc = dot_f32(one_hot, high, NT) + dot_f32(one_hot, low, NT)
+        misc = misc + dot_f32(one_all[:, at], dfront[:, MISC:W_A], TN) + columns[column * span : (column + 1) * span]
+        m_bufs[0][column] = misc.astype(bf16).reshape(levels, block_rows, W_MISC)
+    line.finish()
+    outs.append(pltpu.make_async_copy(f_total, f_out, osem.at[2]))
+    outs[2].start()
     mine, other = [pl.ds(pl.multiple_of(k * shard, 16), shard) for k in (c, 1 - c)]
-    keep = pltpu.make_async_copy(i_total.at[mine], i_out.at[c], osem.at[7])
-    keep.start()
-    swap_i = exchange(i_total.at[other], i_out.at[c], 3)
-    swap_i.start()
-    sf.drain()
-    si.drain()
-    for cp in outs + [out_r, out_f, out_m, keep, swap_i]:
+    for i, (total, out) in enumerate(((i_total, i_out), (o_total, o_out), (a_total, a_out), (m_total, m_out))):
+        outs.append(pltpu.make_async_copy(total.at[mine], out.at[c], osem.at[3 + i]))
+        outs[-1].start()
+        outs.append(exchange(total.at[other], out.at[c], 4 + i))
+        outs[-1].start()
+    for s in sums:
+        s.drain()
+    for cp in outs:
         cp.wait()
 
 
-def kernel_call(body, ins, outs, scratch, sems, collective):
-    hbm = pl.BlockSpec(memory_space=pl.ANY)
-    return pl.pallas_call(
-        body,
-        out_shape=[jax.ShapeDtypeStruct(s, k) for s, k in outs],
-        in_specs=[hbm] * len(ins),
-        out_specs=[hbm] * len(outs),
-        scratch_shapes=[pltpu.VMEM(s, k) for s, k in scratch] + [pltpu.SemaphoreType.DMA(s) for s in sems],
-        compiler_params=pltpu.CompilerParams(
-            collective_id=collective, has_side_effects=True, vmem_limit_bytes=VMEM_BYTES),
-    )(*ins)
-
-
-def middle(levels, batches, local_len, per_device, shard, ins):
+def backward(levels, batches, local_len, per_device, shard, ins):
     bf16, f32 = jnp.bfloat16, jnp.float32
-    w_f, w_i, w_o, act, slope, xs, n2, hidden, vec, att, gates, front, win, probs = ins
+    (w_f, w_i, w_o, w_a, ffn, slope, xs, n2, hidden, vec, att, gates, front, win, probs, mixed, act) = ins
     ff, width = w_f.shape
     rows = batches * local_len
     both = 2 * rows
     f_rows = ff // (4 * levels)
-    i_rows = width // (4 * levels)
-    outs = [
-        ((f_rows, width), f32), ((SIDE, shard, ff), f32), ((rows, width), bf16), ((both, W_A), bf16),
-        ((both, width), bf16), ((rows, width), f32), ((8, width), f32), ((width, W_MISC), f32),
-    ]
-    scratch = [(v.shape, v.dtype) for v in (w_f, w_i, w_o, act, slope)]
+    b_rows = width // (4 * levels)
+    outs = [((f_rows, width), f32)] + [((SIDE, shard, w), f32) for w in (ff, W_O, MISC, W_MISC)]
+    outs += [((rows, width), bf16), ((rows, width), f32)]
+    scratch = [(v.shape, v.dtype) for v in (w_f, w_i, ffn, slope)]
     scratch += [((2, rows, width), bf16), ((2, rows, 128), bf16)]
-    scratch += [(v.shape, v.dtype) for v in (n2, hidden, vec, att, gates)]
-    scratch += [((2, local_len, W_A), f32), ((2,) + win.shape[1:], bf16), ((2,) + probs.shape[1:], f32)]
+    scratch += [(n2.shape, bf16), (hidden.shape, f32), ((8, width), f32), (att.shape, bf16), (gates.shape, f32)]
+    scratch += [((2, local_len, MISC), f32), ((2,) + win.shape[1:], bf16), ((2,) + probs.shape[1:], f32)]
     scratch += [
         ((both, width), f32), ((rows, width), f32), ((rows, width), f32), ((both, width), bf16),
         ((both, W_O), bf16), ((both, W_A), bf16), ((HALF_HEADS, local_len, MEM + local_len), f32),
-        ((8, 128), f32), ((8, width), f32), ((rows, width), bf16), ((width, W_MISC), f32),
-        ((f_rows, width), f32), ((i_rows, ff), f32),
+        ((W_MISC, width), f32), ((f_rows, width), f32),
     ]
-    scratch += scatter_scratch(levels, [(f_rows, width), (i_rows, ff)])
-    sems = [(2, 8 * levels), (2, 8 * levels), (12,), (3, 2), (4,), (4,), (8,)]
-    body = functools.partial(middle_kernel, levels, batches, local_len, per_device, shard)
-    return kernel_call(body, ins, outs, scratch, sems, 2)
-
-
-def last_kernel(
-    levels, batches, local_len, shard,
-    db_in, mixed_in, act_in, dfront_in, wa_in, mbias_in, dnorm_in, dhid_in, xs_in, vec_in,
-    a_out, o_out, m_out, grad_out,
-    db, mixed, act, dfront, w_a, mbias, dnorm, dhid, x_own, vec, branch, arrived, result, norms,
-    a_total, o_total, m_total, *rest,
-):
-    bf16, f32 = jnp.bfloat16, jnp.float32
-    a_bufs, o_bufs, m_bufs = rest[:7], rest[7:14], rest[14:21]
-    send, recv, lsem, esend, erecv, osem = rest[21:]
-    d, t = lax.axis_index("doc"), lax.axis_index("tm")
-    z, c = t // 2, t % 2
-    nb = neighbours(2 * levels)
-    width = db.shape[1]
-    rows = batches * local_len
-    far = pl.ds(pl.multiple_of((1 - c) * rows, rows), rows)
-    near = pl.ds(pl.multiple_of(c * rows, rows), rows)
-    pairs = (
-        (db_in, db), (mixed_in, mixed), (act_in, act), (dfront_in, dfront), (wa_in, w_a), (mbias_in, mbias),
-        (dnorm_in, dnorm), (dhid_in, dhid), (xs_in.at[c, :, pl.ds(0, width)], x_own), (vec_in, vec))
-    loads = [pltpu.make_async_copy(src, dst, lsem.at[i]) for i, (src, dst) in enumerate(pairs)]
-    for cp in loads:
-        cp.start()
-    enter(nb, z, levels)
-    so, sa, sm = [
-        Scatter(bufs[0], bufs[1:], (send.at[i], recv.at[i]), nb, d, z, levels)
-        for i, bufs in enumerate((o_bufs, a_bufs, m_bufs))
-    ]
-    block_rows = o_bufs[0].shape[2]
-    span = levels * block_rows
-
-    def weight_grad(scatter, left, right, chunk):
-        total = right.shape[1] if scatter is so else MISC
-        for place, column in enumerate(scatter.columns):
-            at = pl.ds(pl.multiple_of(column * span, span), span)
-
-            def body(i, carry):
-                cols = pl.ds(pl.multiple_of(i * chunk, chunk), chunk)
-                got = dot_f32(left[:, at], right[:, cols], TN).astype(bf16)
-                scatter.src[column, :, :, cols] = got.reshape(levels, block_rows, chunk)
-                return carry
-
-            lax.fori_loop(0, total // chunk, body, 0)
-            scatter.begin(place)
-
-    loads[0].wait()
-    loads[1].wait()
-    weight_grad(so, db, mixed, 640)
-    loads[2].wait()
-    loads[3].wait()
-    weight_grad(sa, act, dfront, 896)
-    for j in so.order:
-        so.turn(j)
-    loads[4].wait()
-
-    def exchange(src, dst, index):
-        return pltpu.make_async_remote_copy(
-            src_ref=src, dst_ref=dst, send_sem=esend.at[index], recv_sem=erecv.at[index],
-            device_id=nb["c"], device_id_type=MESH)
-
-    def input_side(at):
-        def body(i, carry):
-            cols = pl.ds(pl.multiple_of(i * 256, 256), 256)
-            branch[at, cols] = dot_f32(dfront[at], w_a[cols], NT)
-            return carry
-
-        lax.fori_loop(0, width // 256, body, 0)
-
-    input_side(far)
-    give = exchange(branch.at[far], arrived, 0)
-    give.start()
-    input_side(near)
-    for cp in loads[5:]:
-        cp.wait()
-    give.wait()
-    norms[...] = jnp.zeros_like(norms)
-    norms[COL_NORM + 2 : COL_NORM + 4] = dnorm[0:2]
-    step = 64
-
-    def first(i, carry):
-        at = pl.ds(pl.multiple_of(i * step, step), step)
-        total_at = pl.ds(pl.multiple_of(c * rows + i * step, step), step)
-        normed, inverse = norm_rows(x_own[at].astype(f32))
-        up = branch[total_at] + arrived[at]
-        norms[COL_NORM : COL_NORM + 1] += jnp.sum(up * normed, axis=0, keepdims=True)
-        norms[COL_NORM + 1 : COL_NORM + 2] += jnp.sum(up, axis=0, keepdims=True)
-        got = norm_rows_backward(up, normed, inverse, vec[COL_NORM : COL_NORM + 1])
-        result[at] = dhid[at] + got
-        return carry
-
-    lax.fori_loop(0, rows // step, first, 0)
-    out_g = pltpu.make_async_copy(result, grad_out, osem.at[0])
-    out_g.start()
-    misc = dot_f32(act[...], dfront[:, MISC:W_A], TN) + mbias[...] + norms[...].T
-    misc = misc.astype(bf16).reshape(4, levels, block_rows, W_MISC)
-    for column in range(4):
-        m_bufs[0][column] = misc[column]
-    for place in range(3):
-        sm.begin(place)
-    for j in sa.order:
-        sa.turn(j)
-    for j in so.order:
-        so.column(j)
-    for j in so.order:
-        so.line(j)
-    for j in sm.order:
-        sm.turn(j)
-    for j in sa.order:
-        sa.column(j)
-    for j in sa.order:
-        sa.line(j)
-    for j in sm.order:
-        sm.column(j)
-    for j in sm.order:
-        sm.line(j)
-    mine, other = [pl.ds(pl.multiple_of(k * shard, 16), shard) for k in (c, 1 - c)]
-    ends = []
-    for i, (scatter, total, out) in enumerate(((so, o_total, o_out), (sa, a_total, a_out), (sm, m_total, m_out))):
-        scatter.total(total)
-        keep = pltpu.make_async_copy(total.at[mine], out.at[c], osem.at[1 + i])
-        keep.start()
-        move = exchange(total.at[other], out.at[c], 1 + i)
-        move.start()
-        ends += [keep, move]
-    for scatter in (so, sa, sm):
-        scatter.drain()
-    for cp in ends + [out_g]:
-        cp.wait()
-
-
-def last(levels, batches, local_len, shard, ins):
-    bf16, f32 = jnp.bfloat16, jnp.float32
-    db, mixed, act, dfront, w_a, mbias, dnorm, dhid, xs, vec = ins
-    both, width = db.shape
-    rows = both // 2
-    block_rows = width // (4 * levels)
-    outs = [((SIDE, shard, w), f32) for w in (MISC, W_O, W_MISC)] + [((rows, width), f32)]
-    scratch = [(v.shape, v.dtype) for v in (db, mixed, act, dfront, w_a, mbias, dnorm, dhid)]
-    scratch += [((rows, width), bf16), (vec.shape, f32), ((both, width), f32), ((rows, width), f32)]
-    scratch += [((rows, width), f32), ((W_MISC, width), f32)]
-    scratch += [((block_rows, w), f32) for w in (MISC, W_O, W_MISC)]
-    scratch += scatter_scratch(levels, [(block_rows, w) for w in (MISC, W_O, W_MISC)])
-    sems = [(3, 8 * levels), (3, 8 * levels), (10,), (4,), (4,), (4,)]
-    body = functools.partial(last_kernel, levels, batches, local_len, shard)
-    return kernel_call(body, ins, outs, scratch, sems, 3)
+    scratch += [((b_rows, w), f32) for w in (ff, W_O, MISC, W_MISC)]
+    for r, w in ((f_rows, width), (b_rows, ff), (b_rows, W_MISC)):
+        scratch.append(((4, levels, r, w), bf16))
+        scratch += [((levels, k, w), bf16) for k in (r // 2, r // 2, r, r, r, r)]
+    for w in (W_O, MISC):
+        scratch.append(((4, levels, b_rows, w), bf16))
+        scratch += [((levels, b_rows // 2, w), bf16)] * 2
+    sems = [(5, 8 * levels), (5, 8 * levels), (17,), (3, 2), (8,), (8,), (8,)]
+    hbm = pl.BlockSpec(memory_space=pl.ANY)
+    return pl.pallas_call(
+        functools.partial(backward_kernel, levels, batches, local_len, per_device, shard),
+        out_shape=[jax.ShapeDtypeStruct(s, k) for s, k in outs],
+        in_specs=[hbm] * len(ins),
+        out_specs=[hbm] * len(outs),
+        scratch_shapes=[pltpu.VMEM(s, k) for s, k in scratch]
+        + [pltpu.SemaphoreType.DMA(s) for s in sems]
+        + [pltpu.SemaphoreType.REGULAR] * 2,
+        compiler_params=pltpu.CompilerParams(
+            collective_id=2, has_side_effects=True, vmem_limit_bytes=VMEM_BYTES),
+    )(*ins)
 
 
 def split_heads(a, lead):
@@ -1693,15 +1610,12 @@
     (a_all, o_all, i_all, f_all, xs, act_one, front, gates, win, probs, attended, mixed, hidden, n2, vec, act,
      slope) = forward(levels, batches, local_len, buckets, (a_pack, a_o, i_pack, ffn_out, x_pack, g_pack))
     w_a = a_all.reshape(width, W_A)
-    w_o = o_all.reshape(width, W_O)
     w_i = i_all.reshape(width, -1)
     w_f = f_all.reshape(-1, width)
-    out_share, i_sides, layer_out, d_front, d_branch, d_hidden, d_norm, d_bias = middle(
+    out_share, i_sides, o_sides, a_sides, misc, layer_out, input_grad = backward(
         levels, batches, local_len, buckets, shard,
-        (w_f, w_i, w_o, act, slope, xs, n2, hidden, vec, attended, gates, front, win, probs))
-    a_sides, o_sides, misc, input_grad = last(
-        levels, batches, local_len, shard,
-        (d_branch, mixed, act_one, d_front, w_a, d_bias, d_norm, d_hidden, xs, vec))
+        (w_f, w_i, o_all, w_a, act, slope, xs, n2, hidden, vec, attended, gates, front, win, probs, mixed,
+         act_one.reshape(2, rows, width)))
     layer_out = layer_out.reshape(tokens.shape)
     input_grad = input_grad.reshape(tokens.shape)
     qk_share = join_heads(a_sides[:, :, :W_QK], 2)

time: 409 us -> 365 us (0.89)
  Pallas kernels: 377 us -> 333 us
    pallas_call x2 -> x1, Pallas kernels: 206 us -> 162 us  [backward(): pl.pallas_call(functools.partial(backward_kernel, levels, batches, local_...]
where the time goes in v4:
time: 365 us; the launch traced here: 362 us
  Pallas kernels  333 us (91%)
  local copies, waits for them, and re-layouts  22 us (6%)
  other arithmetic  5.85 us (2%)
    pallas_call x1, Pallas kernels, forward(): pl.pallas_call(functools.partial(forward_kernel, levels, batches, local_l...  171 us
    pallas_call x1, Pallas kernels, backward(): pl.pallas_call(functools.partial(backward_kernel, levels, batches, local_...  162 us

profile of v4, /device:TPU:0, one launch (start us, length us, event | category | flops | bytes accessed | tf_op | source)
XLA Modules:
  0.0 362.3 jit_solution(17473489471635054069)
XLA Ops:
  0.7 0.7 convert_bitcast_fusion
  1.5 0.7 bitcast_convert_fusion
  2.3 0.7 pad_maximum_fusion.4
  3.0 0.7 fusion.20
  3.7 0.8 copy.160
  4.6 0.7 copy.164
  5.4 0.7 copy.167
  6.2 0.8 copy.157
  7.6 0.9 reshape.187
  8.7 1.1 reshape.189
  10.1 0.7 fusion.7.a_in
  11.2 0.7 reshape.195.o_in
  12.2 0.8 reshape.197.i_in
  13.2 1.1 fusion.4.x_in
  14.3 171.0 %shard_map.273 = (bf16[4,4,64,1920]{3,2,1,0:T(8,128)(2,1)}, bf16[4,4,64,1280]{3,2,1,0:T(8,128)(2,1)}, bf16[4,4,64,2048]{3,2,1,0:T(8,128)(2,1)}, bf16[4,4,128,102...) custom-call(bf16[2,32,1920]{2,1,0:T(8,128)(2,1)} %fusion.7.a_in, ...), custom_call_target="tpu_custom_call" | custom-call | tf_op jit(solution)/shard_map/pallas_call | solution.py:976
  185.3 162.3 %shard_map.274 = (f32[128,1024]{1,0:T(8,128)}, f32[2,32,2048]{2,1,0:T(8,128)}, f32[2,32,1280]{2,1,0:T(8,128)}, f32[2,32,1792]{2,1,0:T(8,128)}, f32[2,32,128]{2,1...) custom-call(bf16[2048,1024]{1,0:T(8,128)(2,1)} %bitcast.107, bf16[1024,2048]{1,0:T(8,128)(2,1)} %bitcast.106, ...), custom_call_target="tpu_custom_call" | custom-call | tf_op jit(solution)/shard_map/pallas_call | solution.py:1534
  347.6 0.8 slice_bitcast_fusion.3
  348.4 0.7 copy.178
  349.0 0.8 slice_add_fusion
  349.9 0.5 slice_bitcast_fusion.4
  350.5 0.9 copy.174
  351.4 0.7 copy.182
  352.1 0.9 slice.63
  353.0 1.0 slice.66
  354.3 1.0 reshape.213
  355.5 0.8 reshape.209
  356.7 1.0 reshape.215
  357.9 0.4 copy.179
  358.3 1.2 reshape.218
  359.5 0.8 copy.211
  360.3 1.0 copy.212
  361.3 0.8 copy.213
  (66 shorter events, 3.3 us)
Async XLA Ops:
  0.6 11.3 %copy-start.7 = (bf16[32,4096]{1,0:T(8,128)(2,1)S(1)}, bf16[32,4096]{1,0:T(8,128)(2,1)}, u32[]{:S(2)}) copy-start(bf16[32,4096]{1,0:T(8,128)(2,1)} %param.34) | copy-start | bytes 786436
  0.7 10.2 %copy-start.8 = (bf16[2240,32]{0,1:T(8,128)(2,1)S(1)}, bf16[2240,32]{0,1:T(8,128)(2,1)}, u32[]{:S(2)}) copy-start(bf16[2240,32]{0,1:T(8,128)(2,1)} %param.30) | copy-start | bytes 430084
  7.3 5.7 %copy-start.1 = (bf16[2,1,128,1024]{3,2,1,0:T(8,128)(2,1)S(1)}, bf16[2,1,128,1024]{3,2,1,0:T(8,128)(2,1)}, u32[]{:S(2)}) copy-start(bf16[2,1,128,1024]{3,2,1,0:T(8,128)(2,1)} %param.19) | copy-start | bytes 1572868
  9.8 3.4 copy-start.5
  350.5 5.9 %copy-start.6 = (f32[2,32,1280]{2,1,0:T(8,128)S(1)}, f32[2,32,1280]{2,1,0:T(8,128)}, u32[]{:S(2)}) copy-start(f32[2,32,1280]{2,1,0:T(8,128)} %get-tuple-element.58) | copy-start | bytes 983044
  354.2 3.5 copy-start.4
  356.7 2.8 copy-start.3
  357.8 2.5 copy-start
  358.3 3.0 copy-start.2

commit v5 on v4

--- a/solution.py
+++ b/solution.py
@@ -559,24 +559,25 @@
 
 def forward_kernel(
     levels, batches, local_len, per_device,
-    a_in, o_in, i_in, f_in, x_in, g_in,
+    qk_in, value_in, router_in, norm_in, bias_in, branch_in, up_in, f_in, token_in, cot_in, vr_in, or_in, start_in,
+    count_in, g_in,
     a_out, o_out, i_out, f_all, xs_out, act_out, front_out, gates_out, win_out, probs_out, att_out,
     mixed_out, hidden_out, n2_out, vec_out, ffn_out, slope_out,
-    a_all, o_all, i_all, xs, graw, win, cr, sel, unit, act, front, gates, vec, bias, probs, att, mixed,
+    a_all, o_all, i_all, xs, graw, win, rbuf, sel, unit, act, front, gates, vec, bias, probs, att, mixed,
     arrived, hidden, n2, ffn, slope,
-    send, recv, csend, crecv, lsem, gsend, grecv, msend, mrecv, esend, erecv, osem, psem,
+    qk_raw, value_raw, router_raw, norm_raw, bias_raw, branch_raw, up_raw, vr_raw, or_raw, start_raw, count_raw, f_raw, a_pack, o_pack, i_pack,
+    send, recv, csend, crecv, lsem, gsend, grecv, esend, erecv, osem, psem,
 ):
     bf16, f32 = jnp.bfloat16, jnp.float32
     d, t = lax.axis_index("doc"), lax.axis_index("tm")
     z, c = t // 2, t % 2
     nb = neighbours(2 * levels)
-    shard = a_in.shape[1]
+    shard = qk_in.shape[0]
     width = f_in.shape[1]
     rows = batches * local_len
     both = 2 * rows
     wide = HALF_HEADS * PAD
     own = pl.ds(pl.multiple_of(c * shard, 16), shard)
-    reach = cr.shape[0]
 
     def local(src, dst, index):
         cp = pltpu.make_async_copy(src, dst, lsem.at[index])
@@ -588,31 +589,82 @@
             src_ref=src, dst_ref=dst, send_sem=csend.at[index], recv_sem=crecv.at[index],
             device_id=nb["c"], device_id_type=MESH)
 
-    loc_a = local(a_in.at[c], a_all.at[d, z, own], 0)
-    loc_x = local(x_in, xs.at[c], 1)
-    loc_g = local(g_in, graw.at[c], 2)
-    loc_o = local(o_in.at[c], o_all.at[d, z, own], 3)
-    loc_i = local(i_in.at[c], i_all.at[d, z, own], 4)
-    loc_f = local(f_in, f_all.at[d, z], 5)
+    raws = [
+        local(src, dst, i)
+        for i, (src, dst) in enumerate((
+            (qk_in, qk_raw), (value_in, value_raw), (router_in, router_raw), (norm_in, norm_raw), (bias_in, bias_raw),
+            (branch_in, branch_raw), (up_in, up_raw), (vr_in, vr_raw), (or_in, or_raw), (start_in, start_raw),
+            (count_in, count_raw)))
+    ]
+    loc_f = local(f_in, f_raw, 11)
+    x_parts = ((token_in, pl.ds(0, width)), (cot_in, pl.ds(width, width)))
+    loc_x = [local(src, xs.at[c, :, cols], 12 + i) for i, (src, cols) in enumerate(x_parts)]
     enter(nb, z, levels)
-    rem_a = sibling(a_in.at[1 - c], a_all.at[d, z, own], 0)
-    rem_x = sibling(x_in, xs.at[c], 1)
-    rem_g = sibling(g_in, graw.at[c], 2)
-    rem_o = sibling(o_in.at[1 - c], o_all.at[d, z, own], 3)
-    rem_i = sibling(i_in.at[1 - c], i_all.at[d, z, own], 4)
-    for cp in (rem_a, rem_x, rem_g, rem_o, rem_i):
+    rem_x = [sibling(src, xs.at[c, :, cols], i) for i, (src, cols) in enumerate(x_parts)]
+    for cp in rem_x:
         cp.start()
     ga, go, gi, gf = [
         Gather(ref, (send.at[i], recv.at[i]), nb, d, z, levels)
         for i, ref in enumerate((a_all, o_all, i_all, f_all))
     ]
+
+    for cp in raws[:5]:
+        cp.wait()
+    a_pack[...] = jnp.zeros_like(a_pack)
+    norm_columns = norm_raw[...].astype(f32).T
+    for side in range(SIDE):
+        for h in range(HALF_HEADS):
+            at = (side * HALF_HEADS + h) * HEAD_DIM
+            for kind in range(2):
+                col, src = (kind * HALF_HEADS + h) * PAD, kind * HEADS * HEAD_DIM + at
+                a_pack[side, :, col : col + HEAD_DIM] = qk_raw[:, src : src + HEAD_DIM]
+            for e in range(EXPERTS):
+                col, src = W_QK + (e * HALF_HEADS + h) * PAD, e * HEADS * HEAD_DIM + at
+                a_pack[side, :, col : col + HEAD_DIM] = value_raw[:, src : src + HEAD_DIM]
+        routes = HALF_HEADS * EXPERTS
+        for kind in range(2):
+            src = (kind * SIDE + side) * routes
+            a_pack[side, :, MISC + kind * routes : MISC + (kind + 1) * routes] = router_raw[:, src : src + routes]
+        a_pack[side, :, MISC + COL_NORM : MISC + COL_NORM + 4] = norm_columns.astype(bf16)
+        heads = bias_raw[side * HALF_HEADS : (side + 1) * HALF_HEADS].astype(f32).T
+        tail = jnp.concatenate([heads, jnp.zeros((shard - per_device, HALF_HEADS), f32)], axis=0)
+        a_pack[side, :, MISC + COL_BIAS : MISC + COL_BIAS + HALF_HEADS] = tail.astype(bf16)
+    loc_a = local(a_pack.at[c], a_all.at[d, z, own], 17)
+    rem_a = sibling(a_pack.at[1 - c], a_all.at[d, z, own], 3)
+    rem_a.start()
+    for cp in raws[7:]:
+        cp.wait()
+    row_ids = lax.broadcasted_iota(jnp.int32, (W_MISC, local_len), 0)
+    for batch in range(batches):
+        flags = [
+            jnp.broadcast_to(raw[:, batch : batch + 1].astype(f32), (W_MISC, local_len)) for raw in (start_raw, count_raw)]
+        for side in range(SIDE):
+            rows_of = jnp.where(row_ids == 40, flags[0], jnp.where(row_ids == 41, flags[1], 0.0))
+            for kind, raw in enumerate((vr_raw, or_raw)):
+                for h in range(HALF_HEADS):
+                    chosen = raw[batch, side * HALF_HEADS + h]
+                    first = (kind * HALF_HEADS + h) * EXPERTS
+                    expert = row_ids - first
+                    hit = expert == chosen[0:1]
+                    for k in range(1, TOPK):
+                        hit = jnp.logical_or(hit, expert == chosen[k : k + 1])
+                    inside = jnp.logical_and(row_ids >= first, row_ids < first + EXPERTS)
+                    rows_of = jnp.where(jnp.logical_and(hit, inside), 1.0, rows_of)
+            cols = pl.ds(2 * width + side * 128, 128)
+            xs[c, pl.ds(batch * local_len, local_len), cols] = rows_of.T.astype(bf16)
+    meta_cols = xs.at[c, :, pl.ds(2 * width, SIDE * 128)]
+    rem_x.append(sibling(meta_cols, meta_cols, 2))
+    rem_x[-1].start()
+    loc_g = local(g_in, graw.at[c], 14)
+    rem_g = sibling(g_in, graw.at[c], 4)
+    rem_g.start()
     loc_a.wait()
     rem_a.wait()
     ga.begin()
     sel[...] = selector(c)
 
-    loc_x.wait()
-    rem_x.wait()
+    for cp in loc_x + rem_x:
+        cp.wait()
     step = 64
 
     def stats(i, carry):
@@ -622,10 +674,36 @@
         centered = values - jnp.mean(values, axis=-1, keepdims=True)
         inverse = lax.rsqrt(jnp.mean(centered * centered, axis=-1, keepdims=True) + EPS)
         unit[pl.ds(pl.multiple_of(i * step, step), step)] = centered * inverse
+        counts = xs[block, at, 2 * width : 2 * width + 128][:, 41:42].astype(f32)
+        position = lax.broadcasted_iota(jnp.int32, (step, 1), 0) + (i * step) % local_len
+        gradient = xs[block, at, width : 2 * width].astype(f32)
+        xs[block, at, width : 2 * width] = jnp.where(position.astype(f32) < counts, gradient, 0.0).astype(bf16)
         return carry
 
     lax.fori_loop(0, both // step, stats, 0)
     ga.line(1)
+    raws[6].wait()
+    for side in range(SIDE):
+        for p in range(4 * levels):
+            src = (p * SIDE + side) * PAD
+            i_pack[side, :, p * PAD : (p + 1) * PAD] = up_raw[:, src : src + PAD]
+    raws[5].wait()
+    o_pack[...] = jnp.zeros_like(o_pack)
+    for side in range(SIDE):
+        for h in range(HALF_HEADS):
+            for e in range(EXPERTS):
+                src = e * HEADS * HEAD_DIM + (side * HALF_HEADS + h) * HEAD_DIM
+                col = (e * HALF_HEADS + h) * PAD
+                o_pack[side, :, col : col + HEAD_DIM] = branch_raw[:, src : src + HEAD_DIM]
+    loc_o = local(o_pack.at[c], o_all.at[d, z, own], 15)
+    rem_o = sibling(o_pack.at[1 - c], o_all.at[d, z, own], 5)
+    loc_i = local(i_pack.at[c], i_all.at[d, z, own], 16)
+    rem_i = sibling(i_pack.at[1 - c], i_all.at[d, z, own], 6)
+    rem_o.start()
+    rem_i.start()
+
+    slots = MEM // local_len
+    has_up, has_down = z < levels - 1, z > 0
 
     def slot(s):
         return pl.ds(s * local_len, local_len)
@@ -634,68 +712,68 @@
         column = xs[block, pl.ds(batch * local_len, local_len), 2 * width : 2 * width + 128]
         return column[:, 40:41].astype(f32)
 
-    def place(block, s, follow):
+    def spread_given(i, carry):
+        at = pl.ds(pl.multiple_of((i % slots) * local_len, local_len), local_len)
+        pair = i // slots
+        mine = dot_f32(graw[pair // batches, pair % batches, at], sel[...])
+        win[pair, at] = mine.astype(bf16)
+        return carry
+
+    def keep_or(block, batch, s, moved):
+        at = block * batches + batch
+        held = win[at, slot(s)]
+        first = jnp.broadcast_to(starts_of(block, batch), held.shape) > 0.5
+        win[at, slot(s)] = jnp.where(first, held.astype(f32), moved.astype(f32)).astype(bf16)
+
+    def message(m, batch):
+        src = win.at[batches + batch, pl.ds((slots - 1 - 2 * m) * local_len, 2 * local_len)]
+        return pltpu.make_async_remote_copy(
+            src_ref=src, dst_ref=rbuf.at[m, batch], send_sem=gsend.at[m, batch], recv_sem=grecv.at[m, batch],
+            device_id=nb["up"], device_id_type=MESH)
+
+    rounds = slots // 2
+
+    def send_message(m, batch):
+        if m < rounds:
+            pl.when(has_up)(lambda: message(m, batch).start())
+
+    def take(m):
         for batch in range(batches):
-            at = block * batches + batch
-            mine = dot_f32(graw[block, batch, slot(s)], sel[...]).astype(bf16)
-            if follow:
-                moved = win[at, slot(s)] if block == 0 else win[batch, slot(s + 1)]
-                first = jnp.broadcast_to(starts_of(block, batch), mine.shape) > 0.5
-                mine = jnp.where(first, mine.astype(f32), moved.astype(f32)).astype(bf16)
-            win[at, slot(s)] = mine
-
-    slots = MEM // local_len
-
-    def chain(k):
-        count = min(2, slots - 1 - 2 * k)
-        top = slots - 2 * k
-        src = win.at[pl.ds(batches, batches), pl.ds((top - count) * local_len, count * local_len)]
-        dst = win.at[pl.ds(0, batches), pl.ds((top - count - 1) * local_len, count * local_len)]
-        return pltpu.make_async_remote_copy(
-            src_ref=src, dst_ref=dst, send_sem=gsend.at[k], recv_sem=grecv.at[k],
-            device_id=nb["up"], device_id_type=MESH)
-
-    rounds = slots // 2
-    has_up, has_down = z < levels - 1, z > 0
-
-    def chain_start(k):
-        pl.when(has_up)(lambda: chain(k).start())
-
-    def chain_round(k):
-        pl.when(has_down)(lambda: chain(k).wait_recv())
-        for s in (slots - 2 - 2 * k, slots - 3 - 2 * k):
-            if s >= 0:
-                place(0, s, True)
-        for s in (slots - 3 - 2 * k, slots - 4 - 2 * k):
-            if s >= 0:
-                place(1, s, True)
-        if k + 1 < rounds:
-            chain_start(k + 1)
+            pl.when(has_down)(lambda: message(m, batch).wait_recv())
+            for k in (0, 1):
+                keep_or(0, batch, slots - 1 - 2 * m - k, rbuf[m, batch, slot(1 - k)])
+            for s in (slots - 2 - 2 * m, slots - 3 - 2 * m):
+                if s >= 0:
+                    keep_or(1, batch, s, win[batch, slot(s + 1)])
+            send_message(m + 1, batch)
+
+    def early(m):
+        pl.when(z <= m)(lambda: take(m))
+
+    def late(m):
+        pl.when(z > m)(lambda: take(m))
 
     loc_g.wait()
     rem_g.wait()
-    place(0, slots - 1, False)
-    place(1, slots - 1, False)
-    place(1, slots - 2, True)
-    chain_start(0)
+    lax.fori_loop(0, 2 * batches * slots, spread_given, 0)
+    early(0)
     ga.turn(0)
     ga.line(2)
     ga.turn(1)
-    chain_round(0)
-    ga.line(3) if levels > 3 else None
-    for k in range(4, levels):
+    early(1)
+    for k in range(3, levels):
         ga.line(k)
     loc_o.wait()
     rem_o.wait()
     go.begin()
     for k in range(2, levels):
         ga.turn(k)
-    chain_round(1)
+    go.line(1)
+    early(2)
     for k in range(levels):
         ga.finish(k)
     out_a = pltpu.make_async_copy(a_all, a_out, osem.at[0])
     out_a.start()
-    go.line(1)
 
     w_a = a_all.reshape(4 * levels * 2 * shard, W_A)
     vec[...] = w_a[:, MISC:W_A].astype(f32).T
@@ -714,8 +792,11 @@
 
     lax.fori_loop(0, MISC // 256, project, 0)
     front[:, MISC:W_A] = dot_f32(act[...], w_a[:, MISC:W_A])
+    go.turn(0)
     go.line(2)
-    go.turn(0)
+    loc_i.wait()
+    rem_i.wait()
+    gi.begin()
     meta_at = pl.ds(pl.multiple_of(2 * width + c * 128, 128), 128)
 
     def gate(i, carry):
@@ -736,27 +817,15 @@
 
     lax.fori_loop(0, 2 * batches, gate, 0)
 
-    def hop(k):
-        src = win.at[:, pl.ds(MEM, local_len)] if k == 1 else cr.at[k - 2]
-        return pltpu.make_async_remote_copy(
-            src_ref=src, dst_ref=cr.at[k - 1], send_sem=msend.at[k - 1], recv_sem=mrecv.at[k - 1],
-            device_id=nb["up"], device_id_type=MESH)
-
-    def hop_start(k):
-        pl.when(jnp.logical_and(has_up, z >= k - 1))(lambda: hop(k).start())
-
-    def hop_arrived(k):
-        pl.when(z >= k)(lambda: hop(k).wait_recv())
-
-    hop_start(1)
-    go.line(3) if levels > 3 else None
-    for k in range(4, levels):
+    for batch in range(batches):
+        keep_or(1, batch, slots - 1, win[batch, pl.ds(MEM, local_len)])
+        send_message(0, batch)
+    go.turn(1)
+    for k in range(3, levels):
         go.line(k)
-    go.turn(1)
-    chain_round(2)
-    chain_round(3)
-    for k in range(4, rounds):
-        chain_round(k)
+    gi.line(1)
+    for m in range(3, rounds):
+        early(m)
 
     spread = MEM + 2 * local_len
     table = table_by_offset(w_a, per_device, shard, local_len, spread)
@@ -764,42 +833,23 @@
         line = jnp.broadcast_to(table[COL_BIAS + h : COL_BIAS + h + 1], (local_len, spread))
         turned = pltpu.roll(line, spread - local_len + 1, 1, stride=1, stride_axis=0)
         bias[h] = turned[:, : MEM + local_len]
-    loc_i.wait()
-    rem_i.wait()
-    gi.begin()
     for k in range(2, levels):
         go.turn(k)
-    for k in range(1, reach + 1):
-        hop_arrived(k)
-        if k < reach:
-            hop_start(k + 1)
-    gi.line(1)
-
-    for k in range(rounds):
-        pl.when(has_up)(lambda: chain(k).wait_send())
-    for batch in range(batches):
-        seen = []
-        for back in range(slots + 1):
-            block = jnp.maximum(t - c + 1 - back, 0) + d * 2 * levels
-            tile = w_a[pl.ds(pl.multiple_of(block * shard, 16), 16), MISC:W_A].astype(f32)
-            col = COL_BIAS + HALF_HEADS + batch
-            seen.append(tile[0:1, col : col + 1])
-        for block in range(2):
-            stopped = jnp.zeros((1, 1), f32)
-            for n in range(1, slots + 1):
-                stopped = jnp.maximum(stopped, seen[n - 1 if block else n])
-                if block:
-                    k, which = n // 2, 1 - n % 2
-                else:
-                    k, which = (n + 1) // 2, n % 2
-                if k > reach:
-                    continue
-                at = which * batches + batch
-                source = win[at, pl.ds(MEM, local_len)] if k == 0 else cr[k - 1, at]
-                into = block * batches + batch
-                held = win[into, slot(slots - n)]
-                stop = jnp.broadcast_to(stopped, held.shape) > 0.5
-                win[into, slot(slots - n)] = jnp.where(stop, held.astype(f32), source.astype(f32)).astype(bf16)
+    late(0)
+    gi.turn(0)
+    gi.line(2)
+    loc_f.wait()
+    own_f = local(f_raw, f_all.at[d, z], 18)
+    own_f.wait()
+    gf.begin()
+    late(1)
+    gi.turn(1)
+    for k in range(3, levels):
+        gi.line(k)
+    gf.line(1)
+    late(2)
+    for m in range(3, rounds):
+        late(m)
     out_w = pltpu.make_async_copy(win, win_out, osem.at[1])
     out_w.start()
 
@@ -838,11 +888,17 @@
         probs_copy(i, slot_of).start()
         return carry
 
-    lax.fori_loop(0, 2 * batches, attend, 0)
+    lax.fori_loop(0, batches, attend, 0)
+    gf.turn(0)
+    for k in range(2, levels):
+        gi.turn(k)
+    gf.line(2)
+    lax.fori_loop(batches, 2 * batches, attend, 0)
     for i in range(2 * batches - 2, 2 * batches):
         probs_copy(i, i % 2).wait()
-    gi.line(2)
-    gi.turn(0)
+    gf.turn(1)
+    for k in range(3, levels):
+        gf.line(k)
     for k in range(levels):
         go.finish(k)
 
@@ -886,15 +942,8 @@
     lax.fori_loop(0, rows // step, second, 0)
     pair = exchange(n2.at[near], n2.at[near], 1)
     pair.start()
-    gi.line(3) if levels > 3 else None
-    for k in range(4, levels):
-        gi.line(k)
-    loc_f.wait()
-    gf.begin()
-    for k in range(1, levels):
-        gi.turn(k)
-        gf.line(k)
-    gf.turn(0)
+    for k in range(2, levels):
+        gf.turn(k)
     pair.wait_recv()
     outs = [
         pltpu.make_async_copy(src, dst, osem.at[3 + i])
@@ -920,22 +969,19 @@
         return carry
 
     steps = ffn.shape[1] // 256
-    lax.fori_loop(0, steps // 2, activate, 0)
-    gf.turn(1)
-    lax.fori_loop(steps // 2, steps, activate, 0)
+    lax.fori_loop(0, steps, activate, 0)
     outs += [pltpu.make_async_copy(ffn, ffn_out, osem.at[14]), pltpu.make_async_copy(slope, slope_out, osem.at[15])]
     outs[-2].start()
     outs[-1].start()
-    for k in range(2, levels):
-        gf.turn(k)
     for k in range(levels):
         gf.finish(k)
     for group in (ga, go, gi, gf):
         group.drain()
     for cp in (give, pair):
         cp.wait_send()
-    for k in range(1, reach + 1):
-        pl.when(jnp.logical_and(has_up, z >= k - 1))(lambda: hop(k).wait_send())
+    for m in range(rounds):
+        for batch in range(batches):
+            pl.when(has_up)(lambda: message(m, batch).wait_send())
     out_a.wait()
     out_w.wait()
     out_o.wait()
@@ -944,10 +990,13 @@
         cp.wait()
 
 
-def forward(levels, batches, local_len, per_device, packs):
-    a, o, i, f, x, g = packs
+def forward(levels, batches, local_len, per_device, ins):
     bf16, f32 = jnp.bfloat16, jnp.float32
-    width = f.shape[1]
+    shape = jax.ShapeDtypeStruct
+    qk, value, router, norms, bias_in, branch, up, f, tokens, cot, vr, outr, start, count, g = ins
+    shard, width = qk.shape[0], f.shape[1]
+    a, o, i = [shape((SIDE, shard, w), bf16) for w in (W_A, W_O, up.shape[1] // SIDE)]
+    x = shape((tokens.shape[0], 2 * width + SIDE * 128), bf16)
     rows = batches * local_len
     both = 2 * rows
     wide = HALF_HEADS * PAD
@@ -961,27 +1010,28 @@
         ((rows, width), f32), ((both, width), bf16), ((W_MISC, width), f32), ((both, i.shape[2]), bf16),
         ((both, i.shape[2]), bf16),
     ]
-    reach = min(MEM // local_len // 2, levels - 1)
+    rounds = MEM // local_len // 2
     scratch = [
         (two(a), bf16), (two(o), bf16), (two(i), bf16), ((2,) + x.shape, bf16), ((2,) + g.shape, bf16),
-        (window, bf16), ((reach, 2 * batches, local_len, 2 * wide), bf16), ((g.shape[2], 2 * wide), bf16),
+        (window, bf16), ((rounds, batches, 2 * local_len, 2 * wide), bf16), ((g.shape[2], 2 * wide), bf16),
         ((both, width), f32), ((both, width), bf16), ((both, W_A), f32), ((both, W_MISC), f32),
         ((W_MISC, width), f32), ((HALF_HEADS, local_len, MEM + local_len), f32), ((2,) + probs[1:], f32),
         ((both, wide), bf16), ((both, W_O), bf16), ((rows, width), f32),
         ((rows, width), f32), ((both, width), bf16), ((both, i.shape[2]), bf16), ((both, i.shape[2]), bf16),
     ]
     rounds = MEM // local_len // 2
-    sems = [(4, 6 * levels), (4, 6 * levels), (6,), (6,), (6,), (rounds,), (rounds,), (reach,), (reach,), (2,), (2,), (16,), (2,)]
+    scratch += [(w.shape, w.dtype) for w in (qk, value, router, norms, bias_in, branch, up, vr, outr, start, count, f, a, o, i)]
+    sems = [(4, 6 * levels), (4, 6 * levels), (7,), (7,), (19,), (rounds, batches), (rounds, batches), (2,), (2,), (16,), (2,)]
     hbm = pl.BlockSpec(memory_space=pl.ANY)
     return pl.pallas_call(
         functools.partial(forward_kernel, levels, batches, local_len, per_device),
         out_shape=[jax.ShapeDtypeStruct(s, k) for s, k in outs],
-        in_specs=[hbm] * 6,
+        in_specs=[hbm] * len(ins),
         out_specs=[hbm] * len(outs),
         scratch_shapes=[pltpu.VMEM(s, k) for s, k in scratch] + [pltpu.SemaphoreType.DMA(s) for s in sems],
         compiler_params=pltpu.CompilerParams(
             collective_id=1, has_side_effects=True, vmem_limit_bytes=VMEM_BYTES),
-    )(a, o, i, f, x, g)
+    )(*ins)
 
 
 def add_rows(dst, terms):
@@ -1033,7 +1083,8 @@
 
     def along(self, j, to, first=False):
         base = (6 if to == "up" else 7) * self.levels
-        return self.copy(self.view("rx" if first else to, j), self.view(to, j), base + j, to)
+        there = self.view(to, j, self.z + (1 if to == "up" else -1))
+        return self.copy(self.view("rx" if first else to, j), there, base + j, to)
 
     def issue(self, j):
         self.corner(j, "x").start()
@@ -1087,9 +1138,113 @@
             pl.when(self.z > j)(lambda: self.along(j, "down").wait_send())
 
 
+class LineFirst:
+    def __init__(self, src, view, bufs, sems, nb, d, z, levels, total):
+        self.src, self.view, self.nb, self.d, self.z, self.levels = src, view, nb, d, z, levels
+        self.cx, self.cy, self.rx, self.ry = bufs
+        self.send, self.recv = sems
+        self.sum = total
+        half = src.shape[2] // 2
+        self.by_x, self.by_y = d + 1 - 2 * (d % 2), (d + 2) % 4
+        self.low, self.high = pl.ds(0, half), pl.ds(half, half)
+
+    def copy(self, src, dst, slot, to):
+        return pltpu.make_async_remote_copy(
+            src_ref=src, dst_ref=dst, send_sem=self.send.at[slot], recv_sem=self.recv.at[slot],
+            device_id=self.nb[to], device_id_type=MESH)
+
+    def along(self, j, column, to, level, first=False):
+        slot = (0 if to == "up" else 4 * self.levels) + 4 * j + column
+        after = level + (1 if to == "up" else -1)
+        src = self.src.at[column, j] if first else self.view(j, column)
+        return self.copy(src, self.view(self.levels if to == "down" and after == j else j, column), slot, to)
+
+    def lift(self, j, stage):
+        def hop(to, level):
+            for column in range(4):
+                if stage:
+                    before = level - (1 if to == "up" else -1)
+                    self.along(j, column, to, before).wait_recv()
+                    held = self.view(j, column)
+                    add_rows(held, [held, self.src.at[column, j]])
+                self.along(j, column, to, level, first=stage == 0).start()
+
+        if stage < j:
+            pl.when(self.z == stage)(lambda: hop("up", stage))
+        if self.levels - 1 - stage > j:
+            pl.when(self.z == self.levels - 1 - stage)(lambda: hop("down", self.levels - 1 - stage))
+
+    def gathered(self, j):
+        @pl.when(self.z == j)
+        def _():
+            for column in range(4):
+                terms = [self.src.at[column, j]]
+                if j > 0:
+                    self.along(j, column, "up", j - 1).wait_recv()
+                    terms.append(self.view(j, column))
+                if j < self.levels - 1:
+                    self.along(j, column, "down", j + 1).wait_recv()
+                    terms.append(self.view(self.levels, column))
+                add_rows(terms[0], terms)
+
+    def plane(self, k):
+        base = 8 * self.levels
+        part = lambda column, rows: self.src.at[column, self.z, rows]
+        return (
+            self.copy(part(3 - self.d, self.low), self.cx, base, "x"),
+            self.copy(part(3 - self.d, self.high), self.cy, base + 1, "y"),
+            self.copy(part(self.by_x, self.low), self.rx.at[self.low], base + 2, "x"),
+            self.copy(part(self.by_y, self.high), self.ry.at[self.high], base + 3, "y"),
+            self.copy(self.cy, self.rx.at[self.high], base + 4, "x"),
+            self.copy(self.cx, self.ry.at[self.low], base + 5, "y"),
+        )[k]
+
+    def issue(self):
+        for k in range(4):
+            self.plane(k).start()
+
+    def turn(self):
+        self.plane(0).wait_recv()
+        add_rows(self.cx, [self.cx, self.src.at[self.by_y, self.z, self.low]])
+        self.plane(5).start()
+        self.plane(1).wait_recv()
+        add_rows(self.cy, [self.cy, self.src.at[self.by_x, self.z, self.high]])
+        self.plane(4).start()
+
+    def column(self):
+        for k in range(2, 6):
+            self.plane(k).wait_recv()
+        add_rows(self.sum, [self.rx, self.ry, self.src.at[self.d, self.z]])
+
+    def drain(self):
+        for k in range(6):
+            self.plane(k).wait_send()
+        for j in range(self.levels):
+            for column in range(4):
+                for level in range(self.levels):
+                    if level < j:
+                        pl.when(self.z == level)(lambda: self.along(j, column, "up", level).wait_send())
+                    if level > j:
+                        pl.when(self.z == level)(lambda: self.along(j, column, "down", level).wait_send())
+
+
+A_PART = 896
+AHEAD = 3
+
+
+def LAGS(count):
+    return [2] + [4 + 3 * k for k in range(count - 1)]
+
+
 class Pipeline:
-    def __init__(self, units, levels, ahead):
+    def __init__(self, units, levels, ahead, lags):
         self.units, self.levels, self.ahead, self.now = units, levels, ahead, 0
+        self.follow = [lambda s, j: s.column(j)]
+        for stage in range(levels - 1):
+            self.follow.append(lambda s, j, stage=stage: s.lift(j, stage))
+        self.follow.append(lambda s, j: s.total(j))
+        self.lags = lags(len(self.follow))
+        self.done = [0] * len(units)
 
     def each(self, n, act):
         if 0 <= n < len(self.units):
@@ -1100,19 +1255,27 @@
         for n in range(self.ahead):
             self.each(n, lambda s, j: s.issue(j))
 
+    def advance(self, n):
+        self.each(n, self.follow[self.done[n]])
+        self.done[n] += 1
+
     def step(self):
         n = self.now
-        self.each(n, lambda s, j: s.turn(j))
-        self.each(n + self.ahead, lambda s, j: s.issue(j))
-        self.each(n - 1, lambda s, j: s.column(j))
-        for stage in range(self.levels - 1):
-            self.each(n - 2 - stage, lambda s, j: s.lift(j, stage))
-        self.each(n - 1 - self.levels, lambda s, j: s.total(j))
+        if n < len(self.units):
+            self.each(n, lambda s, j: s.turn(j))
+            self.each(n + self.ahead, lambda s, j: s.issue(j))
+        for m in range(min(n + 1, len(self.units))):
+            while self.done[m] < len(self.lags) and n - m >= self.lags[self.done[m]]:
+                self.advance(m)
         self.now += 1
 
     def finish(self):
-        while self.now < len(self.units) + self.levels + 1:
+        while self.now < len(self.units):
             self.step()
+        while min(self.done) < len(self.follow):
+            for m in range(len(self.units)):
+                if self.done[m] < len(self.follow):
+                    self.advance(m)
 
 
 def norm_rows(values):
@@ -1145,9 +1308,9 @@
     f_total, i_total, o_total, a_total, m_total, *rest,
 ):
     bf16, f32 = jnp.bfloat16, jnp.float32
-    f_bufs, i_bufs, m_bufs = rest[:7], rest[7:14], rest[14:21]
-    o_src, o_cx, o_cy, a_src, a_cx, a_cy = rest[21:27]
-    send, recv, lsem, tsem, esend, erecv, osem, ready, freed = rest[27:]
+    f_bufs, i_bufs, m_bufs = rest[:6], rest[6:12], rest[12:18]
+    a_src, a_cx, a_cy, o_src, o_line, o_cx, o_cy, o_rx, o_ry = rest[18:27]
+    send, recv, osend, orecv, lsem, tsem, esend, erecv, osem, ready, freed = rest[27:]
     d, t = lax.axis_index("doc"), lax.axis_index("tm")
     z, c = t // 2, t % 2
     nb = neighbours(2 * levels)
@@ -1167,6 +1330,9 @@
     meta_at = pl.ds(pl.multiple_of(2 * width + c * 128, 128), 128)
     l_ffn = load(ffn_in, ffn, 0)
     l_grad = load(xs_in.at[:, :, pl.ds(width, width)], grad, 1)
+    enter(nb, z, levels)
+    l_ffn.wait()
+    l_grad.wait()
     l_wf = load(wf_in, w_f, 2)
     l_slope = load(slope_in, slope, 3)
     l_n2 = load(n2_in, n2, 4)
@@ -1184,46 +1350,69 @@
         at = pl.ds(i * local_len, local_len)
         return [
             pltpu.make_async_copy(win_in.at[i], win.at[i % 2], tsem.at[0, i % 2]),
-            pltpu.make_async_copy(probs_in.at[i], probs.at[i % 2], tsem.at[1, i % 2]),
-            pltpu.make_async_copy(front_in.at[at, pl.ds(0, MISC)], front.at[i % 2], tsem.at[2, i % 2]),
+            pltpu.make_async_copy(front_in.at[at, pl.ds(0, wide)], front.at[i % 2, :, pl.ds(0, wide)], tsem.at[2, i % 2]),
+            pltpu.make_async_copy(
+                front_in.at[at, pl.ds(W_QK, W_VAL)], front.at[i % 2, :, pl.ds(wide, W_VAL)], tsem.at[3, i % 2]),
         ]
+
+    def probs_tile(n):
+        return pltpu.make_async_copy(probs_in.at[n // HALF_HEADS, n % HALF_HEADS], probs.at[n % 2], tsem.at[1, n % 2])
 
     for cp in tiles(0):
         cp.start()
-    enter(nb, z, levels)
-
-    names = ("cx", "cy", "rx", "ry", "up", "down")
+    probs_tile(0).start()
+
+    names = ("cx", "cy", "rx", "ry")
 
     def plain(bufs):
-        return lambda name, j: bufs[1 + names.index(name)].at[j]
+        def view(name, j, level=z):
+            if name == "up":
+                return bufs[5].at[j]
+            if name == "down":
+                return bufs[5].at[jnp.where(level == j, levels, j)]
+            return bufs[1 + names.index(name)].at[j]
+
+        return view
 
     block_rows = shard * SIDE
 
     def within(held, cx, cy, cols):
-        def view(name, j):
+        def view(name, j, level=z):
             if name in ("cx", "cy"):
-                return (cx if name == "cx" else cy).at[j]
+                return (cx if name == "cx" else cy).at[j, :, cols]
             ref, base = held[name]
-            return ref.at[pl.ds(base + j * block_rows, block_rows), pl.ds(0, cols)]
+            return ref.at[pl.ds(base + j * block_rows, block_rows), cols]
 
         return view
 
     span = levels * block_rows
-    o_view = within(dict(rx=(ffn, 0), ry=(ffn, span), up=(slope, 0), down=(slope, span)), o_cx, o_cy, W_O)
-    a_view = within(dict(rx=(w_i, 0), ry=(w_i, span), up=(w_i, 2 * span), down=(w_i, 3 * span)), a_cx, a_cy, MISC)
+    a_held = dict(rx=(w_i, 0), ry=(w_i, span), up=(w_i, 2 * span), down=(w_i, 3 * span))
+    a_cols = [pl.ds(k * A_PART, A_PART) for k in range(MISC // A_PART)]
     sums = [
         Scatter(src, view, (send.at[i], recv.at[i]), nb, d, z, levels, total)
         for i, (src, view, total) in enumerate((
             (f_bufs[0], plain(f_bufs), f_total), (i_bufs[0], plain(i_bufs), i_total),
-            (o_src, o_view, o_total), (a_src, a_view, a_total), (m_bufs[0], plain(m_bufs), m_total)))
+            (m_bufs[0], plain(m_bufs), m_total)) + tuple(
+                (a_src.at[:, :, :, cols], within(a_held, a_cx, a_cy, cols), a_total.at[:, cols]) for cols in a_cols))
     ]
-    sf, si, so, sa, sm = sums
+    sf, si, sm = sums[:3]
+    held = []
+    for ref in (ffn, slope):
+        for base in range(0, ref.shape[0], 4 * block_rows):
+            held.append((ref, base))
+    held = held[:levels] + [(o_line, 0)]
+
+    def o_view(slot, column):
+        ref, base = held[slot]
+        return ref.at[pl.ds(base + column * block_rows, block_rows), pl.ds(0, W_O)]
+
+    so = LineFirst(o_src, o_view, (o_cx, o_cy, o_rx, o_ry), (osend, orecv), nb, d, z, levels, o_total)
     order = []
     for k in range((levels + 1) // 2):
         order += [levels - 1 - k, k] if levels - 1 - k != k else [k]
-    units = [[(s, j)] for s in (sf, si, so, sa) for j in order]
+    units = [[(s, j)] for s in [sf, si] + sums[3:] for j in order]
     units[-1] = units[-1] + [(sm, j) for j in order]
-    line = Pipeline(units, levels, 2)
+    line = Pipeline(units, levels, AHEAD, LAGS)
 
     def exchange(src, dst, index):
         return pltpu.make_async_remote_copy(
@@ -1241,8 +1430,6 @@
 
         lax.fori_loop(0, total // chunk, body, 0)
 
-    l_ffn.wait()
-    l_grad.wait()
     g_all = grad.reshape(both, width)
     f_rows = f_bufs[0].shape[2]
     f_span = levels * f_rows
@@ -1331,7 +1518,10 @@
     l_mixed.wait()
     for column in range(4):
         weight_grad(o_src, db, dmix, 640, W_O, column)
-    line.step()
+    ends = jnp.where(z < levels - 1, 1, 0) + jnp.where(z > 0, 1, 0)
+    pl.semaphore_wait(ready, 2 + ends)
+    for j in order:
+        so.lift(j, 0)
     l_wo.wait()
 
     def mix(i, carry):
@@ -1371,7 +1561,11 @@
                 d_att = d_att + gated[:, lane : lane + 1] * part
                 d_gates = jnp.where(lanes == lane, jnp.sum(part * got, axis=-1, keepdims=True), d_gates)
             d_att = d_att.astype(bf16)
-            p = probs[slot, h]
+            n = i * HALF_HEADS + h
+            if n + 1 < 2 * batches * HALF_HEADS:
+                probs_tile(n + 1).start()
+            probs_tile(n).wait()
+            p = probs[n % 2]
             d_p = dot_f32(d_att, win[slot, :, v_cols], NT)
             delta = jnp.sum(d_p * p, axis=-1, keepdims=True)
             d_s = p * (d_p - delta)
@@ -1386,18 +1580,30 @@
             for e in range(EXPERTS):
                 lane = h * EXPERTS + e
                 col = W_QK + (e * HALF_HEADS + h) * PAD
-                part = front[slot, :, col : col + PAD]
+                part = front[slot, :, col - W_QK + wide : col - W_QK + wide + PAD]
                 d_gates = jnp.where(lanes == lane, jnp.sum(part * d_v, axis=-1, keepdims=True), d_gates)
                 dfront[at, col : col + PAD] = (gated[:, lane : lane + 1] * d_v).astype(bf16)
         d_logits = jnp.where(lanes < N_ROUTE, d_gates * picks * gate * (1.0 - gate), 0.0)
         dfront[at, MISC:W_A] = d_logits.astype(bf16)
 
-    for i in range(2 * batches):
+    def o_stage(stage, part):
+        for j in part:
+            so.lift(j, stage)
+
+    outer, inner_levels = order[:2], order[2:]
+    attend(0)
+    line.step()
+    attend(1)
+    o_stage(1, outer)
+    line.step()
+    for i in range(2, 2 * batches):
         attend(i)
-        if line.now + line.ahead == 2 * levels:
-            ends = jnp.where(z < levels - 1, 1, 0) + jnp.where(z > 0, 1, 0)
-            pl.semaphore_wait(ready, 2 + ends)
-        line.step()
+    l_act.wait()
+    one_all = grad.reshape(both, width)
+    for column in range(4):
+        weight_grad(a_src, one_all, dfront, 896, MISC, column)
+    line.step()
+    o_stage(1, inner_levels)
     last.wait()
 
     def final(i, carry):
@@ -1415,11 +1621,9 @@
     outs = [pltpu.make_async_copy(db.at[near], layer_out, osem.at[0])]
     outs[0].start()
 
-    l_act.wait()
-    one_all = grad.reshape(both, width)
-    for column in range(4):
-        weight_grad(a_src, one_all, dfront, 896, MISC, column)
     line.step()
+    for stage in range(2, levels - 1):
+        o_stage(stage, order)
     for cp in l_wa:
         cp.wait()
 
@@ -1440,6 +1644,9 @@
     hand.start()
     through_front(near)
     line.step()
+    for j in order:
+        so.gathered(j)
+    so.issue()
 
     spread = MEM + 2 * local_len
     ids = lax.broadcasted_iota(jnp.int32, (local_len, 1), 0)
@@ -1478,7 +1685,6 @@
     lax.fori_loop(0, rows // step, first, 0)
     outs.append(pltpu.make_async_copy(dhid, grad_out, osem.at[1]))
     outs[1].start()
-    line.step()
     columns = norms[...].T
 
     for column in range(4):
@@ -1488,16 +1694,22 @@
         misc = dot_f32(one_hot, high, NT) + dot_f32(one_hot, low, NT)
         misc = misc + dot_f32(one_all[:, at], dfront[:, MISC:W_A], TN) + columns[column * span : (column + 1) * span]
         m_bufs[0][column] = misc.astype(bf16).reshape(levels, block_rows, W_MISC)
+    line.step()
+    line.step()
+    so.turn()
+    line.step()
+    line.step()
+    so.column()
     line.finish()
     outs.append(pltpu.make_async_copy(f_total, f_out, osem.at[2]))
     outs[2].start()
     mine, other = [pl.ds(pl.multiple_of(k * shard, 16), shard) for k in (c, 1 - c)]
     for i, (total, out) in enumerate(((i_total, i_out), (o_total, o_out), (a_total, a_out), (m_total, m_out))):
+        outs.append(exchange(total.at[other], out.at[c], 4 + i))
+        outs[-1].start()
         outs.append(pltpu.make_async_copy(total.at[mine], out.at[c], osem.at[3 + i]))
         outs[-1].start()
-        outs.append(exchange(total.at[other], out.at[c], 4 + i))
-        outs[-1].start()
-    for s in sums:
+    for s in sums + [so]:
         s.drain()
     for cp in outs:
         cp.wait()
@@ -1511,12 +1723,13 @@
     both = 2 * rows
     f_rows = ff // (4 * levels)
     b_rows = width // (4 * levels)
+    wide = HALF_HEADS * PAD
     outs = [((f_rows, width), f32)] + [((SIDE, shard, w), f32) for w in (ff, W_O, MISC, W_MISC)]
     outs += [((rows, width), bf16), ((rows, width), f32)]
     scratch = [(v.shape, v.dtype) for v in (w_f, w_i, ffn, slope)]
     scratch += [((2, rows, width), bf16), ((2, rows, 128), bf16)]
     scratch += [(n2.shape, bf16), (hidden.shape, f32), ((8, width), f32), (att.shape, bf16), (gates.shape, f32)]
-    scratch += [((2, local_len, MISC), f32), ((2,) + win.shape[1:], bf16), ((2,) + probs.shape[1:], f32)]
+    scratch += [((2, local_len, wide + W_VAL), f32), ((2,) + win.shape[1:], bf16), ((2,) + probs.shape[2:], f32)]
     scratch += [
         ((both, width), f32), ((rows, width), f32), ((rows, width), f32), ((both, width), bf16),
         ((both, W_O), bf16), ((both, W_A), bf16), ((HALF_HEADS, local_len, MEM + local_len), f32),
@@ -1525,11 +1738,13 @@
     scratch += [((b_rows, w), f32) for w in (ff, W_O, MISC, W_MISC)]
     for r, w in ((f_rows, width), (b_rows, ff), (b_rows, W_MISC)):
         scratch.append(((4, levels, r, w), bf16))
-        scratch += [((levels, k, w), bf16) for k in (r // 2, r // 2, r, r, r, r)]
-    for w in (W_O, MISC):
-        scratch.append(((4, levels, b_rows, w), bf16))
-        scratch += [((levels, b_rows // 2, w), bf16)] * 2
-    sems = [(5, 8 * levels), (5, 8 * levels), (17,), (3, 2), (8,), (8,), (8,)]
+        scratch += [((levels, k, w), bf16) for k in (r // 2, r // 2, r, r)]
+        scratch.append(((levels + 1, r, w), bf16))
+    scratch.append(((4, levels, b_rows, MISC), bf16))
+    scratch += [((levels, b_rows // 2, MISC), bf16)] * 2
+    scratch += [((4, levels, b_rows, W_O), bf16), ((4 * b_rows, W_O), bf16)]
+    scratch += [((k, W_O), bf16) for k in (b_rows // 2, b_rows // 2, b_rows, b_rows)]
+    sems = [(3 + MISC // A_PART, 8 * levels)] * 2 + [(8 * levels + 6,), (8 * levels + 6,), (17,), (4, 2), (8,), (8,), (10,)]
     hbm = pl.BlockSpec(memory_space=pl.ANY)
     return pl.pallas_call(
         functools.partial(backward_kernel, levels, batches, local_len, per_device, shard),
@@ -1544,16 +1759,63 @@
     )(*ins)
 
 
-def split_heads(a, lead):
-    rows = a.shape[0]
-    a = pad_last(a.reshape(rows, lead, SIDE, HALF_HEADS, HEAD_DIM), PAD)
-    return jnp.transpose(a, (2, 0, 1, 3, 4)).reshape(SIDE, rows, lead * HALF_HEADS * PAD)
-
-
-def join_heads(a, lead):
-    rows = a.shape[1]
-    a = a.reshape(SIDE, rows, lead, HALF_HEADS, PAD)[..., :HEAD_DIM]
-    return jnp.transpose(a, (1, 2, 0, 3, 4)).reshape(rows, lead * HEADS * HEAD_DIM)
+def share_kernel(
+    per_device, f_in, i_in, o_in, a_in, m_in, layer_in, grad_in,
+    f_out, in_out, branch_out, value_out, qk_out, router_out, gain1, shift1, gain2, shift2, bias_out, layer_out, grad_out,
+    f_hold, layer_hold, grad_hold, sems,
+):
+    big = ((f_in, f_hold, f_out), (layer_in, layer_hold, layer_out), (grad_in, grad_hold, grad_out))
+    there = [pltpu.make_async_copy(src, held, sems.at[i]) for i, (src, held, unused) in enumerate(big)]
+    back = [pltpu.make_async_copy(held, dst, sems.at[3 + i]) for i, (unused, held, dst) in enumerate(big)]
+    for cp in there:
+        cp.start()
+    for side in range(SIDE):
+        for p in range(i_in.shape[2] // PAD):
+            col = (p * SIDE + side) * PAD
+            in_out[:, col : col + PAD] = i_in[side, :, p * PAD : (p + 1) * PAD]
+        for h in range(HALF_HEADS):
+            at = (side * HALF_HEADS + h) * HEAD_DIM
+            for e in range(EXPERTS):
+                col, dst = (e * HALF_HEADS + h) * PAD, e * HEADS * HEAD_DIM + at
+                value_out[:, dst : dst + HEAD_DIM] = a_in[side, :, W_QK + col : W_QK + col + HEAD_DIM]
+                branch_out[:, dst : dst + HEAD_DIM] = o_in[side, :, col : col + HEAD_DIM]
+            for kind in range(2):
+                col, dst = (kind * HALF_HEADS + h) * PAD, kind * HEADS * HEAD_DIM + at
+                qk_out[:, dst : dst + HEAD_DIM] = a_in[side, :, col : col + HEAD_DIM]
+        routes = HALF_HEADS * EXPERTS
+        for kind in range(2):
+            dst = (kind * SIDE + side) * routes
+            router_out[:, dst : dst + routes] = m_in[side, :, kind * routes : (kind + 1) * routes]
+        turned = m_in[side].T
+        bias_out[side * HALF_HEADS : (side + 1) * HALF_HEADS] = turned[COL_BIAS : COL_BIAS + HALF_HEADS, :per_device]
+    turned = (m_in[0] + m_in[1]).T
+    for i, out in enumerate((gain1, shift1, gain2, shift2)):
+        out[...] = turned[COL_NORM + i : COL_NORM + i + 1]
+    for cp, after in zip(there, back):
+        cp.wait()
+        after.start()
+    for cp in back:
+        cp.wait()
+
+
+def shares_of(per_device, ins):
+    f, i, o, a, m, layer, grad = ins
+    shard = i.shape[1]
+    inner = HEADS * HEAD_DIM
+    f32 = jnp.float32
+    shapes = [
+        (f.shape, f32), ((shard, SIDE * i.shape[2]), f32), ((shard, EXPERTS * inner), f32),
+        ((shard, EXPERTS * inner), f32), ((shard, 2 * inner), f32), ((shard, 2 * HEADS * EXPERTS), f32)]
+    shapes += [((1, shard), f32)] * 4 + [((HEADS, per_device), f32), (layer.shape, layer.dtype), (grad.shape, f32)]
+    hbm, vmem = pl.BlockSpec(memory_space=pl.ANY), pl.BlockSpec(memory_space=pltpu.VMEM)
+    return pl.pallas_call(
+        functools.partial(share_kernel, per_device),
+        out_shape=[jax.ShapeDtypeStruct(s, k) for s, k in shapes],
+        in_specs=[hbm] + [vmem] * 4 + [hbm] * 2,
+        out_specs=[hbm] + [vmem] * 10 + [hbm] * 2,
+        scratch_shapes=[pltpu.VMEM(w.shape, w.dtype) for w in (f, layer, grad)] + [pltpu.SemaphoreType.DMA((6,))],
+        compiler_params=pltpu.CompilerParams(vmem_limit_bytes=VMEM_BYTES),
+    )(*ins)
 
 
 def on_chip(
@@ -1570,68 +1832,30 @@
     blocks = 4 * levels
     bf16, f32 = jnp.bfloat16, jnp.float32
 
-    a_qk = split_heads(qk_weight, 2)
-    a_v = split_heads(value_weight, EXPERTS)
-    a_o = split_heads(output_weight.T, EXPERTS)
-    route = jnp.transpose(
-        router_weight.reshape(shard, 2, SIDE, HALF_HEADS * EXPERTS), (2, 0, 1, 3)
-    ).reshape(SIDE, shard, N_ROUTE)
-    norms = jnp.broadcast_to(
-        jnp.stack([norm1_gain, norm1_shift, norm2_gain, norm2_shift], axis=1)[None], (SIDE, shard, 4))
+    norms = jnp.stack([norm1_gain, norm1_shift, norm2_gain, norm2_shift])
+    routes = [
+        jnp.transpose(r.reshape(batches, local_len, HEADS, TOPK), (0, 2, 3, 1)) for r in (value_routes, output_routes)]
     buckets = rel_bias.shape[1]
-    bias_cols = jnp.pad(
-        jnp.transpose(rel_bias.reshape(SIDE, HALF_HEADS, buckets), (0, 2, 1)),
-        ((0, 0), (0, shard - buckets), (0, 0)))
-    starts_cols = jnp.broadcast_to(
-        doc_starts.reshape(1, 1, batches).astype(bf16), (SIDE, shard, batches))
-    misc = pad_last(jnp.concatenate([route, norms, bias_cols, starts_cols], axis=2), W_MISC)
-    a_pack = jnp.concatenate([a_qk, a_v, misc], axis=2)
-    hidden_block = ffn_out.shape[0]
-    i_pack = jnp.transpose(
-        ffn_in.reshape(shard, blocks, SIDE, hidden_block), (2, 0, 1, 3)
-    ).reshape(SIDE, shard, blocks * hidden_block)
-
-    mask = (jnp.arange(local_len)[None, :] < valid_counts.reshape(batches, 1)).astype(f32).reshape(rows, 1)
-    x_own = tokens.reshape(rows, width)
-    grad_own = (cotangent.reshape(rows, width).astype(f32) * mask).astype(bf16)
-    picks = [
-        jnp.transpose(
-            selection(r.reshape(rows, SIDE, HALF_HEADS, TOPK)).reshape(rows, SIDE, HALF_HEADS * EXPERTS), (1, 0, 2))
-        for r in (value_routes, output_routes)
-    ]
-    starts_col = jnp.repeat(doc_starts.reshape(batches), local_len).reshape(rows, 1).astype(bf16)
-    counts_col = jnp.repeat(valid_counts.reshape(batches), local_len).reshape(rows, 1).astype(bf16)
-    metas = [
-        pad_last(jnp.concatenate([picks[0][s], picks[1][s]], axis=1).astype(bf16), 40) for s in range(SIDE)]
-    metas = [pad_last(jnp.concatenate([m, starts_col, counts_col], axis=1), 128) for m in metas]
-    x_pack = jnp.concatenate([x_own, grad_own] + metas, axis=1)
-    g_pack = given_cache.reshape(batches, MEM, 2 * HEADS * HEAD_DIM)
-
     (a_all, o_all, i_all, f_all, xs, act_one, front, gates, win, probs, attended, mixed, hidden, n2, vec, act,
-     slope) = forward(levels, batches, local_len, buckets, (a_pack, a_o, i_pack, ffn_out, x_pack, g_pack))
+     slope) = forward(
+        levels, batches, local_len, buckets,
+        (qk_weight, value_weight, router_weight, norms, rel_bias, output_weight.T, ffn_in, ffn_out,
+         tokens.reshape(rows, width), cotangent.reshape(rows, width), routes[0], routes[1],
+         doc_starts.reshape(1, batches), valid_counts.reshape(1, batches),
+         given_cache.reshape(batches, MEM, 2 * HEADS * HEAD_DIM)))
     w_a = a_all.reshape(width, W_A)
     w_i = i_all.reshape(width, -1)
     w_f = f_all.reshape(-1, width)
-    out_share, i_sides, o_sides, a_sides, misc, layer_out, input_grad = backward(
+    sums = backward(
         levels, batches, local_len, buckets, shard,
         (w_f, w_i, o_all, w_a, act, slope, xs, n2, hidden, vec, attended, gates, front, win, probs, mixed,
          act_one.reshape(2, rows, width)))
-    layer_out = layer_out.reshape(tokens.shape)
-    input_grad = input_grad.reshape(tokens.shape)
-    qk_share = join_heads(a_sides[:, :, :W_QK], 2)
-    value_share = join_heads(a_sides[:, :, W_QK:], EXPERTS)
-    output_share = join_heads(o_sides, EXPERTS).T
-    router_share = jnp.transpose(
-        misc[:, :, :N_ROUTE].reshape(SIDE, shard, 2, HALF_HEADS * EXPERTS), (1, 2, 0, 3)
-    ).reshape(shard, 2 * HEADS * EXPERTS)
-    norm_share = misc[0, :, COL_NORM : COL_NORM + 4] + misc[1, :, COL_NORM : COL_NORM + 4]
-    bias_share = jnp.transpose(misc[:, :buckets, COL_BIAS : COL_BIAS + HALF_HEADS], (0, 2, 1)).reshape(HEADS, buckets)
-    in_share = jnp.transpose(
-        i_sides.reshape(SIDE, shard, blocks, hidden_block), (1, 2, 0, 3)
-    ).reshape(shard, -1)
+    (out_share, in_share, branch_share, value_share, qk_share, router_share, gain1, shift1, gain2, shift2, bias_share,
+     layer_out, input_grad) = shares_of(buckets, sums)
+    gain1, shift1, gain2, shift2 = [v.reshape(shard) for v in (gain1, shift1, gain2, shift2)]
     return (
-        layer_out, input_grad, norm_share[:, 0], norm_share[:, 1], qk_share, router_share, value_share,
-        output_share, bias_share, norm_share[:, 2], norm_share[:, 3], in_share, out_share,
+        layer_out.reshape(tokens.shape), input_grad.reshape(tokens.shape), gain1, shift1, qk_share, router_share,
+        value_share, branch_share.T, bias_share, gain2, shift2, in_share, out_share,
     )
 
 

time: 365 us -> 304 us (0.83)
  Pallas kernels: 333 us -> 302 us
  local copies, waits for them, and re-layouts: 22 us -> 0 us
  other arithmetic: 5.85 us -> 1.28 us
    pallas_call x1, Pallas kernels: 171 us -> 144 us  [forward(): pl.pallas_call(functools.partial(forward_kernel, levels, batches, local_l...]
    reshape x20 -> x0, local copies, waits for them, and re-layouts: 9.57 us -> none  [the longest x3 2.88 us: join_heads(): jnp.transpose(a, (1, 2, 0, 3, 4)).reshape(rows, lead * HEADS * HEAD_DIM)]
    pallas_call x1, Pallas kernels: 162 us -> 153 us  [backward(): pl.pallas_call(functools.partial(backward_kernel, levels, batches, local_...]
    unnamed x30 -> x0, local copies, waits for them, and re-layouts: 5.73 us -> none
    pallas_call x0 -> x1, Pallas kernels: none -> 5.16 us  [shares_of(): pl.pallas_call(functools.partial(share_kernel, per_device), out_shape=[ja...]
where the time goes in v5:
time: 304 us
  Pallas kernels  302 us (99%)
    pallas_call x1, Pallas kernels, backward(): pl.pallas_call(functools.partial(backward_kernel, levels, batches, local_...  153 us
    pallas_call x1, Pallas kernels, forward(): pl.pallas_call(functools.partial(forward_kernel, levels, batches, local_l...  144 us

profile of v5, /device:TPU:0, one launch (start us, length us, event | category | flops | bytes accessed | tf_op | source)
XLA Modules:
  0.0 303.6 jit_solution(17834033339908631197)
XLA Ops:
  0.6 1.3 pad_maximum_fusion.norm_in
  1.9 143.6 %shard_map.273 = (bf16[4,4,64,1920]{3,2,1,0:T(8,128)(2,1)}, bf16[4,4,64,1280]{3,2,1,0:T(8,128)(2,1)}, bf16[4,4,64,2048]{3,2,1,0:T(8,128)(2,1)}, bf16[4,4,128,102...) custom-call(bf16[32,896]{1,0:T(8,128)(2,1)} %qk_in.1, ...), custom_call_target="tpu_custom_call" | custom-call | tf_op jit(solution)/shard_map/pallas_call | solution.py:1026
  145.5 152.8 %shard_map.274 = (f32[128,1024]{1,0:T(8,128)}, f32[2,32,2048]{2,1,0:T(8,128)}, f32[2,32,1280]{2,1,0:T(8,128)}, f32[2,32,1792]{2,1,0:T(8,128)}, f32[2,32,128]{2,1...) custom-call(bf16[2048,1024]{1,0:T(8,128)(2,1)} %bitcast.32, bf16[1024,2048]{1,0:T(8,128)(2,1)} %bitcast.31, ...), custom_call_target="tpu_custom_call" | custom-call | tf_op jit(solution)/shard_map/pallas_call | solution.py:1749
  298.3 5.2 %shard_map.275 = (f32[128,1024]{1,0:T(8,128)}, f32[32,4096]{1,0:T(8,128)}, f32[32,2240]{1,0:T(8,128)}, f32[32,2240]{1,0:T(8,128)}, f32[32,896]{1,0:T(8,128)}, /*...) custom-call(f32[128,1024]{1,0:T(8,128)} %get-tuple-element.67.f_in, ...), custom_call_target="tpu_custom_call" | custom-call | tf_op jit(solution)/shard_map/pallas_call | solution.py:1811

commit v6 on v5

--- a/solution.py
+++ b/solution.py
@@ -557,12 +557,33 @@
     return lax.dot_general(a, b, dims, preferred_element_type=jnp.float32)
 
 
+def steps_of(text):
+    return [(w.split(".")[0], w.split(".")[1][:-1], int(w[-1])) for w in text.split()]
+
+
+EVENTS = {point: steps_of(text) for point, text in dict(
+    f="f.begin0",
+    a="a.begin0",
+    stats="a.line1",
+    packs="",
+    given="m.early0 a.turn0 a.line2 a.turn1 a.line3 a.turn2 o.begin0 m.early1 a.turn3 o.line1 m.early2",
+    front="o.turn0 o.line2 i.begin0",
+    cache="o.turn1 o.line3 i.line1 f.line1 m.early3",
+    memory="o.turn2 o.turn3 i.line2 f.line2 m0.late0 i.turn0 i.line3 f.line3 m0.late1 i.turn1 m0.late2",
+    half="m1.late0 m1.late1 f.turn0 i.turn2 i.turn3 m1.late2",
+    attended="f.turn1",
+    far="",
+    pair="f.turn2 f.turn3",
+    activated="",
+).items()}
+
+
 def forward_kernel(
     levels, batches, local_len, per_device,
     qk_in, value_in, router_in, norm_in, bias_in, branch_in, up_in, f_in, token_in, cot_in, vr_in, or_in, start_in,
     count_in, g_in,
     a_out, o_out, i_out, f_all, xs_out, act_out, front_out, gates_out, win_out, probs_out, att_out,
-    mixed_out, hidden_out, n2_out, vec_out, ffn_out, slope_out,
+    mixed_out, hidden_out, n2_out, vec_out, ffn_out, slope_out, fgrad_out,
     a_all, o_all, i_all, xs, graw, win, rbuf, sel, unit, act, front, gates, vec, bias, probs, att, mixed,
     arrived, hidden, n2, ffn, slope,
     qk_raw, value_raw, router_raw, norm_raw, bias_raw, branch_raw, up_raw, vr_raw, or_raw, start_raw, count_raw, f_raw, a_pack, o_pack, i_pack,
@@ -607,6 +628,45 @@
         Gather(ref, (send.at[i], recv.at[i]), nb, d, z, levels)
         for i, ref in enumerate((a_all, o_all, i_all, f_all))
     ]
+
+    loc_f.wait()
+    own_f = local(f_raw, f_all.at[d, z], 18)
+    own_f.wait()
+    groups = dict(a=ga, o=go, i=gi, f=gf)
+    left = [
+        (name, what, k) for name in groups for what, first in (("begin", 0), ("line", 1), ("turn", 0), ("finish", 0))
+        for k in range(first, 1 if what == "begin" else levels)]
+    left += [("m", "early", k) for k in range(MEM // local_len // 2)]
+    left += [("m%d" % batch, "late", k) for batch in range(batches) for k in range(MEM // local_len // 2)]
+
+    def do(name, what, k):
+        if (name, what, k) not in left:
+            return
+        left.remove((name, what, k))
+        if what == "early":
+            early(k)
+            return
+        if what == "late":
+            late(k, int(name[1:]))
+            return
+        group = groups[name]
+        if what == "begin":
+            for cp in placed[name]:
+                cp.wait()
+            group.begin()
+        else:
+            dict(line=group.line, turn=group.turn, finish=group.finish)[what](k)
+
+    def run(point):
+        for event in EVENTS[point]:
+            do(*event)
+
+    def complete(name):
+        for event in [e for e in left if e[0] == name]:
+            do(*event)
+
+    placed = dict(f=[])
+    run("f")
 
     for cp in raws[:5]:
         cp.wait()
@@ -658,9 +718,8 @@
     loc_g = local(g_in, graw.at[c], 14)
     rem_g = sibling(g_in, graw.at[c], 4)
     rem_g.start()
-    loc_a.wait()
-    rem_a.wait()
-    ga.begin()
+    placed["a"] = (loc_a, rem_a)
+    run("a")
     sel[...] = selector(c)
 
     for cp in loc_x + rem_x:
@@ -681,7 +740,7 @@
         return carry
 
     lax.fori_loop(0, both // step, stats, 0)
-    ga.line(1)
+    run("stats")
     raws[6].wait()
     for side in range(SIDE):
         for p in range(4 * levels):
@@ -701,6 +760,8 @@
     rem_i = sibling(i_pack.at[1 - c], i_all.at[d, z, own], 6)
     rem_o.start()
     rem_i.start()
+    placed["o"], placed["i"] = (loc_o, rem_o), (loc_i, rem_i)
+    run("packs")
 
     slots = MEM // local_len
     has_up, has_down = z < levels - 1, z > 0
@@ -737,8 +798,8 @@
         if m < rounds:
             pl.when(has_up)(lambda: message(m, batch).start())
 
-    def take(m):
-        for batch in range(batches):
+    def take(m, some):
+        for batch in some:
             pl.when(has_down)(lambda: message(m, batch).wait_recv())
             for k in (0, 1):
                 keep_or(0, batch, slots - 1 - 2 * m - k, rbuf[m, batch, slot(1 - k)])
@@ -748,30 +809,16 @@
             send_message(m + 1, batch)
 
     def early(m):
-        pl.when(z <= m)(lambda: take(m))
-
-    def late(m):
-        pl.when(z > m)(lambda: take(m))
+        pl.when(z <= m)(lambda: take(m, range(batches)))
+
+    def late(m, batch):
+        pl.when(z > m)(lambda: take(m, (batch,)))
 
     loc_g.wait()
     rem_g.wait()
     lax.fori_loop(0, 2 * batches * slots, spread_given, 0)
-    early(0)
-    ga.turn(0)
-    ga.line(2)
-    ga.turn(1)
-    early(1)
-    for k in range(3, levels):
-        ga.line(k)
-    loc_o.wait()
-    rem_o.wait()
-    go.begin()
-    for k in range(2, levels):
-        ga.turn(k)
-    go.line(1)
-    early(2)
-    for k in range(levels):
-        ga.finish(k)
+    run("given")
+    complete("a")
     out_a = pltpu.make_async_copy(a_all, a_out, osem.at[0])
     out_a.start()
 
@@ -792,11 +839,7 @@
 
     lax.fori_loop(0, MISC // 256, project, 0)
     front[:, MISC:W_A] = dot_f32(act[...], w_a[:, MISC:W_A])
-    go.turn(0)
-    go.line(2)
-    loc_i.wait()
-    rem_i.wait()
-    gi.begin()
+    run("front")
     meta_at = pl.ds(pl.multiple_of(2 * width + c * 128, 128), 128)
 
     def gate(i, carry):
@@ -820,12 +863,7 @@
     for batch in range(batches):
         keep_or(1, batch, slots - 1, win[batch, pl.ds(MEM, local_len)])
         send_message(0, batch)
-    go.turn(1)
-    for k in range(3, levels):
-        go.line(k)
-    gi.line(1)
-    for m in range(3, rounds):
-        early(m)
+    run("cache")
 
     spread = MEM + 2 * local_len
     table = table_by_offset(w_a, per_device, shard, local_len, spread)
@@ -833,25 +871,9 @@
         line = jnp.broadcast_to(table[COL_BIAS + h : COL_BIAS + h + 1], (local_len, spread))
         turned = pltpu.roll(line, spread - local_len + 1, 1, stride=1, stride_axis=0)
         bias[h] = turned[:, : MEM + local_len]
-    for k in range(2, levels):
-        go.turn(k)
-    late(0)
-    gi.turn(0)
-    gi.line(2)
-    loc_f.wait()
-    own_f = local(f_raw, f_all.at[d, z], 18)
-    own_f.wait()
-    gf.begin()
-    late(1)
-    gi.turn(1)
-    for k in range(3, levels):
-        gi.line(k)
-    gf.line(1)
-    late(2)
-    for m in range(3, rounds):
-        late(m)
-    out_w = pltpu.make_async_copy(win, win_out, osem.at[1])
-    out_w.start()
+    run("memory")
+    complete("m")
+    complete("m0")
 
     key_ids = lax.broadcasted_iota(jnp.int32, (local_len, local_len), 1)
     row_ids = lax.broadcasted_iota(jnp.int32, (local_len, local_len), 0)
@@ -859,15 +881,19 @@
     def probs_copy(i, slot_of):
         return pltpu.make_async_copy(probs.at[slot_of], probs_out.at[i], psem.at[slot_of])
 
-    def attend(i, carry):
+    def pair_of(n):
+        return (n % 2) * batches + n // 2
+
+    def attend(n, carry):
+        i = pair_of(n)
         at = pl.ds(pl.multiple_of(i * local_len, local_len), local_len)
         block, batch = i // batches, i % batches
         rows_at = pl.ds(pl.multiple_of(batch * local_len, local_len), local_len)
         count = xs[block, rows_at, 2 * width : 2 * width + 128][:, 41:42].astype(f32)
         seen = jnp.logical_and(key_ids <= row_ids, key_ids.astype(f32) < count)
         picks = xs[block, rows_at, meta_at].astype(f32) * gates[at]
-        slot_of = lax.rem(i, 2)
-        pl.when(i >= 2)(lambda: probs_copy(i - 2, slot_of).wait())
+        slot_of = lax.rem(n, 2)
+        pl.when(n >= 2)(lambda: probs_copy(pair_of(n - 2), slot_of).wait())
         for h in range(HALF_HEADS):
             cols = slice(h * PAD, (h + 1) * PAD)
             q = front[at, cols].astype(bf16)
@@ -888,19 +914,17 @@
         probs_copy(i, slot_of).start()
         return carry
 
-    lax.fori_loop(0, batches, attend, 0)
-    gf.turn(0)
-    for k in range(2, levels):
-        gi.turn(k)
-    gf.line(2)
-    lax.fori_loop(batches, 2 * batches, attend, 0)
-    for i in range(2 * batches - 2, 2 * batches):
-        probs_copy(i, i % 2).wait()
-    gf.turn(1)
-    for k in range(3, levels):
-        gf.line(k)
-    for k in range(levels):
-        go.finish(k)
+    lax.fori_loop(0, 2, attend, 0)
+    run("half")
+    for batch in range(1, batches):
+        complete("m%d" % batch)
+    out_w = pltpu.make_async_copy(win, win_out, osem.at[1])
+    out_w.start()
+    lax.fori_loop(2, 2 * batches, attend, 0)
+    for n in range(2 * batches - 2, 2 * batches):
+        probs_copy(pair_of(n), n % 2).wait()
+    run("attended")
+    complete("o")
 
     w_o = o_all.reshape(4 * levels * 2 * shard, W_O)
     branch = unit
@@ -923,6 +947,7 @@
     out_project(far)
     give = exchange(branch.at[far], arrived, 0)
     give.start()
+    run("far")
     out_project(near)
     out_o = pltpu.make_async_copy(o_all, o_out, osem.at[2])
     out_o.start()
@@ -942,8 +967,7 @@
     lax.fori_loop(0, rows // step, second, 0)
     pair = exchange(n2.at[near], n2.at[near], 1)
     pair.start()
-    for k in range(2, levels):
-        gf.turn(k)
+    run("pair")
     pair.wait_recv()
     outs = [
         pltpu.make_async_copy(src, dst, osem.at[3 + i])
@@ -953,8 +977,7 @@
     ]
     for cp in outs:
         cp.start()
-    for k in range(levels):
-        gi.finish(k)
+    complete("i")
     out_i = pltpu.make_async_copy(i_all, i_out, osem.at[13])
     out_i.start()
 
@@ -970,20 +993,39 @@
 
     steps = ffn.shape[1] // 256
     lax.fori_loop(0, steps, activate, 0)
+    run("activated")
     outs += [pltpu.make_async_copy(ffn, ffn_out, osem.at[14]), pltpu.make_async_copy(slope, slope_out, osem.at[15])]
     outs[-2].start()
     outs[-1].start()
-    for k in range(levels):
-        gf.finish(k)
+
+    for m in range(rounds):
+        for batch in range(batches):
+            pl.when(has_up)(lambda: message(m, batch).wait_send())
+    out_w.wait()
+    span = ffn.shape[1] // 4
+    half = width // 2
+
+    def ffn_grad(i, carry):
+        at = pl.ds(pl.multiple_of(i * span, span), span)
+        for side in range(2):
+            cols = slice(width + side * half, width + (side + 1) * half)
+            left = jnp.concatenate([xs[0, :, cols], xs[1, :, cols]], axis=0)
+            win[i, side * span : (side + 1) * span] = dot_f32(ffn[:, at], left, TN).astype(bf16)
+        return carry
+
+    lax.fori_loop(0, 4, ffn_grad, 0)
+    for column in range(4):
+        for side in range(2):
+            outs.append(pltpu.make_async_copy(
+                win.at[column, pl.ds(side * span, span)],
+                fgrad_out.at[column, :, pl.ds(side * half, half)], osem.at[16 + 2 * column + side]))
+            outs[-1].start()
+    complete("f")
     for group in (ga, go, gi, gf):
         group.drain()
     for cp in (give, pair):
         cp.wait_send()
-    for m in range(rounds):
-        for batch in range(batches):
-            pl.when(has_up)(lambda: message(m, batch).wait_send())
     out_a.wait()
-    out_w.wait()
     out_o.wait()
     out_i.wait()
     for cp in outs:
@@ -1008,7 +1050,7 @@
         ((2,) + x.shape, bf16), ((both, width), bf16), ((both, W_A), f32), ((both, W_MISC), f32),
         (window, bf16), (probs, f32), ((both, wide), bf16), ((both, W_O), bf16),
         ((rows, width), f32), ((both, width), bf16), ((W_MISC, width), f32), ((both, i.shape[2]), bf16),
-        ((both, i.shape[2]), bf16),
+        ((both, i.shape[2]), bf16), ((4, i.shape[2] // 4, width), bf16),
     ]
     rounds = MEM // local_len // 2
     scratch = [
@@ -1021,7 +1063,7 @@
     ]
     rounds = MEM // local_len // 2
     scratch += [(w.shape, w.dtype) for w in (qk, value, router, norms, bias_in, branch, up, vr, outr, start, count, f, a, o, i)]
-    sems = [(4, 6 * levels), (4, 6 * levels), (7,), (7,), (19,), (rounds, batches), (rounds, batches), (2,), (2,), (16,), (2,)]
+    sems = [(4, 6 * levels), (4, 6 * levels), (7,), (7,), (19,), (rounds, batches), (rounds, batches), (2,), (2,), (24,), (2,)]
     hbm = pl.BlockSpec(memory_space=pl.ANY)
     return pl.pallas_call(
         functools.partial(forward_kernel, levels, batches, local_len, per_device),
@@ -1228,7 +1270,8 @@
                         pl.when(self.z == level)(lambda: self.along(j, column, "down", level).wait_send())
 
 
-A_PART = 896
+M_UNIT = 13
+A_PARTS = (768, 640, 384)
 AHEAD = 3
 
 
@@ -1269,13 +1312,18 @@
                 self.advance(m)
         self.now += 1
 
-    def finish(self):
+    def turns(self):
         while self.now < len(self.units):
             self.step()
+
+    def round(self):
+        for m in range(len(self.units)):
+            if self.done[m] < len(self.follow):
+                self.advance(m)
+
+    def finish(self):
         while min(self.done) < len(self.follow):
-            for m in range(len(self.units)):
-                if self.done[m] < len(self.follow):
-                    self.advance(m)
+            self.round()
 
 
 def norm_rows(values):
@@ -1300,7 +1348,7 @@
 
 def backward_kernel(
     levels, batches, local_len, per_device, shard,
-    wf_in, wi_in, wo_in, wa_in, ffn_in, slope_in, xs_in, n2_in, hidden_in, vec_in, att_in, gates_in, front_in,
+    fgrad_in, wf_in, wi_in, wo_in, wa_in, ffn_in, slope_in, xs_in, n2_in, hidden_in, vec_in, att_in, gates_in, front_in,
     win_in, probs_in, mixed_in, act_in,
     f_out, i_out, o_out, a_out, m_out, layer_out, grad_out,
     w_f, w_i, ffn, slope, grad, meta, n2, hidden, vec, att, gates, front, win, probs,
@@ -1328,13 +1376,13 @@
         return cp
 
     meta_at = pl.ds(pl.multiple_of(2 * width + c * 128, 128), 128)
+    l_first = load(fgrad_in, f_bufs[0], 17)
+    l_grad = load(xs_in.at[:, :, pl.ds(width, width)], grad, 1)
+    l_wf = load(wf_in, w_f, 2)
+    enter(nb, z, levels)
+    l_first.wait()
+    l_slope = load(slope_in, slope, 3)
     l_ffn = load(ffn_in, ffn, 0)
-    l_grad = load(xs_in.at[:, :, pl.ds(width, width)], grad, 1)
-    enter(nb, z, levels)
-    l_ffn.wait()
-    l_grad.wait()
-    l_wf = load(wf_in, w_f, 2)
-    l_slope = load(slope_in, slope, 3)
     l_n2 = load(n2_in, n2, 4)
     l_wi = load(wi_in, w_i, 5)
     l_hid = load(hidden_in, hidden, 6)
@@ -1387,7 +1435,7 @@
 
     span = levels * block_rows
     a_held = dict(rx=(w_i, 0), ry=(w_i, span), up=(w_i, 2 * span), down=(w_i, 3 * span))
-    a_cols = [pl.ds(k * A_PART, A_PART) for k in range(MISC // A_PART)]
+    a_cols = [pl.ds(sum(A_PARTS[:k]), A_PARTS[k]) for k in range(len(A_PARTS))]
     sums = [
         Scatter(src, view, (send.at[i], recv.at[i]), nb, d, z, levels, total)
         for i, (src, view, total) in enumerate((
@@ -1411,7 +1459,7 @@
     for k in range((levels + 1) // 2):
         order += [levels - 1 - k, k] if levels - 1 - k != k else [k]
     units = [[(s, j)] for s in [sf, si] + sums[3:] for j in order]
-    units[-1] = units[-1] + [(sm, j) for j in order]
+    units[M_UNIT] = units[M_UNIT] + [(sm, j) for j in order]
     line = Pipeline(units, levels, AHEAD, LAGS)
 
     def exchange(src, dst, index):
@@ -1430,16 +1478,12 @@
 
         lax.fori_loop(0, total // chunk, body, 0)
 
-    g_all = grad.reshape(both, width)
-    f_rows = f_bufs[0].shape[2]
-    f_span = levels * f_rows
-    for column in (3 - d, sf.by_x, sf.by_y, d):
-        at = pl.ds(pl.multiple_of(column * f_span, f_span), f_span)
-        f_bufs[0][column] = dot_f32(ffn[:, at], g_all[...], TN).astype(bf16).reshape(levels, f_rows, width)
     line.begin()
 
     l_wf.wait()
     l_slope.wait()
+    l_grad.wait()
+    g_all = grad.reshape(both, width)
 
     def back(i, carry):
         at = pl.ds(pl.multiple_of(i * 256, 256), 256)
@@ -1496,6 +1540,7 @@
     l_act = load(act_in, grad, 13)
 
     through_out = times(ffn, lambda cols: w_f[:, cols], (((1,), (0,)), ((), ())))
+    l_ffn.wait()
     through_out(far)
     pair.wait()
     last = exchange(branch.at[far], arrived, 2)
@@ -1644,9 +1689,6 @@
     hand.start()
     through_front(near)
     line.step()
-    for j in order:
-        so.gathered(j)
-    so.issue()
 
     spread = MEM + 2 * local_len
     ids = lax.broadcasted_iota(jnp.int32, (local_len, 1), 0)
@@ -1696,9 +1738,13 @@
         m_bufs[0][column] = misc.astype(bf16).reshape(levels, block_rows, W_MISC)
     line.step()
     line.step()
+    for j in order:
+        so.gathered(j)
+    line.turns()
+    so.issue()
+    line.round()
     so.turn()
-    line.step()
-    line.step()
+    line.round()
     so.column()
     line.finish()
     outs.append(pltpu.make_async_copy(f_total, f_out, osem.at[2]))
@@ -1717,7 +1763,7 @@
 
 def backward(levels, batches, local_len, per_device, shard, ins):
     bf16, f32 = jnp.bfloat16, jnp.float32
-    (w_f, w_i, w_o, w_a, ffn, slope, xs, n2, hidden, vec, att, gates, front, win, probs, mixed, act) = ins
+    (unused, w_f, w_i, w_o, w_a, ffn, slope, xs, n2, hidden, vec, att, gates, front, win, probs, mixed, act) = ins
     ff, width = w_f.shape
     rows = batches * local_len
     both = 2 * rows
@@ -1744,7 +1790,7 @@
     scratch += [((levels, b_rows // 2, MISC), bf16)] * 2
     scratch += [((4, levels, b_rows, W_O), bf16), ((4 * b_rows, W_O), bf16)]
     scratch += [((k, W_O), bf16) for k in (b_rows // 2, b_rows // 2, b_rows, b_rows)]
-    sems = [(3 + MISC // A_PART, 8 * levels)] * 2 + [(8 * levels + 6,), (8 * levels + 6,), (17,), (4, 2), (8,), (8,), (10,)]
+    sems = [(3 + len(A_PARTS), 8 * levels)] * 2 + [(8 * levels + 6,), (8 * levels + 6,), (18,), (4, 2), (8,), (8,), (10,)]
     hbm = pl.BlockSpec(memory_space=pl.ANY)
     return pl.pallas_call(
         functools.partial(backward_kernel, levels, batches, local_len, per_device, shard),
@@ -1836,8 +1882,9 @@
     routes = [
         jnp.transpose(r.reshape(batches, local_len, HEADS, TOPK), (0, 2, 3, 1)) for r in (value_routes, output_routes)]
     buckets = rel_bias.shape[1]
+    hidden_block = ffn_out.shape[0]
     (a_all, o_all, i_all, f_all, xs, act_one, front, gates, win, probs, attended, mixed, hidden, n2, vec, act,
-     slope) = forward(
+     slope, f_grad) = forward(
         levels, batches, local_len, buckets,
         (qk_weight, value_weight, router_weight, norms, rel_bias, output_weight.T, ffn_in, ffn_out,
          tokens.reshape(rows, width), cotangent.reshape(rows, width), routes[0], routes[1],
@@ -1848,7 +1895,7 @@
     w_f = f_all.reshape(-1, width)
     sums = backward(
         levels, batches, local_len, buckets, shard,
-        (w_f, w_i, o_all, w_a, act, slope, xs, n2, hidden, vec, attended, gates, front, win, probs, mixed,
+        (f_grad.reshape(4, levels, hidden_block, width), w_f, w_i, o_all, w_a, act, slope, xs, n2, hidden, vec, attended, gates, front, win, probs, mixed,
          act_one.reshape(2, rows, width)))
     (out_share, in_share, branch_share, value_share, qk_share, router_share, gain1, shift1, gain2, shift2, bias_share,
      layer_out, input_grad) = shares_of(buckets, sums)

time: 304 us -> 289 us (0.951)
  Pallas kernels: 302 us -> 287 us
    pallas_call x1, Pallas kernels: 153 us -> 140 us  [backward(): pl.pallas_call(functools.partial(backward_kernel, levels, batches, local_...]
where the time goes in v6:
time: 289 us
  Pallas kernels  287 us (99%)
    pallas_call x1, Pallas kernels, forward(): pl.pallas_call(functools.partial(forward_kernel, levels, batches, local_l...  142 us
    pallas_call x1, Pallas kernels, backward(): pl.pallas_call(functools.partial(backward_kernel, levels, batches, local_...  140 us

profile of v6, /device:TPU:0, one launch (start us, length us, event | category | flops | bytes accessed | tf_op | source)
XLA Modules:
  0.0 288.7 jit_solution(3195402861919862078)
XLA Ops:
  0.6 1.3 pad_maximum_fusion.norm_in
  1.9 141.8 %shard_map.273 = (bf16[4,4,64,1920]{3,2,1,0:T(8,128)(2,1)}, bf16[4,4,64,1280]{3,2,1,0:T(8,128)(2,1)}, bf16[4,4,64,2048]{3,2,1,0:T(8,128)(2,1)}, bf16[4,4,128,102...) custom-call(bf16[32,896]{1,0:T(8,128)(2,1)} %qk_in.1, ...), custom_call_target="tpu_custom_call" | custom-call | tf_op jit(solution)/shard_map/pallas_call | solution.py:1068
  143.7 139.6 %shard_map.274 = (f32[128,1024]{1,0:T(8,128)}, f32[2,32,2048]{2,1,0:T(8,128)}, f32[2,32,1280]{2,1,0:T(8,128)}, f32[2,32,1792]{2,1,0:T(8,128)}, f32[2,32,128]{2,1...) custom-call(bf16[4,4,128,1024]{3,2,1,0:T(8,128)(2,1)} %bitcast.34, bf16[2048,1024]{1,0:T(8,128)(2,1)} %bitcast.33, ...), custom_call_target="tpu_custom_call" | custom-call | tf_op jit(solution)/shard_map/pallas_call | solution.py:1795
  283.3 5.2 %shard_map.275 = (f32[128,1024]{1,0:T(8,128)}, f32[32,4096]{1,0:T(8,128)}, f32[32,2240]{1,0:T(8,128)}, f32[32,2240]{1,0:T(8,128)}, f32[32,896]{1,0:T(8,128)}, /*...) custom-call(f32[128,1024]{1,0:T(8,128)} %get-tuple-element.69.f_in, ...), custom_call_target="tpu_custom_call" | custom-call | tf_op jit(solution)/shard_map/pallas_call | solution.py:1857

commit v7 on v6

--- a/solution.py
+++ b/solution.py
@@ -1270,13 +1270,15 @@
                         pl.when(self.z == level)(lambda: self.along(j, column, "down", level).wait_send())
 
 
-M_UNIT = 13
-A_PARTS = (768, 640, 384)
+A_PARTS = (1024, 768)
 AHEAD = 3
 
 
-def LAGS(count):
-    return [2] + [4 + 3 * k for k in range(count - 1)]
+def LAGS(unit, k, levels):
+    return 2 + 3 * k if unit < 3 * levels else 1 + k
+
+
+O_STEPS = {4: ((0, 1), (1, 0)), 6: ((1, 1),), 7: ((2, 0), (2, 1))}
 
 
 class Pipeline:
@@ -1286,7 +1288,7 @@
         for stage in range(levels - 1):
             self.follow.append(lambda s, j, stage=stage: s.lift(j, stage))
         self.follow.append(lambda s, j: s.total(j))
-        self.lags = lags(len(self.follow))
+        self.lags = lags
         self.done = [0] * len(units)
 
     def each(self, n, act):
@@ -1308,7 +1310,7 @@
             self.each(n, lambda s, j: s.turn(j))
             self.each(n + self.ahead, lambda s, j: s.issue(j))
         for m in range(min(n + 1, len(self.units))):
-            while self.done[m] < len(self.lags) and n - m >= self.lags[self.done[m]]:
+            while self.done[m] < len(self.follow) and n - m >= self.lags(m, self.done[m], self.levels):
                 self.advance(m)
         self.now += 1
 
@@ -1459,7 +1461,7 @@
     for k in range((levels + 1) // 2):
         order += [levels - 1 - k, k] if levels - 1 - k != k else [k]
     units = [[(s, j)] for s in [sf, si] + sums[3:] for j in order]
-    units[M_UNIT] = units[M_UNIT] + [(sm, j) for j in order]
+    units[3 * levels + 1] = units[3 * levels + 1] + [(sm, j) for j in order]
     line = Pipeline(units, levels, AHEAD, LAGS)
 
     def exchange(src, dst, index):
@@ -1565,8 +1567,19 @@
         weight_grad(o_src, db, dmix, 640, W_O, column)
     ends = jnp.where(z < levels - 1, 1, 0) + jnp.where(z > 0, 1, 0)
     pl.semaphore_wait(ready, 2 + ends)
-    for j in order:
-        so.lift(j, 0)
+    outer, inner_levels = order[:2], order[2:]
+
+    def o_stage(stage, part):
+        for j in part:
+            so.lift(j, stage)
+
+    def tick():
+        for stage, part in O_STEPS.get(line.now, ()):
+            if stage < levels - 1:
+                o_stage(stage, outer if part == 0 else inner_levels)
+        line.step()
+
+    o_stage(0, outer)
     l_wo.wait()
 
     def mix(i, carry):
@@ -1631,24 +1644,17 @@
         d_logits = jnp.where(lanes < N_ROUTE, d_gates * picks * gate * (1.0 - gate), 0.0)
         dfront[at, MISC:W_A] = d_logits.astype(bf16)
 
-    def o_stage(stage, part):
-        for j in part:
-            so.lift(j, stage)
-
-    outer, inner_levels = order[:2], order[2:]
     attend(0)
-    line.step()
+    tick()
     attend(1)
-    o_stage(1, outer)
-    line.step()
+    tick()
     for i in range(2, 2 * batches):
         attend(i)
     l_act.wait()
     one_all = grad.reshape(both, width)
     for column in range(4):
         weight_grad(a_src, one_all, dfront, 896, MISC, column)
-    line.step()
-    o_stage(1, inner_levels)
+    tick()
     last.wait()
 
     def final(i, carry):
@@ -1666,9 +1672,7 @@
     outs = [pltpu.make_async_copy(db.at[near], layer_out, osem.at[0])]
     outs[0].start()
 
-    line.step()
-    for stage in range(2, levels - 1):
-        o_stage(stage, order)
+    tick()
     for cp in l_wa:
         cp.wait()
 
@@ -1688,7 +1692,7 @@
     pl.semaphore_wait(freed, 1)
     hand.start()
     through_front(near)
-    line.step()
+    tick()
 
     spread = MEM + 2 * local_len
     ids = lax.broadcasted_iota(jnp.int32, (local_len, 1), 0)
@@ -1736,11 +1740,12 @@
         misc = dot_f32(one_hot, high, NT) + dot_f32(one_hot, low, NT)
         misc = misc + dot_f32(one_all[:, at], dfront[:, MISC:W_A], TN) + columns[column * span : (column + 1) * span]
         m_bufs[0][column] = misc.astype(bf16).reshape(levels, block_rows, W_MISC)
-    line.step()
-    line.step()
+    while line.now < len(units):
+        tick()
+    for stage in range(3, levels - 1):
+        o_stage(stage, order)
     for j in order:
         so.gathered(j)
-    line.turns()
     so.issue()
     line.round()
     so.turn()
@@ -1908,7 +1913,7 @@
 
 def by_size(*args):
     thin = args[9].shape[0] % 16 != 0
-    paired = lax.axis_size("doc") == 4 and lax.axis_size("tm") % 2 == 0
+    paired = lax.axis_size("doc") == 4 and lax.axis_size("tm") % 2 == 0 and lax.axis_size("tm") >= 8
     return on_device(*args) if thin or not paired else on_chip(*args)
 
 

time: 289 us -> 285 us (0.986)
  Pallas kernels: 287 us -> 282 us
    pallas_call x1, Pallas kernels: 140 us -> 135 us  [backward(): pl.pallas_call(functools.partial(backward_kernel, levels, batches, local_...]
where the time goes in v7:
time: 285 us; the launch traced here: 284 us
  Pallas kernels  282 us (99%)
    pallas_call x1, Pallas kernels, forward(): pl.pallas_call(functools.partial(forward_kernel, levels, batches, local_l...  142 us
    pallas_call x1, Pallas kernels, backward(): pl.pallas_call(functools.partial(backward_kernel, levels, batches, local_...  135 us

profile of v7, /device:TPU:0, one launch (start us, length us, event | category | flops | bytes accessed | tf_op | source)
XLA Modules:
  0.0 284.2 jit_solution(3087802033196591764)
XLA Ops:
  0.6 1.3 pad_maximum_fusion.norm_in
  1.9 141.8 %shard_map.273 = (bf16[4,4,64,1920]{3,2,1,0:T(8,128)(2,1)}, bf16[4,4,64,1280]{3,2,1,0:T(8,128)(2,1)}, bf16[4,4,64,2048]{3,2,1,0:T(8,128)(2,1)}, bf16[4,4,128,102...) custom-call(bf16[32,896]{1,0:T(8,128)(2,1)} %qk_in.1, ...), custom_call_target="tpu_custom_call" | custom-call | tf_op jit(solution)/shard_map/pallas_call | solution.py:1068
  143.7 135.1 %shard_map.274 = (f32[128,1024]{1,0:T(8,128)}, f32[2,32,2048]{2,1,0:T(8,128)}, f32[2,32,1280]{2,1,0:T(8,128)}, f32[2,32,1792]{2,1,0:T(8,128)}, f32[2,32,128]{2,1...) custom-call(bf16[4,4,128,1024]{3,2,1,0:T(8,128)(2,1)} %bitcast.34, bf16[2048,1024]{1,0:T(8,128)(2,1)} %bitcast.33, ...), custom_call_target="tpu_custom_call" | custom-call | tf_op jit(solution)/shard_map/pallas_call | solution.py:1800
  278.9 5.2 %shard_map.275 = (f32[128,1024]{1,0:T(8,128)}, f32[32,4096]{1,0:T(8,128)}, f32[32,2240]{1,0:T(8,128)}, f32[32,2240]{1,0:T(8,128)}, f32[32,896]{1,0:T(8,128)}, /*...) custom-call(f32[128,1024]{1,0:T(8,128)} %get-tuple-element.69.f_in, ...), custom_call_target="tpu_custom_call" | custom-call | tf_op jit(solution)/shard_map/pallas_call | solution.py:1862

commit v8 on v7

--- a/solution.py
+++ b/solution.py
@@ -557,24 +557,26 @@
     return lax.dot_general(a, b, dims, preferred_element_type=jnp.float32)
 
 
-def steps_of(text):
-    return [(w.split(".")[0], w.split(".")[1][:-1], int(w[-1])) for w in text.split()]
-
-
-EVENTS = {point: steps_of(text) for point, text in dict(
-    f="f.begin0",
-    a="a.begin0",
-    stats="a.line1",
-    packs="",
-    given="m.early0 a.turn0 a.line2 a.turn1 a.line3 a.turn2 o.begin0 m.early1 a.turn3 o.line1 m.early2",
-    front="o.turn0 o.line2 i.begin0",
-    cache="o.turn1 o.line3 i.line1 f.line1 m.early3",
-    memory="o.turn2 o.turn3 i.line2 f.line2 m0.late0 i.turn0 i.line3 f.line3 m0.late1 i.turn1 m0.late2",
-    half="m1.late0 m1.late1 f.turn0 i.turn2 i.turn3 m1.late2",
-    attended="f.turn1",
-    far="",
-    pair="f.turn2 f.turn3",
-    activated="",
+def steps_of(words):
+    return [(w[0], w[1], int(w[2])) for w in words]
+
+
+EVENTS = {point: steps_of(words) for point, words in dict(
+    f=("fb0",),
+    a=("ab0",),
+    stats=("al1", "at0",),
+    packs=(),
+    given=("me0", "al2", "at1", "al3", "at2", "ob0", "me1", "at3",
+        "ol1", "me2",),
+    front=("ot0", "ol2", "ib0",),
+    cache=("ot1", "ol3", "il1", "fl1", "me3",),
+    memory=("ot2", "ot3", "il2", "fl2", "0h0", "it0", "il3", "fl3",
+        "0h1", "it1", "0h2",),
+    half=("1h0", "1h1", "ft0", "it2", "it3", "1h2",),
+    attended=("ft1",),
+    far=(),
+    pair=("ft2", "ft3",),
+    activated=(),
 ).items()}
 
 
@@ -634,28 +636,28 @@
     own_f.wait()
     groups = dict(a=ga, o=go, i=gi, f=gf)
     left = [
-        (name, what, k) for name in groups for what, first in (("begin", 0), ("line", 1), ("turn", 0), ("finish", 0))
-        for k in range(first, 1 if what == "begin" else levels)]
-    left += [("m", "early", k) for k in range(MEM // local_len // 2)]
-    left += [("m%d" % batch, "late", k) for batch in range(batches) for k in range(MEM // local_len // 2)]
+        (name, what, k) for name in groups for what, first in (("b", 0), ("l", 1), ("t", 0), ("f", 0))
+        for k in range(first, 1 if what == "b" else levels)]
+    left += [("m", "e", k) for k in range(MEM // local_len // 2)]
+    left += [(str(batch), "h", k) for batch in range(batches) for k in range(MEM // local_len // 2)]
 
     def do(name, what, k):
         if (name, what, k) not in left:
             return
         left.remove((name, what, k))
-        if what == "early":
+        if what == "e":
             early(k)
             return
-        if what == "late":
-            late(k, int(name[1:]))
+        if what == "h":
+            late(k, int(name))
             return
         group = groups[name]
-        if what == "begin":
+        if what == "b":
             for cp in placed[name]:
                 cp.wait()
             group.begin()
         else:
-            dict(line=group.line, turn=group.turn, finish=group.finish)[what](k)
+            dict(l=group.line, t=group.turn, f=group.finish)[what](k)
 
     def run(point):
         for event in EVENTS[point]:
@@ -873,7 +875,7 @@
         bias[h] = turned[:, : MEM + local_len]
     run("memory")
     complete("m")
-    complete("m0")
+    complete("0")
 
     key_ids = lax.broadcasted_iota(jnp.int32, (local_len, local_len), 1)
     row_ids = lax.broadcasted_iota(jnp.int32, (local_len, local_len), 0)
@@ -917,7 +919,7 @@
     lax.fori_loop(0, 2, attend, 0)
     run("half")
     for batch in range(1, batches):
-        complete("m%d" % batch)
+        complete(str(batch))
     out_w = pltpu.make_async_copy(win, win_out, osem.at[1])
     out_w.start()
     lax.fori_loop(2, 2 * batches, attend, 0)
@@ -1323,8 +1325,14 @@
             if self.done[m] < len(self.follow):
                 self.advance(m)
 
-    def finish(self):
-        while min(self.done) < len(self.follow):
+    def finish(self, after):
+        after = list(after)
+        while True:
+            for item in [a for a in after if all(self.done[n] == len(self.follow) for n in a[0])]:
+                after.remove(item)
+                item[1]()
+            if min(self.done) == len(self.follow):
+                return
             self.round()
 
 
@@ -1751,15 +1759,25 @@
     so.turn()
     line.round()
     so.column()
-    line.finish()
-    outs.append(pltpu.make_async_copy(f_total, f_out, osem.at[2]))
-    outs[2].start()
     mine, other = [pl.ds(pl.multiple_of(k * shard, 16), shard) for k in (c, 1 - c)]
-    for i, (total, out) in enumerate(((i_total, i_out), (o_total, o_out), (a_total, a_out), (m_total, m_out))):
+
+    def hand_out(i, total, out):
         outs.append(exchange(total.at[other], out.at[c], 4 + i))
         outs[-1].start()
         outs.append(pltpu.make_async_copy(total.at[mine], out.at[c], osem.at[3 + i]))
         outs[-1].start()
+
+    def hand_out_f():
+        outs.append(pltpu.make_async_copy(f_total, f_out, osem.at[2]))
+        outs[-1].start()
+
+    hand_out(1, o_total, o_out)
+    groups = [range(k * levels, (k + 1) * levels) for k in range(2)] + [range(2 * levels, len(units))]
+    line.finish((
+        (groups[0], hand_out_f),
+        (groups[1], lambda: hand_out(0, i_total, i_out)),
+        (groups[2], lambda: (hand_out(2, a_total, a_out), hand_out(3, m_total, m_out))),
+    ))
     for s in sums + [so]:
         s.drain()
     for cp in outs:
@@ -1811,19 +1829,36 @@
 
 
 def share_kernel(
-    per_device, f_in, i_in, o_in, a_in, m_in, layer_in, grad_in,
-    f_out, in_out, branch_out, value_out, qk_out, router_out, gain1, shift1, gain2, shift2, bias_out, layer_out, grad_out,
-    f_hold, layer_hold, grad_hold, sems,
+    per_device, f_in, i_from, o_from, a_from, m_from, layer_in, grad_in,
+    f_to, in_to, branch_to, value_to, qk_to, router_to, gain1_to, shift1_to, gain2_to, shift2_to, bias_to, layer_to,
+    grad_to, *refs,
 ):
-    big = ((f_in, f_hold, f_out), (layer_in, layer_hold, layer_out), (grad_in, grad_hold, grad_out))
-    there = [pltpu.make_async_copy(src, held, sems.at[i]) for i, (src, held, unused) in enumerate(big)]
-    back = [pltpu.make_async_copy(held, dst, sems.at[3 + i]) for i, (unused, held, dst) in enumerate(big)]
-    for cp in there:
+    held, sems = refs[:-1], refs[-1]
+    f_hold, layer_hold, grad_hold, i_in, o_in, a_in, m_in, in_out, branch_out, value_out, qk_out, router_out = held[:12]
+    gain1, shift1, gain2, shift2, bias_out = held[12:]
+    whole = ((grad_in, grad_hold, grad_to), (layer_in, layer_hold, layer_to), (f_in, f_hold, f_to))
+    parts = ((i_from, i_in), (o_from, o_in), (a_from, a_in), (m_from, m_in))
+    small = [pltpu.make_async_copy(src, dst, sems.at[6 + i]) for i, (src, dst) in enumerate(parts)]
+    there = [pltpu.make_async_copy(src, dst, sems.at[i]) for i, (src, dst, unused) in enumerate(whole)]
+    back = [pltpu.make_async_copy(src, dst, sems.at[3 + i]) for i, (unused, src, dst) in enumerate(whole)]
+    for cp in small + there:
         cp.start()
+    done = (
+        (in_out, in_to), (value_out, value_to), (branch_out, branch_to), (qk_out, qk_to), (router_out, router_to),
+        (gain1, gain1_to), (shift1, shift1_to), (gain2, gain2_to), (shift2, shift2_to), (bias_out, bias_to))
+    done = [pltpu.make_async_copy(src, dst, sems.at[10 + i]) for i, (src, dst) in enumerate(done)]
+    small[0].wait()
     for side in range(SIDE):
         for p in range(i_in.shape[2] // PAD):
             col = (p * SIDE + side) * PAD
             in_out[:, col : col + PAD] = i_in[side, :, p * PAD : (p + 1) * PAD]
+    done[0].start()
+    for cp, after in zip(there, back):
+        cp.wait()
+        after.start()
+    for cp in small[1:]:
+        cp.wait()
+    for side in range(SIDE):
         for h in range(HALF_HEADS):
             at = (side * HALF_HEADS + h) * HEAD_DIM
             for e in range(EXPERTS):
@@ -1842,10 +1877,9 @@
     turned = (m_in[0] + m_in[1]).T
     for i, out in enumerate((gain1, shift1, gain2, shift2)):
         out[...] = turned[COL_NORM + i : COL_NORM + i + 1]
-    for cp, after in zip(there, back):
-        cp.wait()
-        after.start()
-    for cp in back:
+    for cp in done[1:]:
+        cp.start()
+    for cp in back + done:
         cp.wait()
 
 
@@ -1858,13 +1892,15 @@
         (f.shape, f32), ((shard, SIDE * i.shape[2]), f32), ((shard, EXPERTS * inner), f32),
         ((shard, EXPERTS * inner), f32), ((shard, 2 * inner), f32), ((shard, 2 * HEADS * EXPERTS), f32)]
     shapes += [((1, shard), f32)] * 4 + [((HEADS, per_device), f32), (layer.shape, layer.dtype), (grad.shape, f32)]
-    hbm, vmem = pl.BlockSpec(memory_space=pl.ANY), pl.BlockSpec(memory_space=pltpu.VMEM)
+    hbm = pl.BlockSpec(memory_space=pl.ANY)
     return pl.pallas_call(
         functools.partial(share_kernel, per_device),
         out_shape=[jax.ShapeDtypeStruct(s, k) for s, k in shapes],
-        in_specs=[hbm] + [vmem] * 4 + [hbm] * 2,
-        out_specs=[hbm] + [vmem] * 10 + [hbm] * 2,
-        scratch_shapes=[pltpu.VMEM(w.shape, w.dtype) for w in (f, layer, grad)] + [pltpu.SemaphoreType.DMA((6,))],
+        in_specs=[hbm] * 7,
+        out_specs=[hbm] * len(shapes),
+        scratch_shapes=[pltpu.VMEM(w.shape, w.dtype) for w in (f, layer, grad, i, o, a, m)]
+        + [pltpu.VMEM(s, k) for s, k in shapes[1:-2]]
+        + [pltpu.SemaphoreType.DMA((20,))],
         compiler_params=pltpu.CompilerParams(vmem_limit_bytes=VMEM_BYTES),
     )(*ins)
 

time: 285 us -> 281 us (0.986)
  Pallas kernels: 282 us -> 279 us
where the time goes in v8:
time: 281 us
  Pallas kernels  279 us (99%)
    pallas_call x1, Pallas kernels, forward(): pl.pallas_call(functools.partial(forward_kernel, levels, batches, local_l...  139 us
    pallas_call x1, Pallas kernels, backward(): pl.pallas_call(functools.partial(backward_kernel, levels, batches, local_...  136 us

profile of v8, /device:TPU:0, one launch (start us, length us, event | category | flops | bytes accessed | tf_op | source)
XLA Modules:
  0.0 281.1 jit_solution(2287821582972392532)
XLA Ops:
  0.6 1.3 pad_maximum_fusion.norm_in
  1.9 139.2 %shard_map.273 = (bf16[4,4,64,1920]{3,2,1,0:T(8,128)(2,1)}, bf16[4,4,64,1280]{3,2,1,0:T(8,128)(2,1)}, bf16[4,4,64,2048]{3,2,1,0:T(8,128)(2,1)}, bf16[4,4,128,102...) custom-call(bf16[32,896]{1,0:T(8,128)(2,1)} %qk_in.1, ...), custom_call_target="tpu_custom_call" | custom-call | tf_op jit(solution)/shard_map/pallas_call | solution.py:1070
  141.1 136.4 %shard_map.274 = (f32[128,1024]{1,0:T(8,128)}, f32[2,32,2048]{2,1,0:T(8,128)}, f32[2,32,1280]{2,1,0:T(8,128)}, f32[2,32,1792]{2,1,0:T(8,128)}, f32[2,32,128]{2,1...) custom-call(bf16[4,4,128,1024]{3,2,1,0:T(8,128)(2,1)} %bitcast.34, bf16[2048,1024]{1,0:T(8,128)(2,1)} %bitcast.33, ...), custom_call_target="tpu_custom_call" | custom-call | tf_op jit(solution)/shard_map/pallas_call | solution.py:1818
  277.6 3.4 %shard_map.275 = (f32[128,1024]{1,0:T(8,128)}, f32[32,4096]{1,0:T(8,128)}, f32[32,2240]{1,0:T(8,128)}, f32[32,2240]{1,0:T(8,128)}, f32[32,896]{1,0:T(8,128)}, /*...) custom-call(f32[128,1024]{1,0:T(8,128)} %get-tuple-element.69.f_in, ...), custom_call_target="tpu_custom_call" | custom-call | tf_op jit(solution)/shard_map/pallas_call | solution.py:1896

commit v9 on v8

--- a/solution.py
+++ b/solution.py
@@ -1272,7 +1272,7 @@
                         pl.when(self.z == level)(lambda: self.along(j, column, "down", level).wait_send())
 
 
-A_PARTS = (1024, 768)
+A_PARTS = (1280, 512)
 AHEAD = 3
 
 

time: 281 us -> 281 us (level)
  no operation moved by 1% of the time
where the time goes in v9:
time: 281 us
  Pallas kernels  279 us (99%)
    pallas_call x1, Pallas kernels, forward(): pl.pallas_call(functools.partial(forward_kernel, levels, batches, local_l...  139 us
    pallas_call x1, Pallas kernels, backward(): pl.pallas_call(functools.partial(backward_kernel, levels, batches, local_...  136 us

profile of v9, /device:TPU:0, one launch (start us, length us, event | category | flops | bytes accessed | tf_op | source)
XLA Modules:
  0.0 281.1 jit_solution(13494719256013606265)
XLA Ops:
  0.6 1.3 pad_maximum_fusion.norm_in
  1.9 139.2 %shard_map.273 = (bf16[4,4,64,1920]{3,2,1,0:T(8,128)(2,1)}, bf16[4,4,64,1280]{3,2,1,0:T(8,128)(2,1)}, bf16[4,4,64,2048]{3,2,1,0:T(8,128)(2,1)}, bf16[4,4,128,102...) custom-call(bf16[32,896]{1,0:T(8,128)(2,1)} %qk_in.1, ...), custom_call_target="tpu_custom_call" | custom-call | tf_op jit(solution)/shard_map/pallas_call | solution.py:1070
  141.1 136.4 %shard_map.274 = (f32[128,1024]{1,0:T(8,128)}, f32[2,32,2048]{2,1,0:T(8,128)}, f32[2,32,1280]{2,1,0:T(8,128)}, f32[2,32,1792]{2,1,0:T(8,128)}, f32[2,32,128]{2,1...) custom-call(bf16[4,4,128,1024]{3,2,1,0:T(8,128)(2,1)} %bitcast.34, bf16[2048,1024]{1,0:T(8,128)(2,1)} %bitcast.33, ...), custom_call_target="tpu_custom_call" | custom-call | tf_op jit(solution)/shard_map/pallas_call | solution.py:1818
  277.6 3.4 %shard_map.275 = (f32[128,1024]{1,0:T(8,128)}, f32[32,4096]{1,0:T(8,128)}, f32[32,2240]{1,0:T(8,128)}, f32[32,2240]{1,0:T(8,128)}, f32[32,896]{1,0:T(8,128)}, /*...) custom-call(f32[128,1024]{1,0:T(8,128)} %get-tuple-element.69.f_in, ...), custom_call_target="tpu_custom_call" | custom-call | tf_op jit(solution)/shard_map/pallas_call | solution.py:1896
